TPU v7x, 512 devices: a whole 4x4x16 slice. The times are simulated.
512 devices in a mesh: dom: 16 (over z), row: 8 (over y, core), col: 4 (over x).
Axes of the slice: x: 4, y: 4, z: 16, core: 2. Of those that a mesh axis runs over, the one named last changes fastest.
Arguments:
- protein_panel: float32 [8, 4, 128, 16384], P('row', 'col', None, 'dom'), may hold values from 0 to 0.03125
- tile_mask: int32 [8, 4, 1, 128], P('row', 'col', None, 'dom'), may hold values 0 or 1
- domain_class: int32 [16384], P('dom'), may hold values from 0 to 15
- class_weight: float32 [16], replicated, may hold values from 0.1 to 1
Outputs:
- flow: float32 [8, 4, 128, 8, 4, 128], P('row', None, 'dom', None, 'col')
All inputs are finite; a program needn't handle non-finite values. No bound on the sum of `tile_mask` on one device may be relied on, other than what follows from the above.
Results may differ from a plain program's by a relative error of at most 0.00005.
Values sent between devices are 32-bit elements; how exact they have to be, the bound alone decides.
No kernel may reach another device: no remote copies, remote signals or barrier semaphores. Data moves between devices by JAX's collectives and lax.ppermute only.
A program may use at most 64 MiB of HBM per device.

v0:
```python
import jax
import jax.numpy as jnp
from jax import lax
from jax.sharding import PartitionSpec as P

TILE = 128


def per_device(protein_panel, tile_mask, domain_class, class_weight):
    n_rows = lax.axis_size("row")
    n_cols = lax.axis_size("col")
    n_doms = lax.axis_size("dom")
    width = protein_panel.shape[2]
    panel_cols = protein_panel.shape[3]
    local_rows = width // n_doms
    tiles_rows = width // TILE
    tiles_cols = panel_cols // TILE
    expanded = tile_mask.astype(jnp.float32)[:, :, :, None, :, None]
    masked = (protein_panel.reshape(1, 1, tiles_rows, TILE, tiles_cols, TILE) * expanded).reshape(
        1, 1, width, panel_cols
    )
    one_hot = (
        domain_class[:, None] == jnp.arange(class_weight.shape[0], dtype=jnp.int32)[None, :]
    ).astype(jnp.float32)
    weights = jnp.dot(one_hot, class_weight, precision=lax.Precision.HIGHEST)
    row_scores = lax.all_gather(masked, "col", axis=1, tiled=True)[0]
    col_scores = lax.all_gather(masked, "row", axis=0, tiled=True)[:, 0].reshape(
        n_rows * width, panel_cols
    )
    weighted = row_scores * weights[None, None, :]
    block = lax.psum_scatter(
        jnp.einsum("ckd,qd->kcq", weighted, col_scores, precision=lax.Precision.HIGHEST),
        "dom",
        scatter_dimension=0,
        tiled=True,
    )
    totals = lax.psum(jnp.sum(block, axis=(0, 1)), ("dom", "row"))
    totals = totals + 1.0
    block = jnp.transpose(block, (1, 0, 2)).reshape(n_cols, local_rows, n_rows, width)
    grid_shape = (n_cols, local_rows, n_rows, width)
    col_iota = lax.broadcasted_iota(jnp.int32, grid_shape, 0)
    local_iota = lax.broadcasted_iota(jnp.int32, grid_shape, 1)
    row_iota = lax.broadcasted_iota(jnp.int32, grid_shape, 2)
    inner_iota = lax.broadcasted_iota(jnp.int32, grid_shape, 3)
    diagonal = (
        (col_iota == lax.axis_index("col"))
        & (row_iota == lax.axis_index("row"))
        & (inner_iota == lax.axis_index("dom") * local_rows + local_iota)
    )
    unit_diag = diagonal.astype(jnp.float32)
    scaling = n_rows * n_cols * width / totals.reshape(n_rows, width)
    flow = (block + unit_diag) * scaling[None, None, :, :]
    return flow.reshape(1, n_cols, local_rows, n_rows, 1, width)


def solution(mesh):
    placed = (P("row", "col", None, "dom"), P("row", "col", None, "dom"), P("dom"), P())
    return jax.shard_map(
        per_device,
        mesh=mesh,
        in_specs=placed,
        out_specs=P("row", None, "dom", None, "col", None),
        check_vma=False,
    )
```

profile of v0, /device:TPU:6, one launch (start us, length us, event | category | flops | bytes accessed | tf_op | source)
XLA Modules:
  0.0 505.6 jit_solution(2573047469936929664)
XLA Ops:
  6.5 0.0 copy-start
  6.5 0.0 copy-start.1
  6.5 0.0 all-gather.5.cloned.1.call-start
  6.5 0.7 convert_bitcast_fusion
  7.2 0.1 broadcast_bitcast_fusion
  7.3 1.9 fusion.13
  9.2 0.0 all-gather.5.cloned.1.call-update
  9.2 0.0 all-gather.3.cloned.1.call-start
  9.3 1.9 broadcast_multiply_fusion
  11.2 0.0 all-gather.3.cloned.1.call-update
  11.2 0.0 all-reduce.3.cloned.1.call-start
  11.2 0.0 copy-done
  11.2 0.0 copy-done.1
  11.3 0.4 fusion.7
  11.7 38.9 %all-gather.5.cloned.1.call-done = f32[1,4,128,1024]{3,2,0,1:T(8,128)} async-done(((f32[1,1,128,1024]{3,2,0,1:T(8,128)}), f32[1,4,128,1024]{3,2,0,1:T(8,128)}) %all-gather.5.cloned.1.call-update) | async-done | bytes 2097168 | tf_op jit(solution)/shard_map/all_gather | solution.py:26
  50.5 43.9 %all-gather.3.cloned.1.call-done = f32[8,1,128,1024]{3,2,1,0:T(8,128)} async-done(((f32[1,1,128,1024]{3,2,1,0:T(8,128)}), f32[8,1,128,1024]{3,2,1,0:T(8,128)}) %all-gather.3.cloned.1.call-update) | async-done | bytes 4194320 | tf_op jit(solution)/shard_map/all_gather | solution.py:27
  94.5 9.3 %fusion.3 = f32[128,4,1024]{0,2,1:T(8,128)S(1)} fusion(f32[1024,1024,1]{1,0,2:T(8,128)} %bitcast.28, f32[1,4,128,1024]{3,2,0,1:T(8,128)} %all-gather.5.cloned.1.call-done, f32[1024]{0:T(1024)S(1)} %bitcast.29), kind=kOutput, calls=%fused_computation.3 | convolution fusion | flops 6442975232 | bytes 8392704 | tf_op jit(solution)/shard_map/ckd,qd->kcq/dot_general | solution.py:32
  103.8 2.0 copy.7
  105.9 0.0 all-reduce.3.cloned.1.call-update
  105.9 1.3 dynamic-slice
  107.9 142.4 %all-reduce.3.cloned.1.call-done = f32[128,4,1024]{2,1,0:T(4,128)} async-done(((f32[128,4,1024]{2,1,0:T(4,128)}), f32[128,4,1024]{2,1,0:T(4,128)}) %all-reduce.3.cloned.1.call-update) | async-done | bytes 2097168
  250.3 0.9 dynamic-slice_reduce_fusion
  251.3 0.1 reshape.53
  251.3 246.8 %psum.7 = f32[1024]{0:T(1024)S(1)} all-reduce(f32[1024]{0:T(1024)S(1)} %get-tuple-element.5), channel_id=1, replica_groups=mesh['dom'=16,'row'=8,'col'=4] {'dom','row'}, use_global_device_ids=true, to_apply=%region_2.0 | all-reduce | flops 1024 | bytes 8192 | tf_op jit(solution)/shard_map/psum | solution.py:37
  498.2 0.9 fusion.10
  (4 shorter events, 0.0 us)
Async XLA Ops:
  6.5 4.7 copy-start
  6.5 4.7 copy-start.1
  6.5 44.0 %all-gather.5.cloned.1.call-start = ((), (), s32[]{:S(2)}) async-start(), calls=%async_computation.1 | async-start | bytes 2621440 | tf_op jit(solution)/shard_map/all_gather | solution.py:26
  9.2 85.3 %all-gather.3.cloned.1.call-start = ((), (), s32[]{:S(2)}) async-start(), calls=%async_computation | async-start | bytes 4718592 | tf_op jit(solution)/shard_map/all_gather | solution.py:27
  11.2 239.1 %all-reduce.3.cloned.1.call-start = ((), (), s32[]{:S(2)}) async-start(), calls=%async_computation.2 | async-start | bytes 4194304
Sparse Core Ops, SparseCore 0:
  9.5 41.0 all-gather.4
  52.7 41.7 all-gather.2
  106.0 144.2 all-reduce.2
where the time goes:
time: 507 us; the launch traced here: 506 us
  blocking collectives  247 us (49%)
  waiting for transfers between devices  225 us (44%)
  between operations  13.8 us (3%)
  matrix products  9.79 us (2%)
  other arithmetic  6.32 us (1%)
    psum x1, blocking collectives, per_device(): totals = lax.psum(jnp.sum(block, axis=(0, 1)), ('dom', 'row'))  247 us
    unnamed x4, waiting for transfers between devices  142 us
    all_gather x1, waiting for transfers between devices, per_device(): lax.all_gather(masked, 'row', axis=0, tiled=True)[:, 0]  43.9 us
    all_gather x1, waiting for transfers between devices, per_device(): row_scores = lax.all_gather(masked, 'col', axis=1, tiled=True)[0]  38.9 us
  transfers between devices with their start and end apart: 3, of which 3 were waited for; matrix products, arithmetic and copies ran while one was open for 1% of the time, Pallas kernels for 0%

commit v1 on v0

v1 whole, which is shorter than its diff:
```python
import jax
import jax.numpy as jnp
from jax import lax
from jax.sharding import PartitionSpec as P

TILE = 128


def per_device(protein_panel, tile_mask, domain_class, class_weight):
    n_rows = lax.axis_size("row")
    n_cols = lax.axis_size("col")
    n_doms = lax.axis_size("dom")
    width = protein_panel.shape[2]
    panel_cols = protein_panel.shape[3]
    local_rows = width // n_doms
    tiles_cols = panel_cols // TILE
    mask = jnp.broadcast_to(
        tile_mask.astype(jnp.float32).reshape(tiles_cols, 1), (tiles_cols, TILE)
    ).reshape(1, panel_cols)
    masked = protein_panel.reshape(width, panel_cols) * mask
    one_hot = (
        domain_class[:, None] == jnp.arange(class_weight.shape[0], dtype=jnp.int32)[None, :]
    ).astype(jnp.float32)
    weights = jnp.dot(one_hot, class_weight, precision=lax.Precision.HIGHEST)
    q = lax.all_gather(masked, "row", axis=0, tiled=True)
    sums = lax.psum(jnp.sum(q, axis=0), "col")
    p = lax.all_gather(masked, "col", axis=0)
    shares = jnp.einsum(
        "d,qd->q", sums * weights, q, precision=lax.Precision.HIGHEST
    )
    weighted = p.reshape(n_cols, n_doms, local_rows, panel_cols) * weights
    weighted = jnp.transpose(weighted, (1, 0, 2, 3)).reshape(n_cols * width, panel_cols)
    block = jnp.einsum("pd,qd->pq", weighted, q, precision=lax.Precision.HIGH)
    block = block.reshape(n_doms, n_cols * local_rows, n_rows * width)
    extra = jnp.broadcast_to(shares[None, None, :], (n_doms, 8, n_rows * width))
    block = lax.psum_scatter(
        jnp.concatenate([block, extra], axis=1), "dom", scatter_dimension=0, tiled=False
    )
    totals = block[n_cols * local_rows] + 1.0
    block = block[: n_cols * local_rows].reshape(n_cols, local_rows, n_rows, width)
    grid_shape = (n_cols, local_rows, n_rows, width)
    diagonal = (
        (lax.broadcasted_iota(jnp.int32, grid_shape, 0) == lax.axis_index("col"))
        & (lax.broadcasted_iota(jnp.int32, grid_shape, 2) == lax.axis_index("row"))
        & (
            lax.broadcasted_iota(jnp.int32, grid_shape, 3)
            == lax.axis_index("dom") * local_rows
            + lax.broadcasted_iota(jnp.int32, grid_shape, 1)
        )
    )
    scaling = n_rows * n_cols * width / totals.reshape(n_rows, width)
    flow = (block + diagonal.astype(jnp.float32)) * scaling[None, None, :, :]
    return flow.reshape(1, n_cols, local_rows, n_rows, 1, width)


def solution(mesh):
    placed = (P("row", "col", None, "dom"), P("row", "col", None, "dom"), P("dom"), P())
    return jax.shard_map(
        per_device,
        mesh=mesh,
        in_specs=placed,
        out_specs=P("row", None, "dom", None, "col", None),
        check_vma=False,
    )
```

time: 507 us -> 187 us (0.37)
  blocking collectives: 247 us -> 7.48 us
  waiting for transfers between devices: 225 us -> 142 us
    psum x1, blocking collectives: 247 us -> 7.48 us  [per_device(): sums = lax.psum(jnp.sum(q, axis=0), 'col')]
    unnamed x4 -> x3, waiting for transfers between devices: 142 us -> 0.05 us
    reduce_scatter x0 -> x1, waiting for transfers between devices: none -> 76.6 us  [per_device(): lax.psum_scatter(jnp.concatenate([block, extra], axis=1), 'dom', scatter_...]
    all_gather x2, waiting for transfers between devices: 82.8 us -> 65.3 us  [the longest x1 42.1 us: per_device(): q = lax.all_gather(masked, 'row', axis=0, tiled=True)]
    dot_general x1 -> x2, matrix products: 9.34 us -> 12 us  [the longest x1 6.32 us: per_device(): block = jnp.einsum('pd,qd->pq', weighted, q, precision=lax.Precision.HIGH)]
  transfers between devices with their start and end apart: 3 -> 3, of which waited for: 3 -> 3; matrix products, arithmetic and copies ran while one was open for 1% -> 6% of each run, Pallas kernels for 0% -> 0%
where the time goes in v1:
time: 187 us
  waiting for transfers between devices  142 us (76%)
  between operations  13.2 us (7%)
  matrix products  12.4 us (7%)
  other arithmetic  10.4 us (6%)
  blocking collectives  7.48 us (4%)
    reduce_scatter x1, waiting for transfers between devices, per_device(): lax.psum_scatter(jnp.concatenate([block, extra], axis=1), 'dom', scatter_...  76.6 us
    all_gather x1, waiting for transfers between devices, per_device(): q = lax.all_gather(masked, 'row', axis=0, tiled=True)  42.1 us
    all_gather x1, waiting for transfers between devices, per_device(): p = lax.all_gather(masked, 'col', axis=0)  23.2 us
    psum x1, blocking collectives, per_device(): sums = lax.psum(jnp.sum(q, axis=0), 'col')  7.48 us
    dot_general x1, matrix products, per_device(): block = jnp.einsum('pd,qd->pq', weighted, q, precision=lax.Precision.HIGH)  6.32 us
    dot_general x1, matrix products, per_device(): jnp.einsum('d,qd->q', sums * weights, q, precision=lax.Precision.HIGHEST)  5.64 us
    mul x2, other arithmetic, per_device(): masked = protein_panel.reshape(width, panel_cols) * mask  3.79 us
  transfers between devices with their start and end apart: 3, of which 3 were waited for; matrix products, arithmetic and copies ran while one was open for 6% of the time, Pallas kernels for 0%

profile of v1, /device:TPU:6, one launch (start us, length us, event | category | flops | bytes accessed | tf_op | source)
XLA Modules:
  0.0 186.6 jit_solution(9113742445903416742)
XLA Ops:
  6.5 0.0 copy-start
  6.5 0.0 copy-start.1
  6.5 0.0 all-gather.5.cloned.1.call-start
  6.5 0.7 convert_bitcast_fusion
  7.2 0.1 broadcast_bitcast_fusion
  7.3 1.9 %bitcast_multiply_fusion.1 = f32[128,1024]{1,0:T(8,128)} fusion(f32[1,1,128,1024]{3,2,1,0:T(8,128)} %param.4, f32[1024]{0:T(1024)S(1)} %broadcast_bitcast_fusion), kind=kLoop, calls=%fused_computation.7 | loop fusion | flops 131072 | bytes 1052672 | tf_op jit(solution)/shard_map/mul | solution.py:20
  9.2 0.0 all-gather.5.cloned.1.call-update
  9.2 0.0 all-gather.3.cloned.1.call-start
  9.3 1.9 %bitcast_multiply_fusion.2 = f32[1,128,1024]{2,1,0:T(8,128)} fusion(f32[1,1,128,1024]{3,2,1,0:T(8,128)} %param.4, f32[1024]{0:T(1024)S(1)} %broadcast_bitcast_fusion), kind=kLoop, calls=%fused_computation.8 | loop fusion | flops 131072 | bytes 1052672 | tf_op jit(solution)/shard_map/mul | solution.py:20
  11.2 0.0 all-gather.3.cloned.1.call-update
  11.2 0.0 reduce-scatter.2.cloned.1.call-start
  11.2 0.0 copy-done
  11.2 0.0 copy-done.1
  11.3 0.4 fusion.5
  11.7 42.1 %all-gather.5.cloned.1.call-done = f32[1024,1024]{1,0:T(8,128)} async-done(((f32[128,1024]{1,0:T(8,128)}), f32[1024,1024]{1,0:T(8,128)}) %all-gather.5.cloned.1.call-update) | async-done | bytes 4194320 | tf_op jit(solution)/shard_map/all_gather | solution.py:25
  53.8 2.5 %reduce_sum.9 = f32[1024]{0:T(1024)S(1)} reduce(f32[1024,1024]{1,0:T(8,128)} %all-gather.5.cloned.1.call-done, f32[]{:T(128)} %constant.5.clone.1), dimensions={0}, to_apply=%region_0.0 | reduce | flops 1047552 | bytes 4198404 | tf_op jit(solution)/shard_map/reduce_sum | solution.py:26
  56.2 7.5 %psum.7 = f32[1024]{0:T(1024)S(1)} all-reduce(f32[1024]{0:T(1024)S(1)} %reduce_sum.9), channel_id=1, replica_groups=mesh['dom'=16,'row'=8,'col'=4] {'col'}, use_global_device_ids=true, to_apply=%region_1.0 | all-reduce | flops 1024 | bytes 8192 | tf_op jit(solution)/shard_map/psum | solution.py:26
  63.7 5.6 %fusion.11 = f32[1,1024]{1,0:T(1,128)S(1)} fusion(f32[1024,1]{0,1:T(1,128)S(1)} %bitcast.39, f32[1024,1024]{1,0:T(8,128)} %all-gather.5.cloned.1.call-done), kind=kOutput, calls=%fused_computation.24 | convolution fusion | flops 12582912 | bytes 4202496 | tf_op jit(solution)/shard_map/d,qd->q/dot_general | solution.py:28
  69.4 23.2 %all-gather.3.cloned.1.call-done = f32[4,128,1024]{2,1,0:T(8,128)} async-done(((f32[1,128,1024]{2,1,0:T(8,128)}), f32[4,128,1024]{2,1,0:T(8,128)}) %all-gather.3.cloned.1.call-update) | async-done | bytes 2097168 | tf_op jit(solution)/shard_map/all_gather | solution.py:27
  92.6 6.3 %fusion = f32[16,32,1024]{2,1,0:T(8,128)S(1)} fusion(f32[1024,1024]{1,0:T(8,128)} %all-gather.5.cloned.1.call-done, f32[4,128,1024]{2,1,0:T(8,128)} %all-gather.3.cloned.1.call-done, f32[1024]{0:T(1024)S(1)} %bitcast.36), kind=kOutput, calls=%fused_computation | convolution fusion | flops 3221749760 | bytes 8392704 | tf_op jit(solution)/shard_map/pd,qd->pq/dot_general | solution.py:33
  98.9 1.8 pad_maximum_fusion
  100.7 0.0 reduce-scatter.2.cloned.1.call-update
  100.8 76.6 %reduce-scatter.2.cloned.1.call-done = f32[1,40,1024]{2,1,0:T(8,128)} async-done(((f32[16,40,1024]{2,1,0:T(8,128)}), f32[1,40,1024]{2,1,0:T(8,128)}) %reduce-scatter.2.cloned.1.call-update) | async-done | bytes 163856 | tf_op jit(solution)/shard_map/reduce_scatter | solution.py:36
  177.5 0.9 slice_bitcast_fusion
  178.4 0.8 fusion.9
  179.1 0.9 fusion.8
  (5 shorter events, 0.1 us)
Async XLA Ops:
  6.5 4.7 %copy-start = (f32[16]{0:T(128)S(1)}, f32[16]{0:T(128)}, u32[]{:S(2)}) copy-start(f32[16]{0:T(128)} %param.7) | copy-start | bytes 196
  6.5 4.7 %copy-start.1 = (s32[1024]{0:T(1024)S(1)}, s32[1024]{0:T(1024)}, u32[]{:S(2)}) copy-start(s32[1024]{0:T(1024)} %param.6) | copy-start | bytes 12292
  6.5 47.2 %all-gather.5.cloned.1.call-start = ((), (), s32[]{:S(2)}) async-start(), calls=%async_computation.2 | async-start | bytes 4718592 | tf_op jit(solution)/shard_map/all_gather | solution.py:25
  9.2 83.3 %all-gather.3.cloned.1.call-start = ((), (), s32[]{:S(2)}) async-start(), calls=%async_computation.1 | async-start | bytes 2621440 | tf_op jit(solution)/shard_map/all_gather | solution.py:27
  11.2 166.3 %reduce-scatter.2.cloned.1.call-start = ((), (), s32[]{:S(2)}) async-start(), calls=%async_computation.3 | async-start | bytes 2785280 | tf_op jit(solution)/shard_map/reduce_scatter | solution.py:36
Sparse Core Ops, SparseCore 0:
  9.5 44.2 all-gather.4
  55.9 36.6 all-gather.2
  100.9 76.5 reduce-scatter.1

commit v2 on v1

v2 whole, which is shorter than its diff:
```python
import functools

import jax
import jax.numpy as jnp
from jax import lax
from jax.experimental import pallas as pl
from jax.experimental.pallas import tpu as pltpu
from jax.sharding import PartitionSpec as P

TILE = 128
N_DOM, N_ROW, N_COL = 16, 8, 4
WIDTH = 128
PANEL = 1024
POS = WIDTH // N_DOM
UNIT = N_COL * 2 * POS
HALF = 4 * WIDTH
PROT = N_ROW * N_COL * WIDTH
PARAMS = pltpu.CompilerParams(vmem_limit_bytes=32 * 1024 * 1024)
VMEM = pl.BlockSpec(memory_space=pltpu.VMEM)
SMEM = pl.BlockSpec(memory_space=pltpu.SMEM)
F32 = jnp.float32
BF16 = jnp.bfloat16


def call(body, outs, in_specs, flops=0, nbytes=0, scratch=()):
    many = isinstance(outs, list)
    return pl.pallas_call(
        body,
        out_shape=[jax.ShapeDtypeStruct(s, F32) for s in outs] if many else jax.ShapeDtypeStruct(outs, F32),
        in_specs=in_specs,
        out_specs=[VMEM] * len(outs) if many else VMEM,
        scratch_shapes=list(scratch),
        compiler_params=PARAMS,
        cost_estimate=pl.CostEstimate(flops=flops, bytes_accessed=nbytes, transcendentals=0),
    )


def mask_body(panel, tile_mask, classes, class_weight, own, weights):
    for t in range(PANEL // TILE):
        at = pl.ds(t * TILE, TILE)
        kept = panel[:, at] * tile_mask[0, t].astype(F32)
        own[pl.ds(0, WIDTH), at] = kept
        own[pl.ds(WIDTH, 8), at] = jnp.broadcast_to(jnp.sum(kept, axis=0, keepdims=True), (8, TILE))
    of = classes[...]
    found = jnp.zeros((1, PANEL), F32)
    for k in range(class_weight.shape[0]):
        found = jnp.where(of == k, class_weight[k], found)
    weights[...] = found


def pick_body(shards, own, other, weights, out):
    w = weights[...]
    for j in range(8):
        at = pl.ds(pl.multiple_of(shards[j] * POS, POS), POS)
        out[pl.ds(j * 2 * POS, POS), :] = own[at, :] * w
        out[pl.ds(j * 2 * POS + POS, POS), :] = other[at, :] * w


def split(x):
    high = x.astype(BF16)
    return high, (x - high.astype(F32)).astype(BF16)


def dot3(ph, pl_, qh, ql):
    dims = (((1,), (1,)), ((), ()))
    dot = functools.partial(lax.dot_general, dimension_numbers=dims, preferred_element_type=F32)
    return dot(ph, qh) + (dot(ph, ql) + dot(pl_, qh))


def block_body(*refs, with_totals):
    if with_totals:
        ps, qs, rest, sums, weights = refs[:4], refs[4:8], refs[8:12], refs[12:16], refs[16]
        first, second, third, ph, pl_, qh, ql = refs[17:]
    else:
        ps, qs = refs[:4], refs[4:8]
        first, second, third, ph, pl_, qh, ql = refs[8:]
    for n in range(4):
        at = pl.ds(n * WIDTH, WIDTH)
        ph[at, :], pl_[at, :] = split(ps[n][...])
        qh[at, :], ql[at, :] = split(qs[n][pl.ds(0, WIDTH), :])
    block = dot3(ph[...], pl_[...], qh[...], ql[...])
    for n in range(N_COL):
        for j in range(8):
            out = (first, second, third)[j % 3]
            rows = n * WIDTH + j * 2 * POS
            out[pl.ds((j // 3) * UNIT + n * 2 * POS, 2 * POS), :] = block[rows : rows + 2 * POS]
    if with_totals:
        total = (sums[0][...] + sums[1][...] + sums[2][...] + sums[3][...]) * weights[...]
        th, tl = split(jnp.concatenate([total, total], axis=0))
        of_second = dot3(th, tl, qh[...], ql[...])[:8]
        for n in range(4):
            at = pl.ds(n * WIDTH, WIDTH)
            qh[at, :], ql[at, :] = split(rest[n][pl.ds(0, WIDTH), :])
        of_first = dot3(th, tl, qh[...], ql[...])[:8]
        odd = lax.broadcasted_iota(jnp.int32, (8, HALF), 0) % 2 == 1
        share = jnp.where(odd, of_second, of_first)
        first[pl.ds(3 * UNIT, 8), :] = share
        second[pl.ds(3 * UNIT, 8), :] = share


def finish_body(place, f_a, f_b, g_a, g_b, out):
    x, y, core, z = place[0], place[1], place[2], place[3]
    total_a = f_b[pl.ds(UNIT, 1), :] + g_b[pl.ds(UNIT // 2 + 1, 1), :]
    total_b = f_b[pl.ds(UNIT + 1, 1), :] + g_b[pl.ds(UNIT // 2, 1), :]
    scale_a, scale_b = PROT / (total_a + 1.0), PROT / (total_b + 1.0)
    lanes = lax.broadcasted_iota(jnp.int32, (POS, WIDTH), 1)
    rows = lax.broadcasted_iota(jnp.int32, (POS, WIDTH), 0)
    unit = (lanes == z * POS + rows).astype(F32)
    for n in range(N_COL):
        c = (x + n) % N_COL
        mine, theirs = pl.ds(n * 2 * POS, POS), pl.ds(n * POS, POS)
        for m in range(4):
            at = pl.ds(m * WIDTH, WIDTH)
            row = 2 * ((y + m) % 4)
            a = f_a[mine, at] + g_b[theirs, at]
            if n == 0 and m == 0:
                a = a + unit
            b = f_b[mine, at] + g_a[theirs, at]
            base = c * (POS * N_ROW) + row
            out[pl.ds(base + core, POS, stride=N_ROW), :] = a * scale_a[:, m * WIDTH : (m + 1) * WIDTH]
            out[pl.ds(base + 1 - core, POS, stride=N_ROW), :] = b * scale_b[:, m * WIDTH : (m + 1) * WIDTH]


def along_x(a, shift):
    return lax.ppermute(a, "col", [(i, (i + shift) % N_COL) for i in range(N_COL)])


def along_y(a, shift):
    return lax.ppermute(a, "row", [(i, (i + 2 * shift) % N_ROW) for i in range(N_ROW)])


def across(a):
    return lax.ppermute(a, "row", [(i, i ^ 1) for i in range(N_ROW)])


def along_z(a, shift):
    pairs = []
    for z in range(N_DOM):
        for r in range(N_ROW):
            to = (z + (shift if r % 2 == 0 else -shift)) % N_DOM
            pairs.append((z * N_ROW + r, to * N_ROW + r))
    return lax.ppermute(a, ("dom", "row"), pairs)


def per_device(protein_panel, tile_mask, domain_class, class_weight):
    x, r, z = lax.axis_index("col"), lax.axis_index("row"), lax.axis_index("dom")
    y, core = r // 2, r % 2
    steps = jnp.arange(8, dtype=jnp.int32)
    shards = jnp.where(
        core == 0, z + 8 - steps, jnp.where(steps == 0, z, z + 8 + steps)
    ) % N_DOM
    place = jnp.stack([x, y, core, z]).astype(jnp.int32)
    own, weights = call(
        mask_body, [(WIDTH + 8, PANEL), (1, PANEL)], [VMEM, SMEM, VMEM, SMEM], nbytes=1 << 20
    )(
        protein_panel.reshape(WIDTH, PANEL),
        tile_mask.reshape(1, PANEL // TILE),
        domain_class.reshape(1, PANEL),
        class_weight,
    )
    other = across(own)
    y_next = along_y(own, -1)
    y_last = along_y(own, 1)
    y_far = along_y(own, 2)
    picked = call(pick_body, (WIDTH, PANEL), [SMEM, VMEM, VMEM, VMEM], nbytes=3 << 19)(
        shards, own, other, weights
    )
    x_next = along_x(picked, -1)
    x_last = along_x(picked, 1)
    x_far = along_x(picked, 2)
    ps = (picked, x_next, x_far, x_last)
    qa = (own, y_next, y_far, y_last)
    qb = (other, across(y_next), across(y_far), across(y_last))
    halves = lambda count: [pltpu.VMEM((4 * WIDTH, PANEL), BF16) for _ in range(4)]
    flops = 6 * (4 * WIDTH) * HALF * PANEL
    a0, a1, a2 = call(
        functools.partial(block_body, with_totals=False),
        [(3 * UNIT, HALF), (3 * UNIT, HALF), (2 * UNIT, HALF)],
        [VMEM] * 8,
        flops=flops, nbytes=5 << 20, scratch=halves(4),
    )(*ps, *qa)
    ar = along_z(a0, 1)
    sums = sum(q[WIDTH:] for q in qa + qb)
    chips = (sums, along_x(sums, 1), along_x(sums, -1), along_x(sums, 2))
    b0, b1, b2 = call(
        functools.partial(block_body, with_totals=True),
        [(3 * UNIT + 8, HALF), (3 * UNIT + 8, HALF), (2 * UNIT, HALF)],
        [VMEM] * 17,
        flops=flops, nbytes=7 << 20, scratch=halves(4),
    )(*ps, *qb, *qa, *chips, weights)
    br = along_z(b0, 1)

    even = core == 0

    def second_step(u1, r1):
        return u1 + jnp.concatenate([jnp.where(even, r1[:UNIT], 0.0), r1[UNIT:]])

    a_sent = second_step(a1, ar)
    ar = along_z(a_sent, 1)
    b_sent = second_step(b1, br)
    br = along_z(b_sent, 1)
    a_near = a2[UNIT:] + ar[UNIT : 2 * UNIT]
    a_sum = ar[2 * UNIT :] + jnp.where(even, 0.0, a0[:UNIT])
    ar = along_z(a2[:UNIT] + ar[:UNIT], 3)
    share = b1[3 * UNIT :]
    b_near = b2[UNIT:] + br[UNIT : 2 * UNIT]
    b_sum = br[2 * UNIT : 3 * UNIT] + jnp.where(even, 0.0, b0[:UNIT])
    b_total = br[3 * UNIT :] + jnp.where(even, 0.0, share)
    narrow = (lax.broadcasted_iota(jnp.int32, (8, HALF), 0) >= 2) & ~even
    window = jnp.where(narrow, b_sent[3 * UNIT :], share + br[3 * UNIT :])
    br = along_z(jnp.concatenate([b2[:UNIT] + br[:UNIT], window]), 3)
    ar = along_z(a_near + ar, 3)
    b_total = b_total + br[UNIT:]
    br = along_z(jnp.concatenate([b_near + br[:UNIT], br[UNIT:]]), 3)
    f_a = a_sum + ar
    others = lambda f: f.reshape(N_COL, 2, POS, HALF)[:, 1].reshape(UNIT // 2, HALF)
    g_a = across(others(f_a))
    far = jnp.roll(br[UNIT:], -2, axis=0)
    f_b = jnp.concatenate([b_sum + br[:UNIT], b_total + far])
    g_b = across(jnp.concatenate([others(f_b[:UNIT]), f_b[UNIT:]]))
    flow = call(finish_body, (N_COL * POS * N_ROW, WIDTH), [SMEM] + [VMEM] * 4, nbytes=1 << 19)(
        place, f_a, f_b, g_a, g_b
    )
    return flow.reshape(1, N_COL, POS, N_ROW, 1, WIDTH)


def solution(mesh):
    placed = (P("row", "col", None, "dom"), P("row", "col", None, "dom"), P("dom"), P())
    return jax.shard_map(
        per_device,
        mesh=mesh,
        in_specs=placed,
        out_specs=P("row", None, "dom", None, "col", None),
        check_vma=False,
    )
```

time: 187 us -> 138 us (0.74)
  the two profiles are of different devices: /device:TPU:6 before, /device:TPU:1 now
where the time goes in v2:
time: 138 us; the launch traced here: 137 us
  starting transfers between devices  85.5 us (62%)
  waiting for transfers between devices  27.6 us (20%)
  local copies, waits for them, and re-layouts  12.3 us (9%)
  Pallas kernels  8.47 us (6%)
  other arithmetic  2.37 us (2%)
    ppermute x8, starting transfers between devices, along_z(): return lax.ppermute(a, ('dom', 'row'), pairs)  30.9 us
    ppermute x6, starting transfers between devices, across(): return lax.ppermute(a, 'row', [(i, i ^ 1) for i in range(N_ROW)])  28.6 us
    ppermute x6, starting transfers between devices, along_x(): lax.ppermute(a, 'col', [(i, (i + shift) % N_COL) for i in range(N_COL)])  17.6 us
    ppermute x3, waiting for transfers between devices, along_y(): lax.ppermute(a, 'row', [(i, (i + 2 * shift) % N_ROW) for i in range(N_ROW)])  15.8 us
    unnamed x40, local copies, waits for them, and re-layouts  11.3 us
    ppermute x6, waiting for transfers between devices, along_x(): lax.ppermute(a, 'col', [(i, (i + shift) % N_COL) for i in range(N_COL)])  8.51 us
    ppermute x3, starting transfers between devices, along_y(): lax.ppermute(a, 'row', [(i, (i + 2 * shift) % N_ROW) for i in range(N_ROW)])  8.41 us
    pallas_call x1, Pallas kernels, per_device(): call(functools.partial(block_body, with_totals=True), [(3 * UNIT + 8, HAL...  3.43 us
  transfers between devices with their start and end apart: 23, of which 7 were waited for; matrix products, arithmetic and copies ran while one was open for 2% of the time, Pallas kernels for 5%

profile of v2, /device:TPU:1, one launch (start us, length us, event | category | flops | bytes accessed | tf_op | source)
XLA Modules:
  0.0 136.8 jit_solution(13693645834755123735)
XLA Ops:
  0.0 0.7 copy-done.17
  0.7 1.0 copy-done.12
  1.7 0.6 shard_map.46
  2.4 8.8 %collective-permute-start = (f32[136,1024]{1,0:T(8,128)S(1)}, f32[136,1024]{1,0:T(8,128)S(1)}, u32[]{:S(2)}, u32[]{:S(2)}) collective-permute-start(f32[136,1024]{1,0:T(8,128)S(1)} %get-tuple-element.13.own.refs_4_.refs_8_), channel_id=1, source_target_pairs={{0,4},{4,0},{8,12},{12,8},{16,20},{20,16},{24,28},{28,24},{1,5},{5... | collective-permute-start | bytes 1671176 | tf_op jit(solution)/shard_map/ppermute | solution.py:133
  11.2 1.9 %collective-permute-start.6 = (f32[136,1024]{1,0:T(8,128)S(1)}, f32[136,1024]{1,0:T(8,128)S(1)}, u32[]{:S(2)}, u32[]{:S(2)}) collective-permute-start(f32[136,1024]{1,0:T(8,128)S(1)} %get-tuple-element.13.own.refs_4_.refs_8_), channel_id=1, source_target_pairs={{0,8},{4,12},{8,16},{12,20},{16,24},{20,28},{24,0},{28,4},{1,9},{5... | collective-permute-start | bytes 1671176 | tf_op jit(solution)/shard_map/ppermute | solution.py:129
  13.1 1.9 %collective-permute-start.5 = (f32[136,1024]{1,0:T(8,128)S(1)}, f32[136,1024]{1,0:T(8,128)S(1)}, u32[]{:S(2)}, u32[]{:S(2)}) collective-permute-start(f32[136,1024]{1,0:T(8,128)S(1)} %get-tuple-element.13.own.refs_4_.refs_8_), channel_id=1, source_target_pairs={{0,16},{4,20},{8,24},{12,28},{16,0},{20,4},{24,8},{28,12},{1,17},{... | collective-permute-start | bytes 1671176 | tf_op jit(solution)/shard_map/ppermute | solution.py:129
  15.0 4.6 %collective-permute-start.4 = (f32[136,1024]{1,0:T(8,128)S(1)}, f32[136,1024]{1,0:T(8,128)S(1)}, u32[]{:S(2)}, u32[]{:S(2)}) collective-permute-start(f32[136,1024]{1,0:T(8,128)S(1)} %get-tuple-element.13.own.refs_4_.refs_8_), channel_id=1, source_target_pairs={{0,24},{4,28},{8,0},{12,4},{16,8},{20,12},{24,16},{28,20},{1,25},{... | collective-permute-start | bytes 1671176 | tf_op jit(solution)/shard_map/ppermute | solution.py:129
  20.2 1.9 %collective-permute-start.3 = (f32[128,1024]{1,0:T(8,128)S(1)}, f32[128,1024]{1,0:T(8,128)S(1)}, u32[]{:S(2)}, u32[]{:S(2)}) collective-permute-start(f32[128,1024]{1,0:T(8,128)S(1)} %shard_map.47.refs_0_), channel_id=1, source_target_pairs={{0,1},{1,2},{2,3},{3,0},{4,5},{5,6},{6,7},{7,4},{8,9},{9,10},{10,1... | collective-permute-start | bytes 1572872 | tf_op jit(solution)/shard_map/ppermute | solution.py:125
  22.2 2.5 %collective-permute-start.2 = (f32[128,1024]{1,0:T(8,128)S(1)}, f32[128,1024]{1,0:T(8,128)S(1)}, u32[]{:S(2)}, u32[]{:S(2)}) collective-permute-start(f32[128,1024]{1,0:T(8,128)S(1)} %shard_map.47.refs_0_), channel_id=1, source_target_pairs={{0,2},{1,3},{2,0},{3,1},{4,6},{5,7},{6,4},{7,5},{8,10},{9,11},{10,... | collective-permute-start | bytes 1572872 | tf_op jit(solution)/shard_map/ppermute | solution.py:125
  24.6 15.8 %collective-permute-done.6.refs_7_.refs_11_ = f32[136,1024]{1,0:T(8,128)S(1)} collective-permute-done((f32[136,1024]{1,0:T(8,128)S(1)}, f32[136,1024]{1,0:T(8,128)S(1)}, u32[]{:S(2)}, u32[]{:S(2)}) %collective-permute-start.6) | collective-permute-done | bytes 557088 | tf_op jit(solution)/shard_map/ppermute | solution.py:129
  40.4 1.9 %collective-permute-start.1 = (f32[128,1024]{1,0:T(8,128)S(1)}, f32[128,1024]{1,0:T(8,128)S(1)}, u32[]{:S(2)}, u32[]{:S(2)}) collective-permute-start(f32[128,1024]{1,0:T(8,128)S(1)} %shard_map.47.refs_0_), channel_id=1, source_target_pairs={{0,3},{1,0},{2,1},{3,2},{4,7},{5,4},{6,5},{7,6},{8,11},{9,8},{10,9... | collective-permute-start | bytes 1572872 | tf_op jit(solution)/shard_map/ppermute | solution.py:125
  42.4 2.7 %collective-permute-start.13 = (f32[136,1024]{1,0:T(8,128)S(1)}, f32[136,1024]{1,0:T(8,128)S(1)}, u32[]{:S(2)}, u32[]{:S(2)}) collective-permute-start(f32[136,1024]{1,0:T(8,128)S(1)} %collective-permute-done.6.refs_7_.refs_11_), channel_id=1, source_target_pairs={{0,4},{4,0},{8,12},{12,8},{16,20},{20,16},{24,28},{28,24},{1,5},{5... | collective-permute-start | bytes 1671176 | tf_op jit(solution)/shard_map/ppermute | solution.py:133
  45.1 1.9 %collective-permute-start.12 = (f32[136,1024]{1,0:T(8,128)S(1)}, f32[136,1024]{1,0:T(8,128)S(1)}, u32[]{:S(2)}, u32[]{:S(2)}) collective-permute-start(f32[136,1024]{1,0:T(8,128)S(1)} %collective-permute-done.5.refs_6_.refs_10_), channel_id=1, source_target_pairs={{0,4},{4,0},{8,12},{12,8},{16,20},{20,16},{24,28},{28,24},{1,5},{5... | collective-permute-start | bytes 1671176 | tf_op jit(solution)/shard_map/ppermute | solution.py:133
  47.5 3.3 %collective-permute-start.11 = (f32[136,1024]{1,0:T(8,128)S(1)}, f32[136,1024]{1,0:T(8,128)S(1)}, u32[]{:S(2)}, u32[]{:S(2)}) collective-permute-start(f32[136,1024]{1,0:T(8,128)S(1)} %collective-permute-done.4.refs_5_.refs_9_), channel_id=1, source_target_pairs={{0,4},{4,0},{8,12},{12,8},{16,20},{20,16},{24,28},{28,24},{1,5},{5... | collective-permute-start | bytes 1671176 | tf_op jit(solution)/shard_map/ppermute | solution.py:133
  50.8 4.1 %collective-permute-done.1.refs_1_ = f32[128,1024]{1,0:T(8,128)S(1)} collective-permute-done((f32[128,1024]{1,0:T(8,128)S(1)}, f32[128,1024]{1,0:T(8,128)S(1)}, u32[]{:S(2)}, u32[]{:S(2)}) %collective-permute-start.1) | collective-permute-done | bytes 524320 | tf_op jit(solution)/shard_map/ppermute | solution.py:125
  55.0 2.6 %shard_map.48 = (f32[192,512]{1,0:T(8,128)}, f32[192,512]{1,0:T(8,128)S(1)}, f32[128,512]{1,0:T(8,128)S(1)}) custom-call(f32[128,1024]{1,0:T(8,128)S(1)} %shard_map.47.refs_0_, f32[128,1024]{1,0:T(8,128)S(1)} %collective-permute-done.1.refs_1_, f32[128,1024]{1,0:T(8,128)S(1)} %collective-permute-done.2.refs_2_, ...), custom_call_target="tpu_custom_call" | custom-call | flops 1610612736 | bytes 5242880 | tf_op jit(solution)/shard_map/pallas_call | solution.py:176
  57.6 0.8 copy-done.13
  58.3 3.0 %collective-permute-start.7 = (f32[192,512]{1,0:T(8,128)}, f32[192,512]{1,0:T(8,128)}, u32[]{:S(2)}, u32[]{:S(2)}) collective-permute-start(f32[192,512]{1,0:T(8,128)} %get-tuple-element.16), channel_id=1, source_target_pairs={{0,32},{4,484},{8,40},{12,492},{16,48},{20,500},{24,56},{28,508},{... | collective-permute-start | bytes 1179656 | tf_op jit(solution)/shard_map/ppermute | solution.py:142
  61.4 0.8 copy-done
  62.2 0.8 copy-done.2
  63.0 0.8 copy-done.4
  63.8 4.6 %collective-permute-start.16 = (f32[8,1024]{1,0:T(8,128)S(1)}, f32[8,1024]{1,0:T(8,128)S(1)}, u32[]{:S(2)}, u32[]{:S(2)}) collective-permute-start(f32[8,1024]{1,0:T(8,128)S(1)} %slice_add_fusion.8.refs_12_), channel_id=1, source_target_pairs={{0,2},{1,3},{2,0},{3,1},{4,6},{5,7},{6,4},{7,5},{8,10},{9,11},{10,... | collective-permute-start | bytes 98312 | tf_op jit(solution)/shard_map/ppermute | solution.py:125
  68.5 4.7 %collective-permute-start.15 = (f32[8,1024]{1,0:T(8,128)S(1)}, f32[8,1024]{1,0:T(8,128)S(1)}, u32[]{:S(2)}, u32[]{:S(2)}) collective-permute-start(f32[8,1024]{1,0:T(8,128)S(1)} %slice_add_fusion.8.refs_12_), channel_id=1, source_target_pairs={{0,3},{1,0},{2,1},{3,2},{4,7},{5,4},{6,5},{7,6},{8,11},{9,8},{10,9... | collective-permute-start | bytes 98312 | tf_op jit(solution)/shard_map/ppermute | solution.py:125
  73.2 1.9 %collective-permute-start.14 = (f32[8,1024]{1,0:T(8,128)S(1)}, f32[8,1024]{1,0:T(8,128)S(1)}, u32[]{:S(2)}, u32[]{:S(2)}) collective-permute-start(f32[8,1024]{1,0:T(8,128)S(1)} %slice_add_fusion.8.refs_12_), channel_id=1, source_target_pairs={{0,1},{1,2},{2,3},{3,0},{4,5},{5,6},{6,7},{7,4},{8,9},{9,10},{10,1... | collective-permute-start | bytes 98312 | tf_op jit(solution)/shard_map/ppermute | solution.py:125
  75.2 3.9 %collective-permute-done.14.refs_13_ = f32[8,1024]{1,0:T(8,128)S(1)} collective-permute-done((f32[8,1024]{1,0:T(8,128)S(1)}, f32[8,1024]{1,0:T(8,128)S(1)}, u32[]{:S(2)}, u32[]{:S(2)}) %collective-permute-start.14) | collective-permute-done | bytes 32800 | tf_op jit(solution)/shard_map/ppermute | solution.py:125
  79.1 1.1 copy-done.1
  80.1 1.1 copy-done.3
  81.2 1.1 copy-done.5
  82.2 1.0 copy-done.7
  83.3 1.0 copy-done.9
  84.3 1.0 copy-done.11
  85.4 3.4 %shard_map.49 = (f32[200,512]{1,0:T(8,128)S(1)}, f32[200,512]{1,0:T(8,128)S(1)}, f32[128,512]{1,0:T(8,128)S(1)}) custom-call(f32[128,1024]{1,0:T(8,128)S(1)} %shard_map.47.refs_0_, f32[128,1024]{1,0:T(8,128)S(1)} %copy-done.11, f32[128,1024]{1,0:T(8,128)S(1)} %copy-done.9, f32[128,1024]{1,0:T(8,128)S(1)} %copy-done.7, ...), custom_call_target="tpu_custom_call" | custom-call | flops 1610612736 | bytes 7340032 | tf_op jit(solution)/shard_map/pallas_call | solution.py:185
  88.8 2.8 %collective-permute-start.17 = (f32[200,512]{1,0:T(8,128)S(1)}, f32[200,512]{1,0:T(8,128)S(1)}, u32[]{:S(2)}, u32[]{:S(2)}) collective-permute-start(f32[200,512]{1,0:T(8,128)S(1)} %get-tuple-element.19), channel_id=1, source_target_pairs={{0,32},{4,484},{8,40},{12,492},{16,48},{20,500},{24,56},{28,508},{... | collective-permute-start | bytes 1228808 | tf_op jit(solution)/shard_map/ppermute | solution.py:142
  91.6 1.0 slice.144
  92.6 0.9 slice_select_fusion.1
  93.6 2.6 %collective-permute-start.8 = (f32[192,512]{1,0:T(8,128)S(1)}, f32[192,512]{1,0:T(8,128)S(1)}, u32[]{:S(2)}, u32[]{:S(2)}) collective-permute-start(f32[192,512]{1,0:T(8,128)S(1)} %maximum_add_fusion.1), channel_id=1, source_target_pairs={{0,32},{4,484},{8,40},{12,492},{16,48},{20,500},{24,56},{28,508},{... | collective-permute-start | bytes 1179656 | tf_op jit(solution)/shard_map/ppermute | solution.py:142
  96.2 1.7 %collective-permute-done.17 = f32[200,512]{1,0:T(8,128)S(1)} collective-permute-done((f32[200,512]{1,0:T(8,128)S(1)}, f32[200,512]{1,0:T(8,128)S(1)}, u32[]{:S(2)}, u32[]{:S(2)}) %collective-permute-start.17) | collective-permute-done | bytes 409632 | tf_op jit(solution)/shard_map/ppermute | solution.py:142
  98.0 3.5 %collective-permute-start.18 = (f32[200,512]{1,0:T(8,128)S(1)}, f32[200,512]{1,0:T(8,128)S(1)}, u32[]{:S(2)}, u32[]{:S(2)}) collective-permute-start(f32[200,512]{1,0:T(8,128)S(1)} %maximum_add_fusion), channel_id=1, source_target_pairs={{0,32},{4,484},{8,40},{12,492},{16,48},{20,500},{24,56},{28,508},{... | collective-permute-start | bytes 1228808 | tf_op jit(solution)/shard_map/ppermute | solution.py:142
  101.7 0.7 collective-permute-done.8
  102.4 4.7 %collective-permute-start.9 = (f32[64,512]{1,0:T(8,128)S(1)}, f32[64,512]{1,0:T(8,128)S(1)}, u32[]{:S(2)}, u32[]{:S(2)}) collective-permute-start(f32[64,512]{1,0:T(8,128)S(1)} %slice_add_fusion.5), channel_id=1, source_target_pairs={{0,96},{4,420},{8,104},{12,428},{16,112},{20,436},{24,120},{28,444... | collective-permute-start | bytes 393224 | tf_op jit(solution)/shard_map/ppermute | solution.py:142
  107.3 4.3 %collective-permute-start.19 = (f32[72,512]{1,0:T(8,128)S(1)}, f32[72,512]{1,0:T(8,128)S(1)}, u32[]{:S(2)}, u32[]{:S(2)}) collective-permute-start(f32[72,512]{1,0:T(8,128)S(1)} %pad_maximum_fusion), channel_id=1, source_target_pairs={{0,96},{4,420},{8,104},{12,428},{16,112},{20,436},{24,120},{28,444... | collective-permute-start | bytes 442376 | tf_op jit(solution)/shard_map/ppermute | solution.py:142
  111.7 4.7 %collective-permute-start.10 = (f32[64,512]{1,0:T(8,128)S(1)}, f32[64,512]{1,0:T(8,128)S(1)}, u32[]{:S(2)}, u32[]{:S(2)}) collective-permute-start(f32[64,512]{1,0:T(8,128)S(1)} %fusion), channel_id=1, source_target_pairs={{0,96},{4,420},{8,104},{12,428},{16,112},{20,436},{24,120},{28,444... | collective-permute-start | bytes 393224 | tf_op jit(solution)/shard_map/ppermute | solution.py:142
  116.4 5.2 %collective-permute-start.20 = (f32[72,512]{1,0:T(8,128)S(1)}, f32[72,512]{1,0:T(8,128)S(1)}, u32[]{:S(2)}, u32[]{:S(2)}) collective-permute-start(f32[72,512]{1,0:T(8,128)S(1)} %pad_maximum_fusion.1), channel_id=1, source_target_pairs={{0,96},{4,420},{8,104},{12,428},{16,112},{20,436},{24,120},{28,444... | collective-permute-start | bytes 442376 | tf_op jit(solution)/shard_map/ppermute | solution.py:142
  121.7 0.9 fusion.1.f_a
  122.6 8.8 %collective-permute-start.21 = (f32[32,512]{1,0:T(8,128)S(1)}, f32[32,512]{1,0:T(8,128)S(1)}, u32[]{:S(2)}, u32[]{:S(2)}) collective-permute-start(f32[32,512]{1,0:T(8,128)S(1)} %slice_bitcast_fusion.1), channel_id=1, source_target_pairs={{0,4},{4,0},{8,12},{12,8},{16,20},{20,16},{24,28},{28,24},{1,5},{5... | collective-permute-start | bytes 196616 | tf_op jit(solution)/shard_map/ppermute | solution.py:133
  131.6 3.1 %collective-permute-start.22 = (f32[40,512]{1,0:T(8,128)S(1)}, f32[40,512]{1,0:T(8,128)S(1)}, u32[]{:S(2)}, u32[]{:S(2)}) collective-permute-start(f32[40,512]{1,0:T(8,128)S(1)} %pad_maximum_fusion.3), channel_id=1, source_target_pairs={{0,4},{4,0},{8,12},{12,8},{16,20},{20,16},{24,28},{28,24},{1,5},{5... | collective-permute-start | bytes 245768 | tf_op jit(solution)/shard_map/ppermute | solution.py:133
  134.7 0.9 collective-permute-done.22.g_b
  135.6 1.3 shard_map.50
  (70 shorter events, 1.7 us)
Async XLA Ops:
  0.0 0.7 copy-start.17
  0.0 0.7 copy-start.18
  0.0 0.7 copy-start.19
  0.7 1.0 copy-start.12
  2.4 17.3 %collective-permute-start = (f32[136,1024]{1,0:T(8,128)S(1)}, f32[136,1024]{1,0:T(8,128)S(1)}, u32[]{:S(2)}, u32[]{:S(2)}) collective-permute-start(f32[136,1024]{1,0:T(8,128)S(1)} %get-tuple-element.13.own.refs_4_.refs_8_), channel_id=1, source_target_pairs={{0,4},{4,0},{8,12},{12,8},{16,20},{20,16},{24,28},{28,24},{1,5},{5... | collective-permute-start | bytes 1671176 | tf_op jit(solution)/shard_map/ppermute | solution.py:133
  11.2 29.3 %collective-permute-start.6 = (f32[136,1024]{1,0:T(8,128)S(1)}, f32[136,1024]{1,0:T(8,128)S(1)}, u32[]{:S(2)}, u32[]{:S(2)}) collective-permute-start(f32[136,1024]{1,0:T(8,128)S(1)} %get-tuple-element.13.own.refs_4_.refs_8_), channel_id=1, source_target_pairs={{0,8},{4,12},{8,16},{12,20},{16,24},{20,28},{24,0},{28,4},{1,9},{5... | collective-permute-start | bytes 1671176 | tf_op jit(solution)/shard_map/ppermute | solution.py:129
  13.1 29.3 %collective-permute-start.5 = (f32[136,1024]{1,0:T(8,128)S(1)}, f32[136,1024]{1,0:T(8,128)S(1)}, u32[]{:S(2)}, u32[]{:S(2)}) collective-permute-start(f32[136,1024]{1,0:T(8,128)S(1)} %get-tuple-element.13.own.refs_4_.refs_8_), channel_id=1, source_target_pairs={{0,16},{4,20},{8,24},{12,28},{16,0},{20,4},{24,8},{28,12},{1,17},{... | collective-permute-start | bytes 1671176 | tf_op jit(solution)/shard_map/ppermute | solution.py:129
  15.0 30.1 %collective-permute-start.4 = (f32[136,1024]{1,0:T(8,128)S(1)}, f32[136,1024]{1,0:T(8,128)S(1)}, u32[]{:S(2)}, u32[]{:S(2)}) collective-permute-start(f32[136,1024]{1,0:T(8,128)S(1)} %get-tuple-element.13.own.refs_4_.refs_8_), channel_id=1, source_target_pairs={{0,24},{4,28},{8,0},{12,4},{16,8},{20,12},{24,16},{28,20},{1,25},{... | collective-permute-start | bytes 1671176 | tf_op jit(solution)/shard_map/ppermute | solution.py:129
  20.2 27.2 %collective-permute-start.3 = (f32[128,1024]{1,0:T(8,128)S(1)}, f32[128,1024]{1,0:T(8,128)S(1)}, u32[]{:S(2)}, u32[]{:S(2)}) collective-permute-start(f32[128,1024]{1,0:T(8,128)S(1)} %shard_map.47.refs_0_), channel_id=1, source_target_pairs={{0,1},{1,2},{2,3},{3,0},{4,5},{5,6},{6,7},{7,4},{8,9},{9,10},{10,1... | collective-permute-start | bytes 1572872 | tf_op jit(solution)/shard_map/ppermute | solution.py:125
  22.2 28.7 %collective-permute-start.2 = (f32[128,1024]{1,0:T(8,128)S(1)}, f32[128,1024]{1,0:T(8,128)S(1)}, u32[]{:S(2)}, u32[]{:S(2)}) collective-permute-start(f32[128,1024]{1,0:T(8,128)S(1)} %shard_map.47.refs_0_), channel_id=1, source_target_pairs={{0,2},{1,3},{2,0},{3,1},{4,6},{5,7},{6,4},{7,5},{8,10},{9,11},{10,... | collective-permute-start | bytes 1572872 | tf_op jit(solution)/shard_map/ppermute | solution.py:125
  40.4 14.5 %collective-permute-start.1 = (f32[128,1024]{1,0:T(8,128)S(1)}, f32[128,1024]{1,0:T(8,128)S(1)}, u32[]{:S(2)}, u32[]{:S(2)}) collective-permute-start(f32[128,1024]{1,0:T(8,128)S(1)} %shard_map.47.refs_0_), channel_id=1, source_target_pairs={{0,3},{1,0},{2,1},{3,2},{4,7},{5,4},{6,5},{7,6},{8,11},{9,8},{10,9... | collective-permute-start | bytes 1572872 | tf_op jit(solution)/shard_map/ppermute | solution.py:125
  42.4 18.9 %collective-permute-start.13 = (f32[136,1024]{1,0:T(8,128)S(1)}, f32[136,1024]{1,0:T(8,128)S(1)}, u32[]{:S(2)}, u32[]{:S(2)}) collective-permute-start(f32[136,1024]{1,0:T(8,128)S(1)} %collective-permute-done.6.refs_7_.refs_11_), channel_id=1, source_target_pairs={{0,4},{4,0},{8,12},{12,8},{16,20},{20,16},{24,28},{28,24},{1,5},{5... | collective-permute-start | bytes 1671176 | tf_op jit(solution)/shard_map/ppermute | solution.py:133
  45.1 16.2 %collective-permute-start.12 = (f32[136,1024]{1,0:T(8,128)S(1)}, f32[136,1024]{1,0:T(8,128)S(1)}, u32[]{:S(2)}, u32[]{:S(2)}) collective-permute-start(f32[136,1024]{1,0:T(8,128)S(1)} %collective-permute-done.5.refs_6_.refs_10_), channel_id=1, source_target_pairs={{0,4},{4,0},{8,12},{12,8},{16,20},{20,16},{24,28},{28,24},{1,5},{5... | collective-permute-start | bytes 1671176 | tf_op jit(solution)/shard_map/ppermute | solution.py:133
  47.5 10.1 %copy-start.6 = (f32[128,1024]{1,0:T(8,128)}, f32[128,1024]{1,0:T(8,128)S(1)}, u32[]{:S(2)}) copy-start(f32[128,1024]{1,0:T(8,128)S(1)} %collective-permute-done.3.refs_3_) | copy-start | bytes 1572868
  47.5 13.8 %collective-permute-start.11 = (f32[136,1024]{1,0:T(8,128)S(1)}, f32[136,1024]{1,0:T(8,128)S(1)}, u32[]{:S(2)}, u32[]{:S(2)}) collective-permute-start(f32[136,1024]{1,0:T(8,128)S(1)} %collective-permute-done.4.refs_5_.refs_9_), channel_id=1, source_target_pairs={{0,4},{4,0},{8,12},{12,8},{16,20},{20,16},{24,28},{28,24},{1,5},{5... | collective-permute-start | bytes 1671176 | tf_op jit(solution)/shard_map/ppermute | solution.py:133
  50.8 6.7 %copy-start.8 = (f32[128,1024]{1,0:T(8,128)}, f32[128,1024]{1,0:T(8,128)S(1)}, u32[]{:S(2)}) copy-start(f32[128,1024]{1,0:T(8,128)S(1)} %collective-permute-done.2.refs_2_) | copy-start | bytes 1572868
  55.0 2.6 %copy-start.10 = (f32[128,1024]{1,0:T(8,128)}, f32[128,1024]{1,0:T(8,128)S(1)}, u32[]{:S(2)}) copy-start(f32[128,1024]{1,0:T(8,128)S(1)} %collective-permute-done.1.refs_1_) | copy-start | bytes 1572868
  57.6 0.8 copy-start.13
  58.3 3.0 %copy-start.15 = (f32[128,512]{1,0:T(8,128)}, f32[128,512]{1,0:T(8,128)S(1)}, u32[]{:S(2)}) copy-start(f32[128,512]{1,0:T(8,128)S(1)} %get-tuple-element.17) | copy-start | bytes 786436
  58.3 33.2 %collective-permute-start.7 = (f32[192,512]{1,0:T(8,128)}, f32[192,512]{1,0:T(8,128)}, u32[]{:S(2)}, u32[]{:S(2)}) collective-permute-start(f32[192,512]{1,0:T(8,128)} %get-tuple-element.16), channel_id=1, source_target_pairs={{0,32},{4,484},{8,40},{12,492},{16,48},{20,500},{24,56},{28,508},{... | collective-permute-start | bytes 1179656 | tf_op jit(solution)/shard_map/ppermute | solution.py:142
  61.4 0.8 copy-start
  62.2 0.8 copy-start.2
  63.0 0.8 copy-start.4
  63.8 11.3 %collective-permute-start.16 = (f32[8,1024]{1,0:T(8,128)S(1)}, f32[8,1024]{1,0:T(8,128)S(1)}, u32[]{:S(2)}, u32[]{:S(2)}) collective-permute-start(f32[8,1024]{1,0:T(8,128)S(1)} %slice_add_fusion.8.refs_12_), channel_id=1, source_target_pairs={{0,2},{1,3},{2,0},{3,1},{4,6},{5,7},{6,4},{7,5},{8,10},{9,11},{10,... | collective-permute-start | bytes 98312 | tf_op jit(solution)/shard_map/ppermute | solution.py:125
  68.5 6.7 %collective-permute-start.15 = (f32[8,1024]{1,0:T(8,128)S(1)}, f32[8,1024]{1,0:T(8,128)S(1)}, u32[]{:S(2)}, u32[]{:S(2)}) collective-permute-start(f32[8,1024]{1,0:T(8,128)S(1)} %slice_add_fusion.8.refs_12_), channel_id=1, source_target_pairs={{0,3},{1,0},{2,1},{3,2},{4,7},{5,4},{6,5},{7,6},{8,11},{9,8},{10,9... | collective-permute-start | bytes 98312 | tf_op jit(solution)/shard_map/ppermute | solution.py:125
  73.2 5.9 %collective-permute-start.14 = (f32[8,1024]{1,0:T(8,128)S(1)}, f32[8,1024]{1,0:T(8,128)S(1)}, u32[]{:S(2)}, u32[]{:S(2)}) collective-permute-start(f32[8,1024]{1,0:T(8,128)S(1)} %slice_add_fusion.8.refs_12_), channel_id=1, source_target_pairs={{0,1},{1,2},{2,3},{3,0},{4,5},{5,6},{6,7},{7,4},{8,9},{9,10},{10,1... | collective-permute-start | bytes 98312 | tf_op jit(solution)/shard_map/ppermute | solution.py:125
  79.1 1.1 copy-start.1
  80.1 1.1 copy-start.3
  81.2 1.1 copy-start.5
  82.2 1.0 copy-start.7
  83.3 1.0 copy-start.9
  84.3 1.0 copy-start.11
  88.8 4.7 %copy-start.14 = (f32[192,512]{1,0:T(8,128)S(1)}, f32[192,512]{1,0:T(8,128)}, u32[]{:S(2)}) copy-start(f32[192,512]{1,0:T(8,128)} %copy-done.13) | copy-start | bytes 1179652
  88.8 9.1 %collective-permute-start.17 = (f32[200,512]{1,0:T(8,128)S(1)}, f32[200,512]{1,0:T(8,128)S(1)}, u32[]{:S(2)}, u32[]{:S(2)}) collective-permute-start(f32[200,512]{1,0:T(8,128)S(1)} %get-tuple-element.19), channel_id=1, source_target_pairs={{0,32},{4,484},{8,40},{12,492},{16,48},{20,500},{24,56},{28,508},{... | collective-permute-start | bytes 1228808 | tf_op jit(solution)/shard_map/ppermute | solution.py:142
  93.6 8.8 %collective-permute-start.8 = (f32[192,512]{1,0:T(8,128)S(1)}, f32[192,512]{1,0:T(8,128)S(1)}, u32[]{:S(2)}, u32[]{:S(2)}) collective-permute-start(f32[192,512]{1,0:T(8,128)S(1)} %maximum_add_fusion.1), channel_id=1, source_target_pairs={{0,32},{4,484},{8,40},{12,492},{16,48},{20,500},{24,56},{28,508},{... | collective-permute-start | bytes 1179656 | tf_op jit(solution)/shard_map/ppermute | solution.py:142
  98.0 4.4 %copy-start.16 = (f32[128,512]{1,0:T(8,128)S(1)}, f32[128,512]{1,0:T(8,128)}, u32[]{:S(2)}) copy-start(f32[128,512]{1,0:T(8,128)} %copy-done.15) | copy-start | bytes 786436
  98.0 9.1 %collective-permute-start.18 = (f32[200,512]{1,0:T(8,128)S(1)}, f32[200,512]{1,0:T(8,128)S(1)}, u32[]{:S(2)}, u32[]{:S(2)}) collective-permute-start(f32[200,512]{1,0:T(8,128)S(1)} %maximum_add_fusion), channel_id=1, source_target_pairs={{0,32},{4,484},{8,40},{12,492},{16,48},{20,500},{24,56},{28,508},{... | collective-permute-start | bytes 1228808 | tf_op jit(solution)/shard_map/ppermute | solution.py:142
  102.4 9.2 %collective-permute-start.9 = (f32[64,512]{1,0:T(8,128)S(1)}, f32[64,512]{1,0:T(8,128)S(1)}, u32[]{:S(2)}, u32[]{:S(2)}) collective-permute-start(f32[64,512]{1,0:T(8,128)S(1)} %slice_add_fusion.5), channel_id=1, source_target_pairs={{0,96},{4,420},{8,104},{12,428},{16,112},{20,436},{24,120},{28,444... | collective-permute-start | bytes 393224 | tf_op jit(solution)/shard_map/ppermute | solution.py:142
  107.3 9.1 %collective-permute-start.19 = (f32[72,512]{1,0:T(8,128)S(1)}, f32[72,512]{1,0:T(8,128)S(1)}, u32[]{:S(2)}, u32[]{:S(2)}) collective-permute-start(f32[72,512]{1,0:T(8,128)S(1)} %pad_maximum_fusion), channel_id=1, source_target_pairs={{0,96},{4,420},{8,104},{12,428},{16,112},{20,436},{24,120},{28,444... | collective-permute-start | bytes 442376 | tf_op jit(solution)/shard_map/ppermute | solution.py:142
  111.7 10.0 %collective-permute-start.10 = (f32[64,512]{1,0:T(8,128)S(1)}, f32[64,512]{1,0:T(8,128)S(1)}, u32[]{:S(2)}, u32[]{:S(2)}) collective-permute-start(f32[64,512]{1,0:T(8,128)S(1)} %fusion), channel_id=1, source_target_pairs={{0,96},{4,420},{8,104},{12,428},{16,112},{20,436},{24,120},{28,444... | collective-permute-start | bytes 393224 | tf_op jit(solution)/shard_map/ppermute | solution.py:142
  116.4 15.0 %collective-permute-start.20 = (f32[72,512]{1,0:T(8,128)S(1)}, f32[72,512]{1,0:T(8,128)S(1)}, u32[]{:S(2)}, u32[]{:S(2)}) collective-permute-start(f32[72,512]{1,0:T(8,128)S(1)} %pad_maximum_fusion.1), channel_id=1, source_target_pairs={{0,96},{4,420},{8,104},{12,428},{16,112},{20,436},{24,120},{28,444... | collective-permute-start | bytes 442376 | tf_op jit(solution)/shard_map/ppermute | solution.py:142
  122.6 12.1 %collective-permute-start.21 = (f32[32,512]{1,0:T(8,128)S(1)}, f32[32,512]{1,0:T(8,128)S(1)}, u32[]{:S(2)}, u32[]{:S(2)}) collective-permute-start(f32[32,512]{1,0:T(8,128)S(1)} %slice_bitcast_fusion.1), channel_id=1, source_target_pairs={{0,4},{4,0},{8,12},{12,8},{16,20},{20,16},{24,28},{28,24},{1,5},{5... | collective-permute-start | bytes 196616 | tf_op jit(solution)/shard_map/ppermute | solution.py:133
  131.6 4.0 %collective-permute-start.22 = (f32[40,512]{1,0:T(8,128)S(1)}, f32[40,512]{1,0:T(8,128)S(1)}, u32[]{:S(2)}, u32[]{:S(2)}) collective-permute-start(f32[40,512]{1,0:T(8,128)S(1)} %pad_maximum_fusion.3), channel_id=1, source_target_pairs={{0,4},{4,0},{8,12},{12,8},{16,20},{20,16},{24,28},{28,24},{1,5},{5... | collective-permute-start | bytes 245768 | tf_op jit(solution)/shard_map/ppermute | solution.py:133

commit v3 on v1

v3 whole, which is shorter than its diff:
```python
import functools

import jax
import jax.numpy as jnp
from jax import lax
from jax.experimental import pallas as pl
from jax.experimental.pallas import tpu as pltpu
from jax.sharding import PartitionSpec as P

TILE = 128
N_DOM, N_ROW, N_COL = 16, 8, 4
WIDTH = 128
PANEL = 1024
POS = WIDTH // N_DOM
PAIR = 2 * WIDTH
EARLY_ROWS, EARLY_COLS = 3 * 2 * POS, 3 * PAIR
LATE_ROWS, LATE_COLS = 2 * 2 * POS + 3 * POS, 2 * PAIR
TOTALS = 8
PART = N_COL * POS
PROT = N_ROW * N_COL * WIDTH
VMEM = pl.BlockSpec(memory_space=pltpu.VMEM)
HBM = pl.BlockSpec(memory_space=pltpu.HBM)
F32 = jnp.float32
BF16 = jnp.bfloat16


def call(body, outs, operands, in_hbm=False, mib=4, flops=0, nbytes=1 << 19, scratch=()):
    return pl.pallas_call(
        body,
        out_shape=[
            jax.ShapeDtypeStruct(s[:-1], BF16) if s[-1] is BF16 else jax.ShapeDtypeStruct(s, F32) for s in outs
        ],
        in_specs=[HBM if in_hbm else VMEM] * len(operands),
        out_specs=[VMEM] * len(outs),
        scratch_shapes=list(scratch),
        compiler_params=pltpu.CompilerParams(vmem_limit_bytes=mib << 20),
        cost_estimate=pl.CostEstimate(flops=flops, bytes_accessed=nbytes, transcendentals=0),
    )(*operands)


def core_of():
    return lax.rem(lax.axis_index("row"), 2)


def mask_body(*refs):
    sources, (own, sums, weights), targets, done = refs[:4], refs[4:7], refs[7:11], refs[11]
    copies = [pltpu.make_async_copy(a, b, done.at[i]) for i, (a, b) in enumerate(zip(sources, targets))]
    for copy in copies:
        copy.start()
    for copy in copies[1:]:
        copy.wait()
    panel, tile_mask, classes, class_weight = targets
    of = classes[...]
    found = jnp.zeros((1, PANEL), F32)
    for k in range(class_weight.shape[1]):
        found = jnp.where(of == k, class_weight[0, k], found)
    weights[...] = found
    copies[0].wait()
    for t in range(PANEL // TILE):
        at = pl.ds(t * TILE, TILE)
        kept = panel[:, at] * tile_mask[0, t].astype(F32)
        own[:, at] = kept
        sums[:, at] = jnp.broadcast_to(jnp.sum(kept, axis=0, keepdims=True), (8, TILE))


def join_body(own, other, chip, again):
    for out in (chip, again):
        out[pl.ds(0, WIDTH), :] = own[...]
        out[pl.ds(WIDTH, WIDTH), :] = other[...]


def add_body(a, b, out):
    out[...] = a[...] + b[...]


def put_body(a, b, panels, out, sums):
    sums[...] = a[...] + b[...]
    out[pl.ds(0, 2 * WIDTH), :] = panels[pl.ds(0, 2 * WIDTH), :]
    out[pl.ds(2 * WIDTH, 8), :] = sums[...]


def split(x):
    high = x.astype(BF16)
    return high, (x - high.astype(F32)).astype(BF16)


def dot3(ah, al, bh, bl):
    dims = (((1,), (1,)), ((), ()))
    dot = functools.partial(lax.dot_general, dimension_numbers=dims, preferred_element_type=F32)
    return dot(ah, bh) + (dot(ah, bl) + dot(al, bh))


def fill_rows(ph, pl_, weights, start, source, swapped):
    z, core = lax.axis_index("dom"), core_of()
    w = weights[...]
    first, second = (WIDTH, 0) if swapped else (0, WIDTH)
    for j in range(8):
        ahead = z + 8 - j
        behind = z if j == 0 else z + 8 + j
        at = lax.rem(jnp.where(core == 0, ahead, behind), N_DOM) * POS
        mine = source[pl.ds(pl.multiple_of(at + first, POS), POS), :]
        theirs = source[pl.ds(pl.multiple_of(at + second, POS), POS), :]
        to = pl.ds(start + j * 2 * POS, 2 * POS)
        ph[to, :], pl_[to, :] = split(jnp.concatenate([mine, theirs], axis=0) * w)


def fill_columns(qh, ql, start, source, swapped):
    for g in range(2):
        at, of = pl.ds(start + g * WIDTH, WIDTH), pl.ds((1 - g if swapped else g) * WIDTH, WIDTH)
        qh[at, :], ql[at, :] = split(source[of, :])


def early_body(chip, *refs):
    sent, swap, weights = refs[:2], refs[2:4], refs[4]
    outs, (ph, pl_, qh, ql) = refs[5:8], refs[8:]
    core = core_of()
    fill_rows(ph, pl_, weights, 0, chip, False)
    fill_columns(qh, ql, 0, chip, False)

    @pl.when(core == 0)
    def _():
        for i in range(2):
            fill_rows(ph, pl_, weights, (i + 1) * WIDTH, swap[i], True)
            fill_columns(qh, ql, (i + 1) * PAIR, sent[i], False)

    @pl.when(core == 1)
    def _():
        for i in range(2):
            fill_rows(ph, pl_, weights, (i + 1) * WIDTH, sent[i], False)
            fill_columns(qh, ql, (i + 1) * PAIR, swap[i], True)

    block = dot3(ph[...], pl_[...], qh[...], ql[...])
    for i in range(3):
        for j in range(8):
            rows = i * WIDTH + j * 2 * POS
            at = pl.ds((j // 3) * EARLY_ROWS + i * 2 * POS, 2 * POS)
            outs[j % 3][at, :] = block[rows : rows + 2 * POS]


def late_body(sent, swap, weights, ph, pl_, qh, ql, sums, first, second, third, fh, fl, gh, gl):
    core = core_of()

    @pl.when(core == 0)
    def _():
        fill_rows(fh, fl, weights, 0, swap, True)
        fill_columns(gh, gl, 0, sent, False)

    @pl.when(core == 1)
    def _():
        fill_rows(fh, fl, weights, 0, sent, False)
        fill_columns(gh, gl, 0, swap, True)

    total = (sums[...] + swap[pl.ds(2 * WIDTH, 8), :]) * weights[...]
    at = pl.ds(WIDTH, 16)
    fh[at, :], fl[at, :] = split(jnp.concatenate([total, total], axis=0))
    late_early = dot3(fh[...], fl[...], qh[...], ql[...])
    late_late = dot3(fh[...], fl[...], gh[...], gl[...])
    early_late = dot3(ph[...], pl_[...], gh[...], gl[...])
    for j in range(8):
        out, start = (first, second, third)[j % 3], (j // 3) * LATE_ROWS
        rows = slice(j * 2 * POS, (j + 1) * 2 * POS)
        out[pl.ds(start, 2 * POS), :] = late_early[rows, : 2 * PAIR]
        at = pl.ds(start + 2 * POS, 2 * POS)
        out[at, pl.ds(0, PAIR)] = late_early[rows, 2 * PAIR :]
        out[at, pl.ds(PAIR, PAIR)] = late_late[rows]
        for i in range(3):
            for g in range(2):
                begin = i * WIDTH + j * 2 * POS + g * POS
                at = pl.ds(start + 4 * POS + i * POS, POS)
                out[at, pl.ds(g * PAIR, PAIR)] = early_late[begin : begin + POS]
    head = late_early[WIDTH : WIDTH + 8, : 2 * PAIR]
    tail = jnp.concatenate([late_early[WIDTH : WIDTH + 8, 2 * PAIR :], late_late[WIDTH : WIDTH + 8]], axis=1)
    odd = lax.broadcasted_iota(jnp.int32, (TOTALS, LATE_COLS), 0) % 2 == 1
    share = jnp.where(odd, tail, head)
    first[pl.ds(3 * LATE_ROWS, TOTALS), :] = share
    second[pl.ds(3 * LATE_ROWS, TOTALS), :] = share


def second_body(u, r, out, unit):
    far = (core_of() == 0).astype(F32)
    head, tail = pl.ds(0, unit), pl.ds(unit, u.shape[0] - unit)
    out[head, :] = u[head, :] + r[head, :] * far
    out[tail, :] = u[tail, :] + r[tail, :]


def third_body(u2, r2, *refs, unit):
    out = refs[-1]
    out[pl.ds(0, unit), :] = u2[pl.ds(0, unit), :] + r2[pl.ds(0, unit), :]
    if len(refs) == 3:
        u1, s2 = refs[:2]
        at = pl.ds(3 * unit, TOTALS)
        wide = u1[at, :] + r2[at, :]
        narrow = (lax.broadcasted_iota(jnp.int32, wide.shape, 0) >= 2) & (core_of() == 1)
        out[pl.ds(unit, TOTALS), :] = jnp.where(narrow, s2[at, :], wide)


def fourth_body(u2, r2, r3, out, unit):
    at = pl.ds(unit, unit)
    out[pl.ds(0, unit), :] = u2[at, :] + r2[at, :] + r3[pl.ds(0, unit), :]
    if out.shape[0] > unit:
        out[pl.ds(unit, TOTALS), :] = r3[pl.ds(unit, TOTALS), :]


def give_body(u0a, r2a, r4a, u0b, r2b, r3b, r4b, give, keep):
    late = (core_of() == 1).astype(F32)

    def early(start, to):
        at, of = pl.ds(start, POS), pl.ds(2 * EARLY_ROWS + start, POS)
        return r2a[of, to] + u0a[at, to] * late + r4a[at, to]

    def other(start, to):
        at, of = pl.ds(start, POS), pl.ds(2 * LATE_ROWS + start, POS)
        return r2b[of, to] + u0b[at, to] * late + r4b[at, to]

    def pairs(k, count=1):
        return pl.ds(k * PAIR, count * PAIR)

    for g, out in enumerate((keep, give)):
        for n in range(3):
            at = pl.ds(n * POS, POS)
            out[at, pairs(0, 3)] = early(n * 2 * POS + g * POS, pairs(0, 3))
            out[at, pairs(3)] = other(4 * POS + n * POS, pairs(g))
        at = pl.ds(3 * POS, POS)
        out[at, pairs(0, 2)] = other(g * POS, pairs(0, 2))
        out[at, pairs(2, 2)] = other(2 * POS + g * POS, pairs(0, 2))
    at = pl.ds(3 * LATE_ROWS, TOTALS)
    sums = r2b[at, :] + u0b[at, :] * late
    for k in range(2):
        total = sums[k : k + 1] + r3b[pl.ds(LATE_ROWS + k, 1), :] + r4b[pl.ds(LATE_ROWS + 2 + k, 1), :]
        for out in (keep, give):
            out[pl.ds(PART, 1), pairs(2 * k, 2)] = total


def finish_body(keep, here, out):
    x, r, z = lax.axis_index("col"), lax.axis_index("row"), lax.axis_index("dom")
    core = lax.rem(r, 2)
    y = lax.div(r, 2)
    lanes = lax.broadcasted_iota(jnp.int32, (POS, WIDTH), 1)
    rows = lax.broadcasted_iota(jnp.int32, (POS, WIDTH), 0)
    unit = (lanes == z * POS + rows).astype(F32)
    for m in range(4):
        for g in range(2):
            mine, theirs = pl.ds(m * PAIR + g * WIDTH, WIDTH), pl.ds(m * PAIR + (1 - g) * WIDTH, WIDTH)
            total = keep[pl.ds(PART, 1), mine] + here[pl.ds(PART, 1), theirs]
            scale = PROT / (total + 1.0)
            group = 2 * lax.rem(y + m, 4) + (core if g == 0 else 1 - core)
            for n in range(N_COL):
                at = pl.ds(n * POS, POS)
                block = keep[at, mine] + here[at, theirs]
                if n == 0 and m == 0 and g == 0:
                    block = block + unit
                place = lax.rem(x + n, N_COL) * (POS * N_ROW) + group
                out[pl.ds(place, POS, stride=N_ROW), :] = block * scale


def across(a):
    return lax.ppermute(a, "row", [(i, i ^ 1) for i in range(N_ROW)])


def around(a, shift):
    pairs = []
    for r in range(N_ROW):
        for c in range(N_COL):
            to = ((r + 2 * shift) % N_ROW, c) if r % 2 == 0 else (r, (c + shift) % N_COL)
            pairs.append((r * N_COL + c, to[0] * N_COL + to[1]))
    return lax.ppermute(a, ("row", "col"), pairs)


def doubled(a, bit):
    pairs = []
    for r in range(N_ROW):
        for c in range(N_COL):
            to = (r, c ^ bit) if r % 2 == 0 else (r ^ (2 * bit), c)
            pairs.append((r * N_COL + c, to[0] * N_COL + to[1]))
    return lax.ppermute(a, ("row", "col"), pairs)


def after(a, *done):
    return lax.optimization_barrier((a, *done))[0]


def along_z(a, shift):
    pairs = []
    for z in range(N_DOM):
        for r in range(N_ROW):
            to = (z + (shift if r % 2 == 0 else -shift)) % N_DOM
            pairs.append((z * N_ROW + r, to * N_ROW + r))
    return lax.ppermute(a, ("dom", "row"), pairs)


def per_device(protein_panel, tile_mask, domain_class, class_weight):
    tiles, classes = PANEL // TILE, class_weight.shape[0]
    own, sums, weights = call(
        mask_body,
        [(WIDTH, PANEL), (8, PANEL), (1, PANEL)],
        [
            protein_panel.reshape(WIDTH, PANEL),
            tile_mask.reshape(1, tiles),
            domain_class.reshape(1, PANEL),
            class_weight.reshape(1, classes),
        ],
        in_hbm=True, mib=4,
        scratch=[
            pltpu.VMEM((WIDTH, PANEL), F32),
            pltpu.SMEM((1, tiles), jnp.int32),
            pltpu.VMEM((1, PANEL), jnp.int32),
            pltpu.SMEM((1, classes), F32),
            pltpu.SemaphoreType.DMA((4,)),
        ],
    )
    other = across(own)
    chip, again = call(join_body, [(2 * WIDTH, PANEL), (2 * WIDTH + 24, PANEL)], [own, other])
    from_next, from_far, from_last = around(chip, -1), around(chip, 2), around(again, 1)

    def both(a, bit):
        return call(add_body, [(8, PANEL)], [a, doubled(a, bit)])[0]

    sums = both(both(sums, 1), 2)
    swap_next = across(after(from_next, sums))
    sums = across(sums)
    swap_far = across(after(from_far, sums))
    sums = both(sums, 1)
    early, columns = (3 * WIDTH, PANEL, BF16), (EARLY_COLS, PANEL, BF16)
    a0, a1, a2, ph, pl_, qh, ql = call(
        early_body,
        [(k * EARLY_ROWS, EARLY_COLS) for k in (3, 3, 2)] + [early, early, columns, columns],
        [chip, from_next, from_far, swap_next, swap_far, weights],
        mib=16, nbytes=8 << 20,
    )
    ar1 = along_z(a0, 1)
    from_last, sums = call(put_body, [(2 * WIDTH + 8, PANEL), (8, PANEL)], [sums, doubled(sums, 2), after(from_last, a0)])
    swap_last = across(from_last)
    b0, b1, b2 = call(
        late_body,
        [(3 * LATE_ROWS + TOTALS, LATE_COLS), (3 * LATE_ROWS + TOTALS, LATE_COLS), (2 * LATE_ROWS, LATE_COLS)],
        [from_last, swap_last, weights, ph, pl_, qh, ql, sums],
        mib=16, nbytes=0,
        scratch=[pltpu.VMEM((WIDTH + 16, PANEL), BF16)] * 2 + [pltpu.VMEM((PAIR, PANEL), BF16)] * 2,
    )
    br1 = along_z(b0, 1)
    of_a, of_b = {"unit": EARLY_ROWS}, {"unit": LATE_ROWS}
    with_unit = functools.partial
    (as2,) = call(with_unit(second_body, **of_a), [a1.shape], [a1, ar1])
    ar2 = along_z(as2, 1)
    (bs2,) = call(with_unit(second_body, **of_b), [b1.shape], [b1, br1])
    br2 = along_z(bs2, 1)
    (as3,) = call(with_unit(third_body, **of_a), [(EARLY_ROWS, EARLY_COLS)], [a2, ar2])
    ar3 = along_z(as3, 3)
    (bs3,) = call(with_unit(third_body, **of_b), [(LATE_ROWS + TOTALS, LATE_COLS)], [b2, br2, b1, bs2])
    br3 = along_z(bs3, 3)
    (as4,) = call(with_unit(fourth_body, **of_a), [(EARLY_ROWS, EARLY_COLS)], [a2, ar2, ar3])
    ar4 = along_z(as4, 3)
    (bs4,) = call(with_unit(fourth_body, **of_b), [(LATE_ROWS + TOTALS, LATE_COLS)], [b2, br2, br3])
    br4 = along_z(bs4, 3)
    give, keep = call(give_body, [(PART + TOTALS, 4 * PAIR)] * 2, [a0, ar2, ar4, b0, br2, br3, br4])
    (flow,) = call(finish_body, [(N_COL * POS * N_ROW, WIDTH)], [keep, across(give)])
    return flow.reshape(1, N_COL, POS, N_ROW, 1, WIDTH)


def solution(mesh):
    placed = (P("row", "col", None, "dom"), P("row", "col", None, "dom"), P("dom"), P())
    return jax.shard_map(
        per_device,
        mesh=mesh,
        in_specs=placed,
        out_specs=P("row", None, "dom", None, "col", None),
        check_vma=False,
    )
```

time: 187 us -> 120 us (0.64)
  waiting for transfers between devices: 142 us -> 48.8 us
  starting transfers between devices: 0.09 us -> 57.8 us
  between operations: 13.2 us -> 0.27 us
  matrix products: 12.4 us -> 0 us
  other arithmetic: 10.4 us -> 0 us
  Pallas kernels: 0 us -> 7.92 us
  blocking collectives: 7.48 us -> 0 us
  local copies, waits for them, and re-layouts: 1.04 us -> 3.04 us
    reduce_scatter x1 -> x0, waiting for transfers between devices: 76.6 us -> none  [per_device(): lax.psum_scatter(jnp.concatenate([block, extra], axis=1), 'dom', scatter_...]
    all_gather x2 -> x0, waiting for transfers between devices: 65.3 us -> none  [the longest x1 42.1 us: per_device(): q = lax.all_gather(masked, 'row', axis=0, tiled=True)]
    ppermute x0 -> x21, starting transfers between devices: none -> 57.8 us  [the longest x8 21.7 us: along_z(): return lax.ppermute(a, ('dom', 'row'), pairs)]
    ppermute x0 -> x21, waiting for transfers between devices: none -> 48.8 us  [the longest x8 33.3 us: along_z(): return lax.ppermute(a, ('dom', 'row'), pairs)]
    dot_general x3 -> x0, matrix products: 12.4 us -> none  [the longest x1 6.32 us: per_device(): block = jnp.einsum('pd,qd->pq', weighted, q, precision=lax.Precision.HIGH)]
    pallas_call x0 -> x16, Pallas kernels: none -> 7.92 us  [call(): pl.pallas_call(body, out_shape=[jax.ShapeDtypeStruct(s[:-1], BF16) if s[-...]
    psum x1 -> x0, blocking collectives: 7.48 us -> none  [per_device(): sums = lax.psum(jnp.sum(q, axis=0), 'col')]
    mul x4 -> x0, other arithmetic: 4.67 us -> none  [the longest x2 3.79 us: per_device(): masked = protein_panel.reshape(width, panel_cols) * mask]
  transfers between devices with their start and end apart: 3 -> 21, of which waited for: 3 -> 16; matrix products, arithmetic and copies ran while one was open for 6% -> 0% of each run, Pallas kernels for 0% -> 5%
where the time goes in v3:
time: 120 us; the launch traced here: 118 us
  starting transfers between devices  57.8 us (48%)
  waiting for transfers between devices  48.8 us (41%)
  Pallas kernels  7.92 us (7%)
  local copies, waits for them, and re-layouts  3.04 us (3%)
    ppermute x8, waiting for transfers between devices, along_z(): return lax.ppermute(a, ('dom', 'row'), pairs)  33.3 us
    ppermute x8, starting transfers between devices, along_z(): return lax.ppermute(a, ('dom', 'row'), pairs)  21.7 us
    ppermute x4, starting transfers between devices, doubled(): return lax.ppermute(a, ('row', 'col'), pairs)  13.4 us
    ppermute x6, starting transfers between devices, across(): return lax.ppermute(a, 'row', [(i, i ^ 1) for i in range(N_ROW)])  11.7 us
    ppermute x3, starting transfers between devices, around(): return lax.ppermute(a, ('row', 'col'), pairs)  10.9 us
    pallas_call x16, Pallas kernels, call(): pl.pallas_call(body, out_shape=[jax.ShapeDtypeStruct(s[:-1], BF16) if s[-...  7.92 us
    ppermute x4, waiting for transfers between devices, doubled(): return lax.ppermute(a, ('row', 'col'), pairs)  7.79 us
    ppermute x6, waiting for transfers between devices, across(): return lax.ppermute(a, 'row', [(i, i ^ 1) for i in range(N_ROW)])  4.31 us
  transfers between devices with their start and end apart: 21, of which 16 were waited for; matrix products, arithmetic and copies ran while one was open for 0% of the time, Pallas kernels for 5%

profile of v3, /device:TPU:6, one launch (start us, length us, event | category | flops | bytes accessed | tf_op | source)
XLA Modules:
  0.0 117.7 jit_solution(18178985407691235539)
XLA Ops:
  0.0 1.0 copy-done
  1.0 0.7 copy-done.1
  1.7 0.7 copy-done.2
  2.4 0.7 copy-done.3
  3.0 0.7 shard_map.46
  3.8 1.9 %collective-permute-start = (f32[128,1024]{1,0:T(8,128)S(1)}, f32[128,1024]{1,0:T(8,128)S(1)}, u32[]{:S(2)}, u32[]{:S(2)}) collective-permute-start(f32[128,1024]{1,0:T(8,128)S(1)} %get-tuple-element.27.own), channel_id=1, source_target_pairs={{0,4},{4,0},{8,12},{12,8},{16,20},{20,16},{24,28},{28,24},{1,5},{5... | collective-permute-start | bytes 1572872 | tf_op jit(solution)/shard_map/ppermute | solution.py:257
  5.7 1.9 %collective-permute-done.other = f32[128,1024]{1,0:T(8,128)S(1)} collective-permute-done((f32[128,1024]{1,0:T(8,128)S(1)}, f32[128,1024]{1,0:T(8,128)S(1)}, u32[]{:S(2)}, u32[]{:S(2)}) %collective-permute-start) | collective-permute-done | bytes 524320 | tf_op jit(solution)/shard_map/ppermute | solution.py:257
  7.6 0.1 shard_map.47
  7.7 5.1 %collective-permute-start.2 = (f32[256,1024]{1,0:T(8,128)S(1)}, f32[256,1024]{1,0:T(8,128)S(1)}, u32[]{:S(2)}, u32[]{:S(2)}) collective-permute-start(f32[256,1024]{1,0:T(8,128)S(1)} %get-tuple-element.28.chip), channel_id=1, source_target_pairs={{0,16},{1,17},{2,18},{3,19},{4,6},{5,7},{6,4},{7,5},{8,24},{9,25},... | collective-permute-start | bytes 3145736 | tf_op jit(solution)/shard_map/ppermute | solution.py:266
  12.8 3.0 %collective-permute-start.1 = (f32[256,1024]{1,0:T(8,128)S(1)}, f32[256,1024]{1,0:T(8,128)S(1)}, u32[]{:S(2)}, u32[]{:S(2)}) collective-permute-start(f32[256,1024]{1,0:T(8,128)S(1)} %get-tuple-element.28.chip), channel_id=1, source_target_pairs={{0,24},{1,25},{2,26},{3,27},{4,7},{5,4},{6,5},{7,6},{8,0},{9,1},{1... | collective-permute-start | bytes 3145736 | tf_op jit(solution)/shard_map/ppermute | solution.py:266
  15.8 2.7 %collective-permute-start.3 = (f32[8,1024]{1,0:T(8,128)S(1)}, f32[8,1024]{1,0:T(8,128)S(1)}, u32[]{:S(2)}, u32[]{:S(2)}) collective-permute-start(f32[8,1024]{1,0:T(8,128)S(1)} %get-tuple-element.29.a), channel_id=1, source_target_pairs={{0,1},{1,0},{2,3},{3,2},{4,12},{5,13},{6,14},{7,15},{8,9},{9,8},{1... | collective-permute-start | bytes 98312 | tf_op jit(solution)/shard_map/ppermute | solution.py:275
  18.5 2.9 %collective-permute-start.14 = (f32[280,1024]{1,0:T(8,128)S(1)}, f32[280,1024]{1,0:T(8,128)S(1)}, u32[]{:S(2)}, u32[]{:S(2)}) collective-permute-start(f32[280,1024]{1,0:T(8,128)S(1)} %get-tuple-element.36), channel_id=1, source_target_pairs={{0,8},{1,9},{2,10},{3,11},{4,5},{5,6},{6,7},{7,4},{8,16},{9,17},{1... | collective-permute-start | bytes 3440648 | tf_op jit(solution)/shard_map/ppermute | solution.py:266
  21.4 0.6 collective-permute-done.3.b
  22.0 4.6 %collective-permute-start.4 = (f32[8,1024]{1,0:T(8,128)S(1)}, f32[8,1024]{1,0:T(8,128)S(1)}, u32[]{:S(2)}, u32[]{:S(2)}) collective-permute-start(f32[8,1024]{1,0:T(8,128)S(1)} %shard_map.48.a), channel_id=1, source_target_pairs={{0,2},{1,3},{2,0},{3,1},{4,20},{5,21},{6,22},{7,23},{8,10},{9,11},... | collective-permute-start | bytes 98312 | tf_op jit(solution)/shard_map/ppermute | solution.py:275
  26.7 3.1 %collective-permute-done.4.b = f32[8,1024]{1,0:T(8,128)S(1)} collective-permute-done((f32[8,1024]{1,0:T(8,128)S(1)}, f32[8,1024]{1,0:T(8,128)S(1)}, u32[]{:S(2)}, u32[]{:S(2)}) %collective-permute-start.4) | collective-permute-done | bytes 32800 | tf_op jit(solution)/shard_map/ppermute | solution.py:275
  29.7 2.0 %collective-permute-start.6 = (f32[8,1024]{1,0:T(8,128)S(1)}, f32[8,1024]{1,0:T(8,128)S(1)}, u32[]{:S(2)}, u32[]{:S(2)}) collective-permute-start(f32[8,1024]{1,0:T(8,128)S(1)} %shard_map.49), channel_id=1, source_target_pairs={{0,4},{4,0},{8,12},{12,8},{16,20},{20,16},{24,28},{28,24},{1,5},{5... | collective-permute-start | bytes 98312 | tf_op jit(solution)/shard_map/ppermute | solution.py:257
  31.8 1.1 collective-permute-done.6.a
  32.8 2.1 %collective-permute-start.7 = (f32[256,1024]{1,0:T(8,128)S(1)}, f32[256,1024]{1,0:T(8,128)S(1)}, u32[]{:S(2)}, u32[]{:S(2)}) collective-permute-start(f32[256,1024]{1,0:T(8,128)S(1)} %collective-permute-done.2.refs_1_), channel_id=1, source_target_pairs={{0,4},{4,0},{8,12},{12,8},{16,20},{20,16},{24,28},{28,24},{1,5},{5... | collective-permute-start | bytes 3145736 | tf_op jit(solution)/shard_map/ppermute | solution.py:257
  34.9 3.3 %collective-permute-done.1.refs_0_ = f32[256,1024]{1,0:T(8,128)S(1)} collective-permute-done((f32[256,1024]{1,0:T(8,128)S(1)}, f32[256,1024]{1,0:T(8,128)S(1)}, u32[]{:S(2)}, u32[]{:S(2)}) %collective-permute-start.1) | collective-permute-done | bytes 1048608 | tf_op jit(solution)/shard_map/ppermute | solution.py:266
  38.2 1.9 %collective-permute-start.5 = (f32[256,1024]{1,0:T(8,128)S(1)}, f32[256,1024]{1,0:T(8,128)S(1)}, u32[]{:S(2)}, u32[]{:S(2)}) collective-permute-start(f32[256,1024]{1,0:T(8,128)S(1)} %collective-permute-done.1.refs_0_), channel_id=1, source_target_pairs={{0,4},{4,0},{8,12},{12,8},{16,20},{20,16},{24,28},{28,24},{1,5},{5... | collective-permute-start | bytes 3145736 | tf_op jit(solution)/shard_map/ppermute | solution.py:257
  40.1 2.7 %collective-permute-start.12 = (f32[8,1024]{1,0:T(8,128)S(1)}, f32[8,1024]{1,0:T(8,128)S(1)}, u32[]{:S(2)}, u32[]{:S(2)}) collective-permute-start(f32[8,1024]{1,0:T(8,128)S(1)} %collective-permute-done.6.a), channel_id=1, source_target_pairs={{0,1},{1,0},{2,3},{3,2},{4,12},{5,13},{6,14},{7,15},{8,9},{9,8},{1... | collective-permute-start | bytes 98312 | tf_op jit(solution)/shard_map/ppermute | solution.py:275
  42.9 3.1 %collective-permute-done.12.b = f32[8,1024]{1,0:T(8,128)S(1)} collective-permute-done((f32[8,1024]{1,0:T(8,128)S(1)}, f32[8,1024]{1,0:T(8,128)S(1)}, u32[]{:S(2)}, u32[]{:S(2)}) %collective-permute-start.12) | collective-permute-done | bytes 32800 | tf_op jit(solution)/shard_map/ppermute | solution.py:275
  46.0 3.3 %collective-permute-start.13 = (f32[8,1024]{1,0:T(8,128)S(1)}, f32[8,1024]{1,0:T(8,128)S(1)}, u32[]{:S(2)}, u32[]{:S(2)}) collective-permute-start(f32[8,1024]{1,0:T(8,128)S(1)} %shard_map.54.a), channel_id=1, source_target_pairs={{0,2},{1,3},{2,0},{3,1},{4,20},{5,21},{6,22},{7,23},{8,10},{9,11},... | collective-permute-start | bytes 98312 | tf_op jit(solution)/shard_map/ppermute | solution.py:275
  49.3 2.9 %shard_map.50 = (f32[144,768]{1,0:T(8,128)S(1)}, f32[144,768]{1,0:T(8,128)S(1)}, f32[96,768]{1,0:T(8,128)S(1)}, bf16[384,1024]{1,0:T(8,128)(2,1)S(1)}, bf16[384,...) custom-call(f32[256,1024]{1,0:T(8,128)S(1)} %get-tuple-element.28.chip, ...), custom_call_target="tpu_custom_call" | custom-call | bytes 8388608 | tf_op jit(solution)/shard_map/pallas_call | solution.py:28
  52.2 1.1 collective-permute-done.13.b
  53.3 0.1 shard_map.55
  53.3 1.9 %collective-permute-start.15 = (f32[264,1024]{1,0:T(8,128)S(1)}, f32[264,1024]{1,0:T(8,128)S(1)}, u32[]{:S(2)}, u32[]{:S(2)}) collective-permute-start(f32[264,1024]{1,0:T(8,128)S(1)} %get-tuple-element.38.sent), channel_id=1, source_target_pairs={{0,4},{4,0},{8,12},{12,8},{16,20},{20,16},{24,28},{28,24},{1,5},{5... | collective-permute-start | bytes 3244040 | tf_op jit(solution)/shard_map/ppermute | solution.py:257
  55.3 3.8 %collective-permute-start.8 = (f32[144,768]{1,0:T(8,128)S(1)}, f32[144,768]{1,0:T(8,128)S(1)}, u32[]{:S(2)}, u32[]{:S(2)}) collective-permute-start(f32[144,768]{1,0:T(8,128)S(1)} %get-tuple-element.33.u0a), channel_id=1, source_target_pairs={{0,32},{4,484},{8,40},{12,492},{16,48},{20,500},{24,56},{28,508},{... | collective-permute-start | bytes 1327112 | tf_op jit(solution)/shard_map/ppermute | solution.py:288
  59.1 3.2 %shard_map.56 = (f32[176,512]{1,0:T(8,128)S(1)}, f32[176,512]{1,0:T(8,128)S(1)}, f32[112,512]{1,0:T(8,128)S(1)}) custom-call(f32[264,1024]{1,0:T(8,128)S(1)} %get-tuple-element.38.sent, f32[264,1024]{1,0:T(8,128)S(1)} %collective-permute-done.15.swap, f32[1,1024]{1,0:T(1,128)S(1)} %get-tuple-element.32.refs_4_.weights, ...), custom_call_target="tpu_custom_call" | custom-call | tf_op jit(solution)/shard_map/pallas_call | solution.py:28
  62.3 3.8 %collective-permute-start.16 = (f32[176,512]{1,0:T(8,128)S(1)}, f32[176,512]{1,0:T(8,128)S(1)}, u32[]{:S(2)}, u32[]{:S(2)}) collective-permute-start(f32[176,512]{1,0:T(8,128)S(1)} %get-tuple-element.44.u0b), channel_id=1, source_target_pairs={{0,32},{4,484},{8,40},{12,492},{16,48},{20,500},{24,56},{28,508},{... | collective-permute-start | bytes 1081352 | tf_op jit(solution)/shard_map/ppermute | solution.py:288
  66.1 6.8 %collective-permute-done.8.r = f32[144,768]{1,0:T(8,128)S(1)} collective-permute-done((f32[144,768]{1,0:T(8,128)S(1)}, f32[144,768]{1,0:T(8,128)S(1)}, u32[]{:S(2)}, u32[]{:S(2)}) %collective-permute-start.8) | collective-permute-done | bytes 442400 | tf_op jit(solution)/shard_map/ppermute | solution.py:288
  73.0 1.9 %collective-permute-start.9 = (f32[144,768]{1,0:T(8,128)S(1)}, f32[144,768]{1,0:T(8,128)S(1)}, u32[]{:S(2)}, u32[]{:S(2)}) collective-permute-start(f32[144,768]{1,0:T(8,128)S(1)} %shard_map.51), channel_id=1, source_target_pairs={{0,32},{4,484},{8,40},{12,492},{16,48},{20,500},{24,56},{28,508},{... | collective-permute-start | bytes 1327112 | tf_op jit(solution)/shard_map/ppermute | solution.py:288
  74.9 3.0 %collective-permute-done.16.r = f32[176,512]{1,0:T(8,128)S(1)} collective-permute-done((f32[176,512]{1,0:T(8,128)S(1)}, f32[176,512]{1,0:T(8,128)S(1)}, u32[]{:S(2)}, u32[]{:S(2)}) %collective-permute-start.16) | collective-permute-done | bytes 360480 | tf_op jit(solution)/shard_map/ppermute | solution.py:288
  77.9 1.9 %collective-permute-start.17 = (f32[176,512]{1,0:T(8,128)S(1)}, f32[176,512]{1,0:T(8,128)S(1)}, u32[]{:S(2)}, u32[]{:S(2)}) collective-permute-start(f32[176,512]{1,0:T(8,128)S(1)} %shard_map.57.refs_1_), channel_id=1, source_target_pairs={{0,32},{4,484},{8,40},{12,492},{16,48},{20,500},{24,56},{28,508},{... | collective-permute-start | bytes 1081352 | tf_op jit(solution)/shard_map/ppermute | solution.py:288
  79.9 4.5 %collective-permute-done.9.r2.r2a = f32[144,768]{1,0:T(8,128)S(1)} collective-permute-done((f32[144,768]{1,0:T(8,128)S(1)}, f32[144,768]{1,0:T(8,128)S(1)}, u32[]{:S(2)}, u32[]{:S(2)}) %collective-permute-start.9) | collective-permute-done | bytes 442400 | tf_op jit(solution)/shard_map/ppermute | solution.py:288
  84.4 1.9 %collective-permute-start.10 = (f32[48,768]{1,0:T(8,128)S(1)}, f32[48,768]{1,0:T(8,128)S(1)}, u32[]{:S(2)}, u32[]{:S(2)}) collective-permute-start(f32[48,768]{1,0:T(8,128)S(1)} %shard_map.52), channel_id=1, source_target_pairs={{0,96},{4,420},{8,104},{12,428},{16,112},{20,436},{24,120},{28,444... | collective-permute-start | bytes 442376 | tf_op jit(solution)/shard_map/ppermute | solution.py:288
  86.4 2.1 %collective-permute-done.17.r2.r2b = f32[176,512]{1,0:T(8,128)S(1)} collective-permute-done((f32[176,512]{1,0:T(8,128)S(1)}, f32[176,512]{1,0:T(8,128)S(1)}, u32[]{:S(2)}, u32[]{:S(2)}) %collective-permute-start.17) | collective-permute-done | bytes 360480 | tf_op jit(solution)/shard_map/ppermute | solution.py:288
  88.5 3.5 %collective-permute-start.18 = (f32[64,512]{1,0:T(8,128)S(1)}, f32[64,512]{1,0:T(8,128)S(1)}, u32[]{:S(2)}, u32[]{:S(2)}) collective-permute-start(f32[64,512]{1,0:T(8,128)S(1)} %shard_map.58), channel_id=1, source_target_pairs={{0,96},{4,420},{8,104},{12,428},{16,112},{20,436},{24,120},{28,444... | collective-permute-start | bytes 393224 | tf_op jit(solution)/shard_map/ppermute | solution.py:288
  92.0 5.2 %collective-permute-done.10.r3 = f32[48,768]{1,0:T(8,128)S(1)} collective-permute-done((f32[48,768]{1,0:T(8,128)S(1)}, f32[48,768]{1,0:T(8,128)S(1)}, u32[]{:S(2)}, u32[]{:S(2)}) %collective-permute-start.10) | collective-permute-done | bytes 147488 | tf_op jit(solution)/shard_map/ppermute | solution.py:288
  97.2 1.9 %collective-permute-start.11 = (f32[48,768]{1,0:T(8,128)S(1)}, f32[48,768]{1,0:T(8,128)S(1)}, u32[]{:S(2)}, u32[]{:S(2)}) collective-permute-start(f32[48,768]{1,0:T(8,128)S(1)} %shard_map.53), channel_id=1, source_target_pairs={{0,96},{4,420},{8,104},{12,428},{16,112},{20,436},{24,120},{28,444... | collective-permute-start | bytes 442376 | tf_op jit(solution)/shard_map/ppermute | solution.py:288
  99.1 2.4 %collective-permute-done.18.r3.r3b = f32[64,512]{1,0:T(8,128)S(1)} collective-permute-done((f32[64,512]{1,0:T(8,128)S(1)}, f32[64,512]{1,0:T(8,128)S(1)}, u32[]{:S(2)}, u32[]{:S(2)}) %collective-permute-start.18) | collective-permute-done | bytes 131104 | tf_op jit(solution)/shard_map/ppermute | solution.py:288
  101.6 2.9 %collective-permute-start.19 = (f32[64,512]{1,0:T(8,128)S(1)}, f32[64,512]{1,0:T(8,128)S(1)}, u32[]{:S(2)}, u32[]{:S(2)}) collective-permute-start(f32[64,512]{1,0:T(8,128)S(1)} %shard_map.59), channel_id=1, source_target_pairs={{0,96},{4,420},{8,104},{12,428},{16,112},{20,436},{24,120},{28,444... | collective-permute-start | bytes 393224 | tf_op jit(solution)/shard_map/ppermute | solution.py:288
  104.4 2.9 %collective-permute-done.11.r4a = f32[48,768]{1,0:T(8,128)S(1)} collective-permute-done((f32[48,768]{1,0:T(8,128)S(1)}, f32[48,768]{1,0:T(8,128)S(1)}, u32[]{:S(2)}, u32[]{:S(2)}) %collective-permute-start.11) | collective-permute-done | bytes 147488 | tf_op jit(solution)/shard_map/ppermute | solution.py:288
  107.3 6.4 %collective-permute-done.19.r4b = f32[64,512]{1,0:T(8,128)S(1)} collective-permute-done((f32[64,512]{1,0:T(8,128)S(1)}, f32[64,512]{1,0:T(8,128)S(1)}, u32[]{:S(2)}, u32[]{:S(2)}) %collective-permute-start.19) | collective-permute-done | bytes 131104 | tf_op jit(solution)/shard_map/ppermute | solution.py:288
  113.7 0.1 shard_map.60
  113.8 1.9 %collective-permute-start.20 = (f32[40,1024]{1,0:T(8,128)S(1)}, f32[40,1024]{1,0:T(8,128)S(1)}, u32[]{:S(2)}, u32[]{:S(2)}) collective-permute-start(f32[40,1024]{1,0:T(8,128)S(1)} %get-tuple-element.48), channel_id=1, source_target_pairs={{0,4},{4,0},{8,12},{12,8},{16,20},{20,16},{24,28},{28,24},{1,5},{5... | collective-permute-start | bytes 491528 | tf_op jit(solution)/shard_map/ppermute | solution.py:257
  115.7 1.4 %collective-permute-done.20.here = f32[40,1024]{1,0:T(8,128)S(1)} collective-permute-done((f32[40,1024]{1,0:T(8,128)S(1)}, f32[40,1024]{1,0:T(8,128)S(1)}, u32[]{:S(2)}, u32[]{:S(2)}) %collective-permute-start.20) | collective-permute-done | bytes 163872 | tf_op jit(solution)/shard_map/ppermute | solution.py:257
  117.1 0.7 shard_map.61
  (18 shorter events, 0.2 us)
Async XLA Ops:
  0.0 1.0 copy-start
  1.0 0.7 copy-start.1
  1.7 0.7 copy-start.2
  2.4 0.7 copy-start.3
  3.8 3.8 %collective-permute-start = (f32[128,1024]{1,0:T(8,128)S(1)}, f32[128,1024]{1,0:T(8,128)S(1)}, u32[]{:S(2)}, u32[]{:S(2)}) collective-permute-start(f32[128,1024]{1,0:T(8,128)S(1)} %get-tuple-element.27.own), channel_id=1, source_target_pairs={{0,4},{4,0},{8,12},{12,8},{16,20},{20,16},{24,28},{28,24},{1,5},{5... | collective-permute-start | bytes 1572872 | tf_op jit(solution)/shard_map/ppermute | solution.py:257
  7.7 25.1 %collective-permute-start.2 = (f32[256,1024]{1,0:T(8,128)S(1)}, f32[256,1024]{1,0:T(8,128)S(1)}, u32[]{:S(2)}, u32[]{:S(2)}) collective-permute-start(f32[256,1024]{1,0:T(8,128)S(1)} %get-tuple-element.28.chip), channel_id=1, source_target_pairs={{0,16},{1,17},{2,18},{3,19},{4,6},{5,7},{6,4},{7,5},{8,24},{9,25},... | collective-permute-start | bytes 3145736 | tf_op jit(solution)/shard_map/ppermute | solution.py:266
  12.8 25.4 %collective-permute-start.1 = (f32[256,1024]{1,0:T(8,128)S(1)}, f32[256,1024]{1,0:T(8,128)S(1)}, u32[]{:S(2)}, u32[]{:S(2)}) collective-permute-start(f32[256,1024]{1,0:T(8,128)S(1)} %get-tuple-element.28.chip), channel_id=1, source_target_pairs={{0,24},{1,25},{2,26},{3,27},{4,7},{5,4},{6,5},{7,6},{8,0},{9,1},{1... | collective-permute-start | bytes 3145736 | tf_op jit(solution)/shard_map/ppermute | solution.py:266
  15.8 6.2 %collective-permute-start.3 = (f32[8,1024]{1,0:T(8,128)S(1)}, f32[8,1024]{1,0:T(8,128)S(1)}, u32[]{:S(2)}, u32[]{:S(2)}) collective-permute-start(f32[8,1024]{1,0:T(8,128)S(1)} %get-tuple-element.29.a), channel_id=1, source_target_pairs={{0,1},{1,0},{2,3},{3,2},{4,12},{5,13},{6,14},{7,15},{8,9},{9,8},{1... | collective-permute-start | bytes 98312 | tf_op jit(solution)/shard_map/ppermute | solution.py:275
  18.5 33.6 %collective-permute-start.14 = (f32[280,1024]{1,0:T(8,128)S(1)}, f32[280,1024]{1,0:T(8,128)S(1)}, u32[]{:S(2)}, u32[]{:S(2)}) collective-permute-start(f32[280,1024]{1,0:T(8,128)S(1)} %get-tuple-element.36), channel_id=1, source_target_pairs={{0,8},{1,9},{2,10},{3,11},{4,5},{5,6},{6,7},{7,4},{8,16},{9,17},{1... | collective-permute-start | bytes 3440648 | tf_op jit(solution)/shard_map/ppermute | solution.py:266
  22.0 7.7 %collective-permute-start.4 = (f32[8,1024]{1,0:T(8,128)S(1)}, f32[8,1024]{1,0:T(8,128)S(1)}, u32[]{:S(2)}, u32[]{:S(2)}) collective-permute-start(f32[8,1024]{1,0:T(8,128)S(1)} %shard_map.48.a), channel_id=1, source_target_pairs={{0,2},{1,3},{2,0},{3,1},{4,20},{5,21},{6,22},{7,23},{8,10},{9,11},... | collective-permute-start | bytes 98312 | tf_op jit(solution)/shard_map/ppermute | solution.py:275
  29.7 3.1 %collective-permute-start.6 = (f32[8,1024]{1,0:T(8,128)S(1)}, f32[8,1024]{1,0:T(8,128)S(1)}, u32[]{:S(2)}, u32[]{:S(2)}) collective-permute-start(f32[8,1024]{1,0:T(8,128)S(1)} %shard_map.49), channel_id=1, source_target_pairs={{0,4},{4,0},{8,12},{12,8},{16,20},{20,16},{24,28},{28,24},{1,5},{5... | collective-permute-start | bytes 98312 | tf_op jit(solution)/shard_map/ppermute | solution.py:257
  32.8 16.4 %collective-permute-start.7 = (f32[256,1024]{1,0:T(8,128)S(1)}, f32[256,1024]{1,0:T(8,128)S(1)}, u32[]{:S(2)}, u32[]{:S(2)}) collective-permute-start(f32[256,1024]{1,0:T(8,128)S(1)} %collective-permute-done.2.refs_1_), channel_id=1, source_target_pairs={{0,4},{4,0},{8,12},{12,8},{16,20},{20,16},{24,28},{28,24},{1,5},{5... | collective-permute-start | bytes 3145736 | tf_op jit(solution)/shard_map/ppermute | solution.py:257
  38.2 11.1 %collective-permute-start.5 = (f32[256,1024]{1,0:T(8,128)S(1)}, f32[256,1024]{1,0:T(8,128)S(1)}, u32[]{:S(2)}, u32[]{:S(2)}) collective-permute-start(f32[256,1024]{1,0:T(8,128)S(1)} %collective-permute-done.1.refs_0_), channel_id=1, source_target_pairs={{0,4},{4,0},{8,12},{12,8},{16,20},{20,16},{24,28},{28,24},{1,5},{5... | collective-permute-start | bytes 3145736 | tf_op jit(solution)/shard_map/ppermute | solution.py:257
  40.1 5.8 %collective-permute-start.12 = (f32[8,1024]{1,0:T(8,128)S(1)}, f32[8,1024]{1,0:T(8,128)S(1)}, u32[]{:S(2)}, u32[]{:S(2)}) collective-permute-start(f32[8,1024]{1,0:T(8,128)S(1)} %collective-permute-done.6.a), channel_id=1, source_target_pairs={{0,1},{1,0},{2,3},{3,2},{4,12},{5,13},{6,14},{7,15},{8,9},{9,8},{1... | collective-permute-start | bytes 98312 | tf_op jit(solution)/shard_map/ppermute | solution.py:275
  46.0 7.3 %collective-permute-start.13 = (f32[8,1024]{1,0:T(8,128)S(1)}, f32[8,1024]{1,0:T(8,128)S(1)}, u32[]{:S(2)}, u32[]{:S(2)}) collective-permute-start(f32[8,1024]{1,0:T(8,128)S(1)} %shard_map.54.a), channel_id=1, source_target_pairs={{0,2},{1,3},{2,0},{3,1},{4,20},{5,21},{6,22},{7,23},{8,10},{9,11},... | collective-permute-start | bytes 98312 | tf_op jit(solution)/shard_map/ppermute | solution.py:275
  53.3 5.8 %collective-permute-start.15 = (f32[264,1024]{1,0:T(8,128)S(1)}, f32[264,1024]{1,0:T(8,128)S(1)}, u32[]{:S(2)}, u32[]{:S(2)}) collective-permute-start(f32[264,1024]{1,0:T(8,128)S(1)} %get-tuple-element.38.sent), channel_id=1, source_target_pairs={{0,4},{4,0},{8,12},{12,8},{16,20},{20,16},{24,28},{28,24},{1,5},{5... | collective-permute-start | bytes 3244040 | tf_op jit(solution)/shard_map/ppermute | solution.py:257
  55.3 17.7 %collective-permute-start.8 = (f32[144,768]{1,0:T(8,128)S(1)}, f32[144,768]{1,0:T(8,128)S(1)}, u32[]{:S(2)}, u32[]{:S(2)}) collective-permute-start(f32[144,768]{1,0:T(8,128)S(1)} %get-tuple-element.33.u0a), channel_id=1, source_target_pairs={{0,32},{4,484},{8,40},{12,492},{16,48},{20,500},{24,56},{28,508},{... | collective-permute-start | bytes 1327112 | tf_op jit(solution)/shard_map/ppermute | solution.py:288
  62.3 15.6 %collective-permute-start.16 = (f32[176,512]{1,0:T(8,128)S(1)}, f32[176,512]{1,0:T(8,128)S(1)}, u32[]{:S(2)}, u32[]{:S(2)}) collective-permute-start(f32[176,512]{1,0:T(8,128)S(1)} %get-tuple-element.44.u0b), channel_id=1, source_target_pairs={{0,32},{4,484},{8,40},{12,492},{16,48},{20,500},{24,56},{28,508},{... | collective-permute-start | bytes 1081352 | tf_op jit(solution)/shard_map/ppermute | solution.py:288
  73.0 11.4 %collective-permute-start.9 = (f32[144,768]{1,0:T(8,128)S(1)}, f32[144,768]{1,0:T(8,128)S(1)}, u32[]{:S(2)}, u32[]{:S(2)}) collective-permute-start(f32[144,768]{1,0:T(8,128)S(1)} %shard_map.51), channel_id=1, source_target_pairs={{0,32},{4,484},{8,40},{12,492},{16,48},{20,500},{24,56},{28,508},{... | collective-permute-start | bytes 1327112 | tf_op jit(solution)/shard_map/ppermute | solution.py:288
  77.9 10.5 %collective-permute-start.17 = (f32[176,512]{1,0:T(8,128)S(1)}, f32[176,512]{1,0:T(8,128)S(1)}, u32[]{:S(2)}, u32[]{:S(2)}) collective-permute-start(f32[176,512]{1,0:T(8,128)S(1)} %shard_map.57.refs_1_), channel_id=1, source_target_pairs={{0,32},{4,484},{8,40},{12,492},{16,48},{20,500},{24,56},{28,508},{... | collective-permute-start | bytes 1081352 | tf_op jit(solution)/shard_map/ppermute | solution.py:288
  84.4 12.8 %collective-permute-start.10 = (f32[48,768]{1,0:T(8,128)S(1)}, f32[48,768]{1,0:T(8,128)S(1)}, u32[]{:S(2)}, u32[]{:S(2)}) collective-permute-start(f32[48,768]{1,0:T(8,128)S(1)} %shard_map.52), channel_id=1, source_target_pairs={{0,96},{4,420},{8,104},{12,428},{16,112},{20,436},{24,120},{28,444... | collective-permute-start | bytes 442376 | tf_op jit(solution)/shard_map/ppermute | solution.py:288
  88.5 13.0 %collective-permute-start.18 = (f32[64,512]{1,0:T(8,128)S(1)}, f32[64,512]{1,0:T(8,128)S(1)}, u32[]{:S(2)}, u32[]{:S(2)}) collective-permute-start(f32[64,512]{1,0:T(8,128)S(1)} %shard_map.58), channel_id=1, source_target_pairs={{0,96},{4,420},{8,104},{12,428},{16,112},{20,436},{24,120},{28,444... | collective-permute-start | bytes 393224 | tf_op jit(solution)/shard_map/ppermute | solution.py:288
  97.2 10.1 %collective-permute-start.11 = (f32[48,768]{1,0:T(8,128)S(1)}, f32[48,768]{1,0:T(8,128)S(1)}, u32[]{:S(2)}, u32[]{:S(2)}) collective-permute-start(f32[48,768]{1,0:T(8,128)S(1)} %shard_map.53), channel_id=1, source_target_pairs={{0,96},{4,420},{8,104},{12,428},{16,112},{20,436},{24,120},{28,444... | collective-permute-start | bytes 442376 | tf_op jit(solution)/shard_map/ppermute | solution.py:288
  101.6 12.1 %collective-permute-start.19 = (f32[64,512]{1,0:T(8,128)S(1)}, f32[64,512]{1,0:T(8,128)S(1)}, u32[]{:S(2)}, u32[]{:S(2)}) collective-permute-start(f32[64,512]{1,0:T(8,128)S(1)} %shard_map.59), channel_id=1, source_target_pairs={{0,96},{4,420},{8,104},{12,428},{16,112},{20,436},{24,120},{28,444... | collective-permute-start | bytes 393224 | tf_op jit(solution)/shard_map/ppermute | solution.py:288
  113.8 3.3 %collective-permute-start.20 = (f32[40,1024]{1,0:T(8,128)S(1)}, f32[40,1024]{1,0:T(8,128)S(1)}, u32[]{:S(2)}, u32[]{:S(2)}) collective-permute-start(f32[40,1024]{1,0:T(8,128)S(1)} %get-tuple-element.48), channel_id=1, source_target_pairs={{0,4},{4,0},{8,12},{12,8},{16,20},{20,16},{24,28},{28,24},{1,5},{5... | collective-permute-start | bytes 491528 | tf_op jit(solution)/shard_map/ppermute | solution.py:257

commit v4 on v3

--- a/solution.py
+++ b/solution.py
@@ -17,6 +17,7 @@
 LATE_ROWS, LATE_COLS = 2 * 2 * POS + 3 * POS, 2 * PAIR
 TOTALS = 8
 PART = N_COL * POS
+ORDER = (7, 3, 5, 1, 6, 2, 4, 0)
 PROT = N_ROW * N_COL * WIDTH
 VMEM = pl.BlockSpec(memory_space=pltpu.VMEM)
 HBM = pl.BlockSpec(memory_space=pltpu.HBM)
@@ -24,13 +25,13 @@
 BF16 = jnp.bfloat16
 
 
-def call(body, outs, operands, in_hbm=False, mib=4, flops=0, nbytes=1 << 19, scratch=()):
+def call(body, outs, operands, in_hbm=(), mib=4, flops=0, nbytes=1 << 19, scratch=()):
     return pl.pallas_call(
         body,
         out_shape=[
             jax.ShapeDtypeStruct(s[:-1], BF16) if s[-1] is BF16 else jax.ShapeDtypeStruct(s, F32) for s in outs
         ],
-        in_specs=[HBM if in_hbm else VMEM] * len(operands),
+        in_specs=[HBM if i in in_hbm else VMEM for i in range(len(operands))],
         out_specs=[VMEM] * len(outs),
         scratch_shapes=list(scratch),
         compiler_params=pltpu.CompilerParams(vmem_limit_bytes=mib << 20),
@@ -94,10 +95,8 @@
     z, core = lax.axis_index("dom"), core_of()
     w = weights[...]
     first, second = (WIDTH, 0) if swapped else (0, WIDTH)
-    for j in range(8):
-        ahead = z + 8 - j
-        behind = z if j == 0 else z + 8 + j
-        at = lax.rem(jnp.where(core == 0, ahead, behind), N_DOM) * POS
+    for j, far in enumerate(ORDER):
+        at = lax.rem(jnp.where(core == 0, z + far, z + N_DOM - 1 - far), N_DOM) * POS
         mine = source[pl.ds(pl.multiple_of(at + first, POS), POS), :]
         theirs = source[pl.ds(pl.multiple_of(at + second, POS), POS), :]
         to = pl.ds(start + j * 2 * POS, 2 * POS)
@@ -112,7 +111,7 @@
 
 def early_body(chip, *refs):
     sent, swap, weights = refs[:2], refs[2:4], refs[4]
-    outs, (ph, pl_, qh, ql) = refs[5:8], refs[8:]
+    outs, (ph, pl_, qh, ql) = refs[5:7], refs[7:]
     core = core_of()
     fill_rows(ph, pl_, weights, 0, chip, False)
     fill_columns(qh, ql, 0, chip, False)
@@ -133,11 +132,11 @@
     for i in range(3):
         for j in range(8):
             rows = i * WIDTH + j * 2 * POS
-            at = pl.ds((j // 3) * EARLY_ROWS + i * 2 * POS, 2 * POS)
-            outs[j % 3][at, :] = block[rows : rows + 2 * POS]
-
-
-def late_body(sent, swap, weights, ph, pl_, qh, ql, sums, first, second, third, fh, fl, gh, gl):
+            at = pl.ds((j % 4) * EARLY_ROWS + i * 2 * POS, 2 * POS)
+            outs[j // 4][at, :] = block[rows : rows + 2 * POS]
+
+
+def late_body(sent, swap, weights, ph, pl_, qh, ql, sums, first, second, fh, fl, gh, gl):
     core = core_of()
 
     @pl.when(core == 0)
@@ -157,7 +156,7 @@
     late_late = dot3(fh[...], fl[...], gh[...], gl[...])
     early_late = dot3(ph[...], pl_[...], gh[...], gl[...])
     for j in range(8):
-        out, start = (first, second, third)[j % 3], (j // 3) * LATE_ROWS
+        out, start = (first, second)[j // 4], (j % 4) * LATE_ROWS
         rows = slice(j * 2 * POS, (j + 1) * 2 * POS)
         out[pl.ds(start, 2 * POS), :] = late_early[rows, : 2 * PAIR]
         at = pl.ds(start + 2 * POS, 2 * POS)
@@ -172,45 +171,26 @@
     tail = jnp.concatenate([late_early[WIDTH : WIDTH + 8, 2 * PAIR :], late_late[WIDTH : WIDTH + 8]], axis=1)
     odd = lax.broadcasted_iota(jnp.int32, (TOTALS, LATE_COLS), 0) % 2 == 1
     share = jnp.where(odd, tail, head)
-    first[pl.ds(3 * LATE_ROWS, TOTALS), :] = share
-    second[pl.ds(3 * LATE_ROWS, TOTALS), :] = share
-
-
-def second_body(u, r, out, unit):
-    far = (core_of() == 0).astype(F32)
-    head, tail = pl.ds(0, unit), pl.ds(unit, u.shape[0] - unit)
-    out[head, :] = u[head, :] + r[head, :] * far
-    out[tail, :] = u[tail, :] + r[tail, :]
-
-
-def third_body(u2, r2, *refs, unit):
-    out = refs[-1]
-    out[pl.ds(0, unit), :] = u2[pl.ds(0, unit), :] + r2[pl.ds(0, unit), :]
-    if len(refs) == 3:
-        u1, s2 = refs[:2]
-        at = pl.ds(3 * unit, TOTALS)
-        wide = u1[at, :] + r2[at, :]
-        narrow = (lax.broadcasted_iota(jnp.int32, wide.shape, 0) >= 2) & (core_of() == 1)
-        out[pl.ds(unit, TOTALS), :] = jnp.where(narrow, s2[at, :], wide)
-
-
-def fourth_body(u2, r2, r3, out, unit):
-    at = pl.ds(unit, unit)
-    out[pl.ds(0, unit), :] = u2[at, :] + r2[at, :] + r3[pl.ds(0, unit), :]
-    if out.shape[0] > unit:
-        out[pl.ds(unit, TOTALS), :] = r3[pl.ds(unit, TOTALS), :]
-
-
-def give_body(u0a, r2a, r4a, u0b, r2b, r3b, r4b, give, keep):
-    late = (core_of() == 1).astype(F32)
-
+    first[pl.ds(4 * LATE_ROWS, TOTALS), :] = share
+    second[pl.ds(4 * LATE_ROWS, TOTALS), :] = share
+
+
+def step_body(mine, came, go, stay, half):
+    go[pl.ds(0, half), :] = mine[pl.ds(0, half), :] + came[pl.ds(0, half), :]
+    stay[pl.ds(0, half), :] = mine[pl.ds(half, half), :] + came[pl.ds(half, half), :]
+    if half < go.shape[0]:
+        at = pl.ds(2 * half, TOTALS)
+        both = mine[at, :] + came[at, :]
+        go[pl.ds(half, TOTALS), :] = both
+        stay[pl.ds(half, TOTALS), :] = both
+
+
+def give_body(mine_a, came_a, mine_b, came_b, give, keep):
     def early(start, to):
-        at, of = pl.ds(start, POS), pl.ds(2 * EARLY_ROWS + start, POS)
-        return r2a[of, to] + u0a[at, to] * late + r4a[at, to]
+        return mine_a[pl.ds(start, POS), to] + came_a[pl.ds(start, POS), to]
 
     def other(start, to):
-        at, of = pl.ds(start, POS), pl.ds(2 * LATE_ROWS + start, POS)
-        return r2b[of, to] + u0b[at, to] * late + r4b[at, to]
+        return mine_b[pl.ds(start, POS), to] + came_b[pl.ds(start, POS), to]
 
     def pairs(k, count=1):
         return pl.ds(k * PAIR, count * PAIR)
@@ -223,10 +203,9 @@
         at = pl.ds(3 * POS, POS)
         out[at, pairs(0, 2)] = other(g * POS, pairs(0, 2))
         out[at, pairs(2, 2)] = other(2 * POS + g * POS, pairs(0, 2))
-    at = pl.ds(3 * LATE_ROWS, TOTALS)
-    sums = r2b[at, :] + u0b[at, :] * late
     for k in range(2):
-        total = sums[k : k + 1] + r3b[pl.ds(LATE_ROWS + k, 1), :] + r4b[pl.ds(LATE_ROWS + 2 + k, 1), :]
+        at = pl.ds(LATE_ROWS + k, 1)
+        total = mine_b[at, :] + came_b[at, :]
         for out in (keep, give):
             out[pl.ds(PART, 1), pairs(2 * k, 2)] = total
 
@@ -288,6 +267,15 @@
     return lax.ppermute(a, ("dom", "row"), pairs)
 
 
+def settled(a, cross):
+    pairs = []
+    for z in range(N_DOM):
+        for r in range(N_ROW):
+            to = z if r % 2 == 0 else (z - 1) % N_DOM
+            pairs.append((z * N_ROW + r, to * N_ROW + (r ^ cross)))
+    return lax.ppermute(a, ("dom", "row"), pairs)
+
+
 def per_device(protein_panel, tile_mask, domain_class, class_weight):
     tiles, classes = PANEL // TILE, class_weight.shape[0]
     own, sums, weights = call(
@@ -299,7 +287,7 @@
             domain_class.reshape(1, PANEL),
             class_weight.reshape(1, classes),
         ],
-        in_hbm=True, mib=4,
+        in_hbm=range(4),
         scratch=[
             pltpu.VMEM((WIDTH, PANEL), F32),
             pltpu.SMEM((1, tiles), jnp.int32),
@@ -315,45 +303,40 @@
     def both(a, bit):
         return call(add_body, [(8, PANEL)], [a, doubled(a, bit)])[0]
 
-    sums = both(both(sums, 1), 2)
-    swap_next = across(after(from_next, sums))
-    sums = across(sums)
+    sums = across(both(both(sums, 1), 2))
     swap_far = across(after(from_far, sums))
     sums = both(sums, 1)
+    swap_next = across(after(from_next, sums))
     early, columns = (3 * WIDTH, PANEL, BF16), (EARLY_COLS, PANEL, BF16)
-    a0, a1, a2, ph, pl_, qh, ql = call(
+    a0, a1, ph, pl_, qh, ql = call(
         early_body,
-        [(k * EARLY_ROWS, EARLY_COLS) for k in (3, 3, 2)] + [early, early, columns, columns],
+        [(4 * EARLY_ROWS, EARLY_COLS)] * 2 + [early, early, columns, columns],
         [chip, from_next, from_far, swap_next, swap_far, weights],
         mib=16, nbytes=8 << 20,
     )
-    ar1 = along_z(a0, 1)
+    came_a = along_z(a0, 1)
     from_last, sums = call(put_body, [(2 * WIDTH + 8, PANEL), (8, PANEL)], [sums, doubled(sums, 2), after(from_last, a0)])
     swap_last = across(from_last)
-    b0, b1, b2 = call(
+    b0, b1 = call(
         late_body,
-        [(3 * LATE_ROWS + TOTALS, LATE_COLS), (3 * LATE_ROWS + TOTALS, LATE_COLS), (2 * LATE_ROWS, LATE_COLS)],
+        [(4 * LATE_ROWS + TOTALS, LATE_COLS)] * 2,
         [from_last, swap_last, weights, ph, pl_, qh, ql, sums],
         mib=16, nbytes=0,
         scratch=[pltpu.VMEM((WIDTH + 16, PANEL), BF16)] * 2 + [pltpu.VMEM((PAIR, PANEL), BF16)] * 2,
     )
-    br1 = along_z(b0, 1)
-    of_a, of_b = {"unit": EARLY_ROWS}, {"unit": LATE_ROWS}
-    with_unit = functools.partial
-    (as2,) = call(with_unit(second_body, **of_a), [a1.shape], [a1, ar1])
-    ar2 = along_z(as2, 1)
-    (bs2,) = call(with_unit(second_body, **of_b), [b1.shape], [b1, br1])
-    br2 = along_z(bs2, 1)
-    (as3,) = call(with_unit(third_body, **of_a), [(EARLY_ROWS, EARLY_COLS)], [a2, ar2])
-    ar3 = along_z(as3, 3)
-    (bs3,) = call(with_unit(third_body, **of_b), [(LATE_ROWS + TOTALS, LATE_COLS)], [b2, br2, b1, bs2])
-    br3 = along_z(bs3, 3)
-    (as4,) = call(with_unit(fourth_body, **of_a), [(EARLY_ROWS, EARLY_COLS)], [a2, ar2, ar3])
-    ar4 = along_z(as4, 3)
-    (bs4,) = call(with_unit(fourth_body, **of_b), [(LATE_ROWS + TOTALS, LATE_COLS)], [b2, br2, br3])
-    br4 = along_z(bs4, 3)
-    give, keep = call(give_body, [(PART + TOTALS, 4 * PAIR)] * 2, [a0, ar2, ar4, b0, br2, br3, br4])
-    (flow,) = call(finish_body, [(N_COL * POS * N_ROW, WIDTH)], [keep, across(give)])
+    came_b = along_z(b0, 1)
+
+    def step(mine, came, rows, totals, shift):
+        shape = (rows + totals, mine.shape[1])
+        go, stay = call(functools.partial(step_body, half=rows), [shape] * 2, [mine, came])
+        return stay, along_z(go, shift)
+
+    a1, came_a = step(a1, came_a, 2 * EARLY_ROWS, 0, 2)
+    b1, came_b = step(b1, came_b, 2 * LATE_ROWS, TOTALS, 2)
+    a1, came_a = step(a1, came_a, EARLY_ROWS, 0, 4)
+    b1, came_b = step(b1, came_b, LATE_ROWS, TOTALS, 4)
+    give, keep = call(give_body, [(PART + TOTALS, 4 * PAIR)] * 2, [a1, came_a, b1, came_b])
+    (flow,) = call(finish_body, [(N_COL * POS * N_ROW, WIDTH)], [settled(keep, 0), settled(give, 1)])
     return flow.reshape(1, N_COL, POS, N_ROW, 1, WIDTH)
 
 

time: 120 us -> 113 us (0.942); the launches traced: 118 us -> 113 us
  starting transfers between devices: 57.8 us -> 54.7 us
  waiting for transfers between devices: 48.8 us -> 46.8 us
    ppermute x0 -> x2, waiting for transfers between devices: none -> 4.44 us  [settled(): return lax.ppermute(a, ('dom', 'row'), pairs)]
    ppermute x8 -> x6, waiting for transfers between devices: 33.3 us -> 29.7 us  [along_z(): return lax.ppermute(a, ('dom', 'row'), pairs)]
    ppermute x8 -> x6, starting transfers between devices: 21.7 us -> 18.2 us  [along_z(): return lax.ppermute(a, ('dom', 'row'), pairs)]
    ppermute x3, waiting for transfers between devices: 3.33 us -> 0.01 us  [around(): return lax.ppermute(a, ('row', 'col'), pairs)]
    ppermute x0 -> x2, starting transfers between devices: none -> 2.85 us  [settled(): return lax.ppermute(a, ('dom', 'row'), pairs)]
    ppermute x4, starting transfers between devices: 13.4 us -> 10.7 us  [doubled(): return lax.ppermute(a, ('row', 'col'), pairs)]
    ppermute x4, waiting for transfers between devices: 7.79 us -> 9.91 us  [doubled(): return lax.ppermute(a, ('row', 'col'), pairs)]
    ppermute x6 -> x5, waiting for transfers between devices: 4.31 us -> 2.72 us  [across(): return lax.ppermute(a, 'row', [(i, i ^ 1) for i in range(N_ROW)])]
  transfers between devices with their start and end apart: 21 -> 20, of which waited for: 16 -> 13; matrix products, arithmetic and copies ran while one was open for 0% -> 0% of each run, Pallas kernels for 5% -> 6%
where the time goes in v4:
time: 113 us
  starting transfers between devices  54.7 us (48%)
  waiting for transfers between devices  46.8 us (41%)
  Pallas kernels  7.9 us (7%)
  local copies, waits for them, and re-layouts  3.04 us (3%)
    ppermute x6, waiting for transfers between devices, along_z(): return lax.ppermute(a, ('dom', 'row'), pairs)  29.7 us
    ppermute x6, starting transfers between devices, along_z(): return lax.ppermute(a, ('dom', 'row'), pairs)  18.2 us
    ppermute x5, starting transfers between devices, across(): return lax.ppermute(a, 'row', [(i, i ^ 1) for i in range(N_ROW)])  11.6 us
    ppermute x3, starting transfers between devices, around(): return lax.ppermute(a, ('row', 'col'), pairs)  11.4 us
    ppermute x4, starting transfers between devices, doubled(): return lax.ppermute(a, ('row', 'col'), pairs)  10.7 us
    ppermute x4, waiting for transfers between devices, doubled(): return lax.ppermute(a, ('row', 'col'), pairs)  9.91 us
    pallas_call x14, Pallas kernels, call(): pl.pallas_call(body, out_shape=[jax.ShapeDtypeStruct(s[:-1], BF16) if s[-...  7.9 us
    ppermute x2, waiting for transfers between devices, settled(): return lax.ppermute(a, ('dom', 'row'), pairs)  4.44 us
  transfers between devices with their start and end apart: 20, of which 13 were waited for; matrix products, arithmetic and copies ran while one was open for 0% of the time, Pallas kernels for 6%

profile of v4, /device:TPU:6, one launch (start us, length us, event | category | flops | bytes accessed | tf_op | source)
XLA Modules:
  0.0 112.8 jit_solution(7636632995019006017)
XLA Ops:
  0.0 1.0 copy-done
  1.0 0.7 copy-done.1
  1.7 0.7 copy-done.2
  2.4 0.7 copy-done.3
  3.0 0.7 shard_map.46
  3.8 1.9 %collective-permute-start = (f32[128,1024]{1,0:T(8,128)S(1)}, f32[128,1024]{1,0:T(8,128)S(1)}, u32[]{:S(2)}, u32[]{:S(2)}) collective-permute-start(f32[128,1024]{1,0:T(8,128)S(1)} %get-tuple-element.33.own), channel_id=1, source_target_pairs={{0,4},{4,0},{8,12},{12,8},{16,20},{20,16},{24,28},{28,24},{1,5},{5... | collective-permute-start | bytes 1572872 | tf_op jit(solution)/shard_map/ppermute | solution.py:236
  5.7 1.9 %collective-permute-done.other = f32[128,1024]{1,0:T(8,128)S(1)} collective-permute-done((f32[128,1024]{1,0:T(8,128)S(1)}, f32[128,1024]{1,0:T(8,128)S(1)}, u32[]{:S(2)}, u32[]{:S(2)}) %collective-permute-start) | collective-permute-done | bytes 524320 | tf_op jit(solution)/shard_map/ppermute | solution.py:236
  7.6 0.1 shard_map.47
  7.7 4.9 %collective-permute-start.1 = (f32[256,1024]{1,0:T(8,128)S(1)}, f32[256,1024]{1,0:T(8,128)S(1)}, u32[]{:S(2)}, u32[]{:S(2)}) collective-permute-start(f32[256,1024]{1,0:T(8,128)S(1)} %get-tuple-element.34.chip), channel_id=1, source_target_pairs={{0,24},{1,25},{2,26},{3,27},{4,7},{5,4},{6,5},{7,6},{8,0},{9,1},{1... | collective-permute-start | bytes 3145736 | tf_op jit(solution)/shard_map/ppermute | solution.py:245
  12.6 2.5 %collective-permute-start.2 = (f32[256,1024]{1,0:T(8,128)S(1)}, f32[256,1024]{1,0:T(8,128)S(1)}, u32[]{:S(2)}, u32[]{:S(2)}) collective-permute-start(f32[256,1024]{1,0:T(8,128)S(1)} %get-tuple-element.34.chip), channel_id=1, source_target_pairs={{0,16},{1,17},{2,18},{3,19},{4,6},{5,7},{6,4},{7,5},{8,24},{9,25},... | collective-permute-start | bytes 3145736 | tf_op jit(solution)/shard_map/ppermute | solution.py:245
  15.2 2.7 %collective-permute-start.3 = (f32[8,1024]{1,0:T(8,128)S(1)}, f32[8,1024]{1,0:T(8,128)S(1)}, u32[]{:S(2)}, u32[]{:S(2)}) collective-permute-start(f32[8,1024]{1,0:T(8,128)S(1)} %get-tuple-element.35.a), channel_id=1, source_target_pairs={{0,1},{1,0},{2,3},{3,2},{4,12},{5,13},{6,14},{7,15},{8,9},{9,8},{1... | collective-permute-start | bytes 98312 | tf_op jit(solution)/shard_map/ppermute | solution.py:254
  17.9 3.5 %collective-permute-done.3.b = f32[8,1024]{1,0:T(8,128)S(1)} collective-permute-done((f32[8,1024]{1,0:T(8,128)S(1)}, f32[8,1024]{1,0:T(8,128)S(1)}, u32[]{:S(2)}, u32[]{:S(2)}) %collective-permute-start.3) | collective-permute-done | bytes 32800 | tf_op jit(solution)/shard_map/ppermute | solution.py:254
  21.4 3.6 %collective-permute-start.4 = (f32[8,1024]{1,0:T(8,128)S(1)}, f32[8,1024]{1,0:T(8,128)S(1)}, u32[]{:S(2)}, u32[]{:S(2)}) collective-permute-start(f32[8,1024]{1,0:T(8,128)S(1)} %shard_map.48.a), channel_id=1, source_target_pairs={{0,2},{1,3},{2,0},{3,1},{4,20},{5,21},{6,22},{7,23},{8,10},{9,11},... | collective-permute-start | bytes 98312 | tf_op jit(solution)/shard_map/ppermute | solution.py:254
  25.0 3.9 %collective-permute-start.13 = (f32[280,1024]{1,0:T(8,128)S(1)}, f32[280,1024]{1,0:T(8,128)S(1)}, u32[]{:S(2)}, u32[]{:S(2)}) collective-permute-start(f32[280,1024]{1,0:T(8,128)S(1)} %get-tuple-element.45), channel_id=1, source_target_pairs={{0,8},{1,9},{2,10},{3,11},{4,5},{5,6},{6,7},{7,4},{8,16},{9,17},{1... | collective-permute-start | bytes 3440648 | tf_op jit(solution)/shard_map/ppermute | solution.py:245
  28.9 0.2 collective-permute-done.4.b
  29.1 3.4 %collective-permute-start.5 = (f32[8,1024]{1,0:T(8,128)S(1)}, f32[8,1024]{1,0:T(8,128)S(1)}, u32[]{:S(2)}, u32[]{:S(2)}) collective-permute-start(f32[8,1024]{1,0:T(8,128)S(1)} %shard_map.49), channel_id=1, source_target_pairs={{0,4},{4,0},{8,12},{12,8},{16,20},{20,16},{24,28},{28,24},{1,5},{5... | collective-permute-start | bytes 98312 | tf_op jit(solution)/shard_map/ppermute | solution.py:236
  32.6 0.8 collective-permute-done.5.a
  33.4 1.9 %collective-permute-start.6 = (f32[8,1024]{1,0:T(8,128)S(1)}, f32[8,1024]{1,0:T(8,128)S(1)}, u32[]{:S(2)}, u32[]{:S(2)}) collective-permute-start(f32[8,1024]{1,0:T(8,128)S(1)} %collective-permute-done.5.a), channel_id=1, source_target_pairs={{0,1},{1,0},{2,3},{3,2},{4,12},{5,13},{6,14},{7,15},{8,9},{9,8},{1... | collective-permute-start | bytes 98312 | tf_op jit(solution)/shard_map/ppermute | solution.py:254
  35.4 4.3 %collective-permute-done.6.b = f32[8,1024]{1,0:T(8,128)S(1)} collective-permute-done((f32[8,1024]{1,0:T(8,128)S(1)}, f32[8,1024]{1,0:T(8,128)S(1)}, u32[]{:S(2)}, u32[]{:S(2)}) %collective-permute-start.6) | collective-permute-done | bytes 32800 | tf_op jit(solution)/shard_map/ppermute | solution.py:254
  39.6 0.0 collective-permute-done.1.refs_0_
  39.6 1.9 %collective-permute-start.7 = (f32[256,1024]{1,0:T(8,128)S(1)}, f32[256,1024]{1,0:T(8,128)S(1)}, u32[]{:S(2)}, u32[]{:S(2)}) collective-permute-start(f32[256,1024]{1,0:T(8,128)S(1)} %collective-permute-done.1.refs_0_), channel_id=1, source_target_pairs={{0,4},{4,0},{8,12},{12,8},{16,20},{20,16},{24,28},{28,24},{1,5},{5... | collective-permute-start | bytes 3145736 | tf_op jit(solution)/shard_map/ppermute | solution.py:236
  41.6 0.0 collective-permute-done.2.refs_1_
  41.6 2.4 %collective-permute-start.8 = (f32[256,1024]{1,0:T(8,128)S(1)}, f32[256,1024]{1,0:T(8,128)S(1)}, u32[]{:S(2)}, u32[]{:S(2)}) collective-permute-start(f32[256,1024]{1,0:T(8,128)S(1)} %collective-permute-done.2.refs_1_), channel_id=1, source_target_pairs={{0,4},{4,0},{8,12},{12,8},{16,20},{20,16},{24,28},{28,24},{1,5},{5... | collective-permute-start | bytes 3145736 | tf_op jit(solution)/shard_map/ppermute | solution.py:236
  44.0 2.4 %collective-permute-start.12 = (f32[8,1024]{1,0:T(8,128)S(1)}, f32[8,1024]{1,0:T(8,128)S(1)}, u32[]{:S(2)}, u32[]{:S(2)}) collective-permute-start(f32[8,1024]{1,0:T(8,128)S(1)} %shard_map.50.a), channel_id=1, source_target_pairs={{0,2},{1,3},{2,0},{3,1},{4,20},{5,21},{6,22},{7,23},{8,10},{9,11},... | collective-permute-start | bytes 98312 | tf_op jit(solution)/shard_map/ppermute | solution.py:254
  46.4 0.0 collective-permute-done.7.refs_2_
  46.4 2.9 %shard_map.51 = (f32[192,768]{1,0:T(8,128)S(1)}, f32[192,768]{1,0:T(8,128)S(1)}, bf16[384,1024]{1,0:T(8,128)(2,1)S(1)}, bf16[384,1024]{1,0:T(8,128)(2,1)S(1)}, b...) custom-call(f32[256,1024]{1,0:T(8,128)S(1)} %get-tuple-element.34.chip, ...), custom_call_target="tpu_custom_call" | custom-call | bytes 8388608 | tf_op jit(solution)/shard_map/pallas_call | solution.py:29
  49.3 2.0 %collective-permute-done.12.b = f32[8,1024]{1,0:T(8,128)S(1)} collective-permute-done((f32[8,1024]{1,0:T(8,128)S(1)}, f32[8,1024]{1,0:T(8,128)S(1)}, u32[]{:S(2)}, u32[]{:S(2)}) %collective-permute-start.12) | collective-permute-done | bytes 32800 | tf_op jit(solution)/shard_map/ppermute | solution.py:254
  51.3 0.1 shard_map.54
  51.4 2.0 %collective-permute-start.14 = (f32[264,1024]{1,0:T(8,128)S(1)}, f32[264,1024]{1,0:T(8,128)S(1)}, u32[]{:S(2)}, u32[]{:S(2)}) collective-permute-start(f32[264,1024]{1,0:T(8,128)S(1)} %get-tuple-element.47.sent), channel_id=1, source_target_pairs={{0,4},{4,0},{8,12},{12,8},{16,20},{20,16},{24,28},{28,24},{1,5},{5... | collective-permute-start | bytes 3244040 | tf_op jit(solution)/shard_map/ppermute | solution.py:236
  53.3 2.8 %collective-permute-start.9 = (f32[192,768]{1,0:T(8,128)S(1)}, f32[192,768]{1,0:T(8,128)S(1)}, u32[]{:S(2)}, u32[]{:S(2)}) collective-permute-start(f32[192,768]{1,0:T(8,128)S(1)} %get-tuple-element.40), channel_id=1, source_target_pairs={{0,32},{4,484},{8,40},{12,492},{16,48},{20,500},{24,56},{28,508},{... | collective-permute-start | bytes 1769480 | tf_op jit(solution)/shard_map/ppermute | solution.py:267
  56.2 3.2 %shard_map.55 = (f32[232,512]{1,0:T(8,128)S(1)}, f32[232,512]{1,0:T(8,128)S(1)}) custom-call(f32[264,1024]{1,0:T(8,128)S(1)} %get-tuple-element.47.sent, f32[264,1024]{1,0:T(8,128)S(1)} %collective-permute-done.14.swap, f32[1,1024]{1,0:T(1,128)S(1)} %get-tuple-element.38.refs_4_.weights, bf16[384,1024]{1,0:T(8,128)(2,1)S(1)} %get-tuple-element.48.ph, ...), custom_call_target="tpu_custom_call" | custom-call | tf_op jit(solution)/shard_map/pallas_call | solution.py:29
  59.4 3.8 %collective-permute-start.15 = (f32[232,512]{1,0:T(8,128)S(1)}, f32[232,512]{1,0:T(8,128)S(1)}, u32[]{:S(2)}, u32[]{:S(2)}) collective-permute-start(f32[232,512]{1,0:T(8,128)S(1)} %get-tuple-element.54), channel_id=1, source_target_pairs={{0,32},{4,484},{8,40},{12,492},{16,48},{20,500},{24,56},{28,508},{... | collective-permute-start | bytes 1425416 | tf_op jit(solution)/shard_map/ppermute | solution.py:267
  63.2 8.4 %collective-permute-done.9.came = f32[192,768]{1,0:T(8,128)S(1)} collective-permute-done((f32[192,768]{1,0:T(8,128)S(1)}, f32[192,768]{1,0:T(8,128)S(1)}, u32[]{:S(2)}, u32[]{:S(2)}) %collective-permute-start.9) | collective-permute-done | bytes 589856 | tf_op jit(solution)/shard_map/ppermute | solution.py:267
  71.6 0.1 shard_map.52
  71.7 1.9 %collective-permute-start.10 = (f32[96,768]{1,0:T(8,128)S(1)}, f32[96,768]{1,0:T(8,128)S(1)}, u32[]{:S(2)}, u32[]{:S(2)}) collective-permute-start(f32[96,768]{1,0:T(8,128)S(1)} %get-tuple-element.42), channel_id=1, source_target_pairs={{0,64},{4,452},{8,72},{12,460},{16,80},{20,468},{24,88},{28,476},{... | collective-permute-start | bytes 884744 | tf_op jit(solution)/shard_map/ppermute | solution.py:267
  73.6 3.1 %collective-permute-done.15.came = f32[232,512]{1,0:T(8,128)S(1)} collective-permute-done((f32[232,512]{1,0:T(8,128)S(1)}, f32[232,512]{1,0:T(8,128)S(1)}, u32[]{:S(2)}, u32[]{:S(2)}) %collective-permute-start.15) | collective-permute-done | bytes 475168 | tf_op jit(solution)/shard_map/ppermute | solution.py:267
  76.7 0.1 shard_map.56
  76.7 1.9 %collective-permute-start.16 = (f32[120,512]{1,0:T(8,128)S(1)}, f32[120,512]{1,0:T(8,128)S(1)}, u32[]{:S(2)}, u32[]{:S(2)}) collective-permute-start(f32[120,512]{1,0:T(8,128)S(1)} %get-tuple-element.56), channel_id=1, source_target_pairs={{0,64},{4,452},{8,72},{12,460},{16,80},{20,468},{24,88},{28,476},{... | collective-permute-start | bytes 737288 | tf_op jit(solution)/shard_map/ppermute | solution.py:267
  78.7 6.1 %collective-permute-done.10.came = f32[96,768]{1,0:T(8,128)S(1)} collective-permute-done((f32[96,768]{1,0:T(8,128)S(1)}, f32[96,768]{1,0:T(8,128)S(1)}, u32[]{:S(2)}, u32[]{:S(2)}) %collective-permute-start.10) | collective-permute-done | bytes 294944 | tf_op jit(solution)/shard_map/ppermute | solution.py:267
  84.8 1.9 %collective-permute-start.11 = (f32[48,768]{1,0:T(8,128)S(1)}, f32[48,768]{1,0:T(8,128)S(1)}, u32[]{:S(2)}, u32[]{:S(2)}) collective-permute-start(f32[48,768]{1,0:T(8,128)S(1)} %get-tuple-element.44), channel_id=1, source_target_pairs={{0,128},{4,388},{8,136},{12,396},{16,144},{20,404},{24,152},{28,41... | collective-permute-start | bytes 442376 | tf_op jit(solution)/shard_map/ppermute | solution.py:267
  86.8 3.8 %collective-permute-done.16.came = f32[120,512]{1,0:T(8,128)S(1)} collective-permute-done((f32[120,512]{1,0:T(8,128)S(1)}, f32[120,512]{1,0:T(8,128)S(1)}, u32[]{:S(2)}, u32[]{:S(2)}) %collective-permute-start.16) | collective-permute-done | bytes 245792 | tf_op jit(solution)/shard_map/ppermute | solution.py:267
  90.6 5.8 %collective-permute-start.17 = (f32[64,512]{1,0:T(8,128)S(1)}, f32[64,512]{1,0:T(8,128)S(1)}, u32[]{:S(2)}, u32[]{:S(2)}) collective-permute-start(f32[64,512]{1,0:T(8,128)S(1)} %get-tuple-element.58), channel_id=1, source_target_pairs={{0,128},{4,388},{8,136},{12,396},{16,144},{20,404},{24,152},{28,41... | collective-permute-start | bytes 393224 | tf_op jit(solution)/shard_map/ppermute | solution.py:267
  96.4 6.2 %collective-permute-done.11.came_a = f32[48,768]{1,0:T(8,128)S(1)} collective-permute-done((f32[48,768]{1,0:T(8,128)S(1)}, f32[48,768]{1,0:T(8,128)S(1)}, u32[]{:S(2)}, u32[]{:S(2)}) %collective-permute-start.11) | collective-permute-done | bytes 147488 | tf_op jit(solution)/shard_map/ppermute | solution.py:267
  102.7 2.0 %collective-permute-done.17.came_b = f32[64,512]{1,0:T(8,128)S(1)} collective-permute-done((f32[64,512]{1,0:T(8,128)S(1)}, f32[64,512]{1,0:T(8,128)S(1)}, u32[]{:S(2)}, u32[]{:S(2)}) %collective-permute-start.17) | collective-permute-done | bytes 131104 | tf_op jit(solution)/shard_map/ppermute | solution.py:267
  104.7 0.7 collective-permute-start.18
  105.4 2.2 %collective-permute-start.19 = (f32[40,1024]{1,0:T(8,128)S(1)}, f32[40,1024]{1,0:T(8,128)S(1)}, u32[]{:S(2)}, u32[]{:S(2)}) collective-permute-start(f32[40,1024]{1,0:T(8,128)S(1)} %get-tuple-element.60), channel_id=1, source_target_pairs={{0,4},{4,480},{8,12},{12,488},{16,20},{20,496},{24,28},{28,504},{3... | collective-permute-start | bytes 491528 | tf_op jit(solution)/shard_map/ppermute | solution.py:276
  107.6 4.4 %collective-permute-done.19.here = f32[40,1024]{1,0:T(8,128)S(1)} collective-permute-done((f32[40,1024]{1,0:T(8,128)S(1)}, f32[40,1024]{1,0:T(8,128)S(1)}, u32[]{:S(2)}, u32[]{:S(2)}) %collective-permute-start.19) | collective-permute-done | bytes 163872 | tf_op jit(solution)/shard_map/ppermute | solution.py:276
  112.1 0.7 shard_map.59
  (14 shorter events, 0.1 us)
Async XLA Ops:
  0.0 1.0 copy-start
  1.0 0.7 copy-start.1
  1.7 0.7 copy-start.2
  2.4 0.7 copy-start.3
  3.8 3.8 %collective-permute-start = (f32[128,1024]{1,0:T(8,128)S(1)}, f32[128,1024]{1,0:T(8,128)S(1)}, u32[]{:S(2)}, u32[]{:S(2)}) collective-permute-start(f32[128,1024]{1,0:T(8,128)S(1)} %get-tuple-element.33.own), channel_id=1, source_target_pairs={{0,4},{4,0},{8,12},{12,8},{16,20},{20,16},{24,28},{28,24},{1,5},{5... | collective-permute-start | bytes 1572872 | tf_op jit(solution)/shard_map/ppermute | solution.py:236
  7.7 31.9 %collective-permute-start.1 = (f32[256,1024]{1,0:T(8,128)S(1)}, f32[256,1024]{1,0:T(8,128)S(1)}, u32[]{:S(2)}, u32[]{:S(2)}) collective-permute-start(f32[256,1024]{1,0:T(8,128)S(1)} %get-tuple-element.34.chip), channel_id=1, source_target_pairs={{0,24},{1,25},{2,26},{3,27},{4,7},{5,4},{6,5},{7,6},{8,0},{9,1},{1... | collective-permute-start | bytes 3145736 | tf_op jit(solution)/shard_map/ppermute | solution.py:245
  12.6 28.9 %collective-permute-start.2 = (f32[256,1024]{1,0:T(8,128)S(1)}, f32[256,1024]{1,0:T(8,128)S(1)}, u32[]{:S(2)}, u32[]{:S(2)}) collective-permute-start(f32[256,1024]{1,0:T(8,128)S(1)} %get-tuple-element.34.chip), channel_id=1, source_target_pairs={{0,16},{1,17},{2,18},{3,19},{4,6},{5,7},{6,4},{7,5},{8,24},{9,25},... | collective-permute-start | bytes 3145736 | tf_op jit(solution)/shard_map/ppermute | solution.py:245
  15.2 6.2 %collective-permute-start.3 = (f32[8,1024]{1,0:T(8,128)S(1)}, f32[8,1024]{1,0:T(8,128)S(1)}, u32[]{:S(2)}, u32[]{:S(2)}) collective-permute-start(f32[8,1024]{1,0:T(8,128)S(1)} %get-tuple-element.35.a), channel_id=1, source_target_pairs={{0,1},{1,0},{2,3},{3,2},{4,12},{5,13},{6,14},{7,15},{8,9},{9,8},{1... | collective-permute-start | bytes 98312 | tf_op jit(solution)/shard_map/ppermute | solution.py:254
  21.4 7.7 %collective-permute-start.4 = (f32[8,1024]{1,0:T(8,128)S(1)}, f32[8,1024]{1,0:T(8,128)S(1)}, u32[]{:S(2)}, u32[]{:S(2)}) collective-permute-start(f32[8,1024]{1,0:T(8,128)S(1)} %shard_map.48.a), channel_id=1, source_target_pairs={{0,2},{1,3},{2,0},{3,1},{4,20},{5,21},{6,22},{7,23},{8,10},{9,11},... | collective-permute-start | bytes 98312 | tf_op jit(solution)/shard_map/ppermute | solution.py:254
  25.0 24.3 %collective-permute-start.13 = (f32[280,1024]{1,0:T(8,128)S(1)}, f32[280,1024]{1,0:T(8,128)S(1)}, u32[]{:S(2)}, u32[]{:S(2)}) collective-permute-start(f32[280,1024]{1,0:T(8,128)S(1)} %get-tuple-element.45), channel_id=1, source_target_pairs={{0,8},{1,9},{2,10},{3,11},{4,5},{5,6},{6,7},{7,4},{8,16},{9,17},{1... | collective-permute-start | bytes 3440648 | tf_op jit(solution)/shard_map/ppermute | solution.py:245
  29.1 4.3 %collective-permute-start.5 = (f32[8,1024]{1,0:T(8,128)S(1)}, f32[8,1024]{1,0:T(8,128)S(1)}, u32[]{:S(2)}, u32[]{:S(2)}) collective-permute-start(f32[8,1024]{1,0:T(8,128)S(1)} %shard_map.49), channel_id=1, source_target_pairs={{0,4},{4,0},{8,12},{12,8},{16,20},{20,16},{24,28},{28,24},{1,5},{5... | collective-permute-start | bytes 98312 | tf_op jit(solution)/shard_map/ppermute | solution.py:236
  33.4 6.2 %collective-permute-start.6 = (f32[8,1024]{1,0:T(8,128)S(1)}, f32[8,1024]{1,0:T(8,128)S(1)}, u32[]{:S(2)}, u32[]{:S(2)}) collective-permute-start(f32[8,1024]{1,0:T(8,128)S(1)} %collective-permute-done.5.a), channel_id=1, source_target_pairs={{0,1},{1,0},{2,3},{3,2},{4,12},{5,13},{6,14},{7,15},{8,9},{9,8},{1... | collective-permute-start | bytes 98312 | tf_op jit(solution)/shard_map/ppermute | solution.py:254
  39.6 6.8 %collective-permute-start.7 = (f32[256,1024]{1,0:T(8,128)S(1)}, f32[256,1024]{1,0:T(8,128)S(1)}, u32[]{:S(2)}, u32[]{:S(2)}) collective-permute-start(f32[256,1024]{1,0:T(8,128)S(1)} %collective-permute-done.1.refs_0_), channel_id=1, source_target_pairs={{0,4},{4,0},{8,12},{12,8},{16,20},{20,16},{24,28},{28,24},{1,5},{5... | collective-permute-start | bytes 3145736 | tf_op jit(solution)/shard_map/ppermute | solution.py:236
  41.6 4.8 %collective-permute-start.8 = (f32[256,1024]{1,0:T(8,128)S(1)}, f32[256,1024]{1,0:T(8,128)S(1)}, u32[]{:S(2)}, u32[]{:S(2)}) collective-permute-start(f32[256,1024]{1,0:T(8,128)S(1)} %collective-permute-done.2.refs_1_), channel_id=1, source_target_pairs={{0,4},{4,0},{8,12},{12,8},{16,20},{20,16},{24,28},{28,24},{1,5},{5... | collective-permute-start | bytes 3145736 | tf_op jit(solution)/shard_map/ppermute | solution.py:236
  44.0 7.3 %collective-permute-start.12 = (f32[8,1024]{1,0:T(8,128)S(1)}, f32[8,1024]{1,0:T(8,128)S(1)}, u32[]{:S(2)}, u32[]{:S(2)}) collective-permute-start(f32[8,1024]{1,0:T(8,128)S(1)} %shard_map.50.a), channel_id=1, source_target_pairs={{0,2},{1,3},{2,0},{3,1},{4,20},{5,21},{6,22},{7,23},{8,10},{9,11},... | collective-permute-start | bytes 98312 | tf_op jit(solution)/shard_map/ppermute | solution.py:254
  51.4 4.8 %collective-permute-start.14 = (f32[264,1024]{1,0:T(8,128)S(1)}, f32[264,1024]{1,0:T(8,128)S(1)}, u32[]{:S(2)}, u32[]{:S(2)}) collective-permute-start(f32[264,1024]{1,0:T(8,128)S(1)} %get-tuple-element.47.sent), channel_id=1, source_target_pairs={{0,4},{4,0},{8,12},{12,8},{16,20},{20,16},{24,28},{28,24},{1,5},{5... | collective-permute-start | bytes 3244040 | tf_op jit(solution)/shard_map/ppermute | solution.py:236
  53.3 18.3 %collective-permute-start.9 = (f32[192,768]{1,0:T(8,128)S(1)}, f32[192,768]{1,0:T(8,128)S(1)}, u32[]{:S(2)}, u32[]{:S(2)}) collective-permute-start(f32[192,768]{1,0:T(8,128)S(1)} %get-tuple-element.40), channel_id=1, source_target_pairs={{0,32},{4,484},{8,40},{12,492},{16,48},{20,500},{24,56},{28,508},{... | collective-permute-start | bytes 1769480 | tf_op jit(solution)/shard_map/ppermute | solution.py:267
  59.4 17.3 %collective-permute-start.15 = (f32[232,512]{1,0:T(8,128)S(1)}, f32[232,512]{1,0:T(8,128)S(1)}, u32[]{:S(2)}, u32[]{:S(2)}) collective-permute-start(f32[232,512]{1,0:T(8,128)S(1)} %get-tuple-element.54), channel_id=1, source_target_pairs={{0,32},{4,484},{8,40},{12,492},{16,48},{20,500},{24,56},{28,508},{... | collective-permute-start | bytes 1425416 | tf_op jit(solution)/shard_map/ppermute | solution.py:267
  71.7 13.1 %collective-permute-start.10 = (f32[96,768]{1,0:T(8,128)S(1)}, f32[96,768]{1,0:T(8,128)S(1)}, u32[]{:S(2)}, u32[]{:S(2)}) collective-permute-start(f32[96,768]{1,0:T(8,128)S(1)} %get-tuple-element.42), channel_id=1, source_target_pairs={{0,64},{4,452},{8,72},{12,460},{16,80},{20,468},{24,88},{28,476},{... | collective-permute-start | bytes 884744 | tf_op jit(solution)/shard_map/ppermute | solution.py:267
  76.7 13.9 %collective-permute-start.16 = (f32[120,512]{1,0:T(8,128)S(1)}, f32[120,512]{1,0:T(8,128)S(1)}, u32[]{:S(2)}, u32[]{:S(2)}) collective-permute-start(f32[120,512]{1,0:T(8,128)S(1)} %get-tuple-element.56), channel_id=1, source_target_pairs={{0,64},{4,452},{8,72},{12,460},{16,80},{20,468},{24,88},{28,476},{... | collective-permute-start | bytes 737288 | tf_op jit(solution)/shard_map/ppermute | solution.py:267
  84.8 17.8 %collective-permute-start.11 = (f32[48,768]{1,0:T(8,128)S(1)}, f32[48,768]{1,0:T(8,128)S(1)}, u32[]{:S(2)}, u32[]{:S(2)}) collective-permute-start(f32[48,768]{1,0:T(8,128)S(1)} %get-tuple-element.44), channel_id=1, source_target_pairs={{0,128},{4,388},{8,136},{12,396},{16,144},{20,404},{24,152},{28,41... | collective-permute-start | bytes 442376 | tf_op jit(solution)/shard_map/ppermute | solution.py:267
  90.6 14.1 %collective-permute-start.17 = (f32[64,512]{1,0:T(8,128)S(1)}, f32[64,512]{1,0:T(8,128)S(1)}, u32[]{:S(2)}, u32[]{:S(2)}) collective-permute-start(f32[64,512]{1,0:T(8,128)S(1)} %get-tuple-element.58), channel_id=1, source_target_pairs={{0,128},{4,388},{8,136},{12,396},{16,144},{20,404},{24,152},{28,41... | collective-permute-start | bytes 393224 | tf_op jit(solution)/shard_map/ppermute | solution.py:267
  104.7 2.9 %collective-permute-start.18 = (f32[40,1024]{1,0:T(8,128)S(1)}, f32[40,1024]{1,0:T(8,128)S(1)}, u32[]{:S(2)}, u32[]{:S(2)}) collective-permute-start(f32[40,1024]{1,0:T(8,128)S(1)} %get-tuple-element.59), channel_id=1, source_target_pairs={{0,0},{4,484},{8,8},{12,492},{16,16},{20,500},{24,24},{28,508},{32... | collective-permute-start | bytes 491528 | tf_op jit(solution)/shard_map/ppermute | solution.py:276
  105.4 6.6 %collective-permute-start.19 = (f32[40,1024]{1,0:T(8,128)S(1)}, f32[40,1024]{1,0:T(8,128)S(1)}, u32[]{:S(2)}, u32[]{:S(2)}) collective-permute-start(f32[40,1024]{1,0:T(8,128)S(1)} %get-tuple-element.60), channel_id=1, source_target_pairs={{0,4},{4,480},{8,12},{12,488},{16,20},{20,496},{24,28},{28,504},{3... | collective-permute-start | bytes 491528 | tf_op jit(solution)/shard_map/ppermute | solution.py:276

commit v5 on v4

--- a/solution.py
+++ b/solution.py
@@ -185,32 +185,27 @@
         stay[pl.ds(half, TOTALS), :] = both
 
 
-def give_body(mine_a, came_a, mine_b, came_b, give, keep):
-    def early(start, to):
-        return mine_a[pl.ds(start, POS), to] + came_a[pl.ds(start, POS), to]
-
-    def other(start, to):
-        return mine_b[pl.ds(start, POS), to] + came_b[pl.ds(start, POS), to]
-
-    def pairs(k, count=1):
-        return pl.ds(k * PAIR, count * PAIR)
-
+def give_early_body(mine, came, give, keep):
     for g, out in enumerate((keep, give)):
         for n in range(3):
-            at = pl.ds(n * POS, POS)
-            out[at, pairs(0, 3)] = early(n * 2 * POS + g * POS, pairs(0, 3))
-            out[at, pairs(3)] = other(4 * POS + n * POS, pairs(g))
-        at = pl.ds(3 * POS, POS)
-        out[at, pairs(0, 2)] = other(g * POS, pairs(0, 2))
-        out[at, pairs(2, 2)] = other(2 * POS + g * POS, pairs(0, 2))
-    for k in range(2):
-        at = pl.ds(LATE_ROWS + k, 1)
-        total = mine_b[at, :] + came_b[at, :]
-        for out in (keep, give):
-            out[pl.ds(PART, 1), pairs(2 * k, 2)] = total
-
-
-def finish_body(keep, here, out):
+            at = pl.ds(n * 2 * POS + g * POS, POS)
+            out[pl.ds(n * POS, POS), :] = mine[at, :] + came[at, :]
+
+
+def give_late_body(mine, came, give, keep):
+    for g, out in enumerate((keep, give)):
+        for k in range(2):
+            at = pl.ds(k * 2 * POS + g * POS, POS)
+            out[pl.ds(k * POS, POS), :] = mine[at, :] + came[at, :]
+        for n in range(3):
+            at, to = pl.ds(4 * POS + n * POS, POS), pl.ds(g * PAIR, PAIR)
+            out[pl.ds((2 + n) * POS, POS), pl.ds(0, PAIR)] = mine[at, to] + came[at, to]
+        out[pl.ds(2 * POS, 3 * POS), pl.ds(PAIR, PAIR)] = jnp.zeros((3 * POS, PAIR), F32)
+        at = pl.ds(LATE_ROWS, TOTALS)
+        out[pl.ds(5 * POS, TOTALS), :] = mine[at, :] + came[at, :]
+
+
+def finish_body(keep_a, here_a, keep_b, here_b, out):
     x, r, z = lax.axis_index("col"), lax.axis_index("row"), lax.axis_index("dom")
     core = lax.rem(r, 2)
     y = lax.div(r, 2)
@@ -219,13 +214,25 @@
     unit = (lanes == z * POS + rows).astype(F32)
     for m in range(4):
         for g in range(2):
-            mine, theirs = pl.ds(m * PAIR + g * WIDTH, WIDTH), pl.ds(m * PAIR + (1 - g) * WIDTH, WIDTH)
-            total = keep[pl.ds(PART, 1), mine] + here[pl.ds(PART, 1), theirs]
+            mine, theirs = m * PAIR + g * WIDTH, m * PAIR + (1 - g) * WIDTH
+
+            def folded(ref, row, lane):
+                return ref[row, pl.ds(lane % LATE_COLS, WIDTH)]
+
+            at = pl.ds(5 * POS + m // 2, 1)
+            total = folded(keep_b, at, mine) + folded(here_b, at, theirs)
             scale = PROT / (total + 1.0)
             group = 2 * lax.rem(y + m, 4) + (core if g == 0 else 1 - core)
             for n in range(N_COL):
-                at = pl.ds(n * POS, POS)
-                block = keep[at, mine] + here[at, theirs]
+                if n < 3 and m < 3:
+                    at = pl.ds(n * POS, POS)
+                    block = keep_a[at, pl.ds(mine, WIDTH)] + here_a[at, pl.ds(theirs, WIDTH)]
+                elif n < 3:
+                    at = pl.ds((2 + n) * POS, POS)
+                    block = folded(keep_b, at, g * WIDTH) + folded(here_b, at, (1 - g) * WIDTH)
+                else:
+                    at = pl.ds((m // 2) * POS, POS)
+                    block = folded(keep_b, at, mine) + folded(here_b, at, theirs)
                 if n == 0 and m == 0 and g == 0:
                     block = block + unit
                 place = lax.rem(x + n, N_COL) * (POS * N_ROW) + group
@@ -334,9 +341,12 @@
     a1, came_a = step(a1, came_a, 2 * EARLY_ROWS, 0, 2)
     b1, came_b = step(b1, came_b, 2 * LATE_ROWS, TOTALS, 2)
     a1, came_a = step(a1, came_a, EARLY_ROWS, 0, 4)
-    b1, came_b = step(b1, came_b, LATE_ROWS, TOTALS, 4)
-    give, keep = call(give_body, [(PART + TOTALS, 4 * PAIR)] * 2, [a1, came_a, b1, came_b])
-    (flow,) = call(finish_body, [(N_COL * POS * N_ROW, WIDTH)], [settled(keep, 0), settled(give, 1)])
+    b1, came_b = step(after(b1, a1), came_b, LATE_ROWS, TOTALS, 4)
+    give, keep = call(give_early_body, [(3 * POS, EARLY_COLS)] * 2, [a1, came_a])
+    ends = [settled(keep, 0), settled(give, 1)]
+    give, keep = call(give_late_body, [(5 * POS + TOTALS, LATE_COLS)] * 2, [after(b1, *ends), came_b])
+    ends += [settled(keep, 0), settled(give, 1)]
+    (flow,) = call(finish_body, [(N_COL * POS * N_ROW, WIDTH)], ends)
     return flow.reshape(1, N_COL, POS, N_ROW, 1, WIDTH)
 
 

time: 113 us -> 117 us (1.035)
  starting transfers between devices: 54.7 us -> 57 us
  waiting for transfers between devices: 46.8 us -> 48.1 us
    ppermute x2 -> x4, waiting for transfers between devices: 4.44 us -> 7.74 us  [settled(): return lax.ppermute(a, ('dom', 'row'), pairs)]
    ppermute x2 -> x4, starting transfers between devices: 2.85 us -> 5.17 us  [settled(): return lax.ppermute(a, ('dom', 'row'), pairs)]
    ppermute x6, waiting for transfers between devices: 29.7 us -> 27.7 us  [along_z(): return lax.ppermute(a, ('dom', 'row'), pairs)]
    pallas_call x14 -> x15, Pallas kernels: 7.9 us -> 7.91 us  [call(): pl.pallas_call(body, out_shape=[jax.ShapeDtypeStruct(s[:-1], BF16) if s[-...]
  transfers between devices with their start and end apart: 20 -> 22, of which waited for: 13 -> 13; matrix products, arithmetic and copies ran while one was open for 0% -> 0% of each run, Pallas kernels for 6% -> 5%
where the time goes in v5:
time: 117 us; the launch traced here: 116 us
  starting transfers between devices  57 us (49%)
  waiting for transfers between devices  48.1 us (41%)
  Pallas kernels  7.91 us (7%)
  local copies, waits for them, and re-layouts  3.04 us (3%)
    ppermute x6, waiting for transfers between devices, along_z(): return lax.ppermute(a, ('dom', 'row'), pairs)  27.7 us
    ppermute x6, starting transfers between devices, along_z(): return lax.ppermute(a, ('dom', 'row'), pairs)  18.2 us
    ppermute x5, starting transfers between devices, across(): return lax.ppermute(a, 'row', [(i, i ^ 1) for i in range(N_ROW)])  11.6 us
    ppermute x3, starting transfers between devices, around(): return lax.ppermute(a, ('row', 'col'), pairs)  11.4 us
    ppermute x4, starting transfers between devices, doubled(): return lax.ppermute(a, ('row', 'col'), pairs)  10.7 us
    ppermute x4, waiting for transfers between devices, doubled(): return lax.ppermute(a, ('row', 'col'), pairs)  9.91 us
    pallas_call x15, Pallas kernels, call(): pl.pallas_call(body, out_shape=[jax.ShapeDtypeStruct(s[:-1], BF16) if s[-...  7.91 us
    ppermute x4, waiting for transfers between devices, settled(): return lax.ppermute(a, ('dom', 'row'), pairs)  7.74 us
  transfers between devices with their start and end apart: 22, of which 13 were waited for; matrix products, arithmetic and copies ran while one was open for 0% of the time, Pallas kernels for 5%

profile of v5, /device:TPU:6, one launch (start us, length us, event | category | flops | bytes accessed | tf_op | source)
XLA Modules:
  0.0 116.4 jit_solution(640259490990987338)
XLA Ops:
  0.0 1.0 copy-done
  1.0 0.7 copy-done.1
  1.7 0.7 copy-done.2
  2.4 0.7 copy-done.3
  3.0 0.7 shard_map.46
  3.8 1.9 %collective-permute-start = (f32[128,1024]{1,0:T(8,128)S(1)}, f32[128,1024]{1,0:T(8,128)S(1)}, u32[]{:S(2)}, u32[]{:S(2)}) collective-permute-start(f32[128,1024]{1,0:T(8,128)S(1)} %get-tuple-element.37.own), channel_id=1, source_target_pairs={{0,4},{4,0},{8,12},{12,8},{16,20},{20,16},{24,28},{28,24},{1,5},{5... | collective-permute-start | bytes 1572872 | tf_op jit(solution)/shard_map/ppermute | solution.py:243
  5.7 1.9 %collective-permute-done.other = f32[128,1024]{1,0:T(8,128)S(1)} collective-permute-done((f32[128,1024]{1,0:T(8,128)S(1)}, f32[128,1024]{1,0:T(8,128)S(1)}, u32[]{:S(2)}, u32[]{:S(2)}) %collective-permute-start) | collective-permute-done | bytes 524320 | tf_op jit(solution)/shard_map/ppermute | solution.py:243
  7.6 0.1 shard_map.47
  7.7 4.9 %collective-permute-start.1 = (f32[256,1024]{1,0:T(8,128)S(1)}, f32[256,1024]{1,0:T(8,128)S(1)}, u32[]{:S(2)}, u32[]{:S(2)}) collective-permute-start(f32[256,1024]{1,0:T(8,128)S(1)} %get-tuple-element.38.chip), channel_id=1, source_target_pairs={{0,24},{1,25},{2,26},{3,27},{4,7},{5,4},{6,5},{7,6},{8,0},{9,1},{1... | collective-permute-start | bytes 3145736 | tf_op jit(solution)/shard_map/ppermute | solution.py:252
  12.6 2.5 %collective-permute-start.2 = (f32[256,1024]{1,0:T(8,128)S(1)}, f32[256,1024]{1,0:T(8,128)S(1)}, u32[]{:S(2)}, u32[]{:S(2)}) collective-permute-start(f32[256,1024]{1,0:T(8,128)S(1)} %get-tuple-element.38.chip), channel_id=1, source_target_pairs={{0,16},{1,17},{2,18},{3,19},{4,6},{5,7},{6,4},{7,5},{8,24},{9,25},... | collective-permute-start | bytes 3145736 | tf_op jit(solution)/shard_map/ppermute | solution.py:252
  15.2 2.7 %collective-permute-start.3 = (f32[8,1024]{1,0:T(8,128)S(1)}, f32[8,1024]{1,0:T(8,128)S(1)}, u32[]{:S(2)}, u32[]{:S(2)}) collective-permute-start(f32[8,1024]{1,0:T(8,128)S(1)} %get-tuple-element.39.a), channel_id=1, source_target_pairs={{0,1},{1,0},{2,3},{3,2},{4,12},{5,13},{6,14},{7,15},{8,9},{9,8},{1... | collective-permute-start | bytes 98312 | tf_op jit(solution)/shard_map/ppermute | solution.py:261
  17.9 3.5 %collective-permute-done.3.b = f32[8,1024]{1,0:T(8,128)S(1)} collective-permute-done((f32[8,1024]{1,0:T(8,128)S(1)}, f32[8,1024]{1,0:T(8,128)S(1)}, u32[]{:S(2)}, u32[]{:S(2)}) %collective-permute-start.3) | collective-permute-done | bytes 32800 | tf_op jit(solution)/shard_map/ppermute | solution.py:261
  21.4 3.6 %collective-permute-start.4 = (f32[8,1024]{1,0:T(8,128)S(1)}, f32[8,1024]{1,0:T(8,128)S(1)}, u32[]{:S(2)}, u32[]{:S(2)}) collective-permute-start(f32[8,1024]{1,0:T(8,128)S(1)} %shard_map.48.a), channel_id=1, source_target_pairs={{0,2},{1,3},{2,0},{3,1},{4,20},{5,21},{6,22},{7,23},{8,10},{9,11},... | collective-permute-start | bytes 98312 | tf_op jit(solution)/shard_map/ppermute | solution.py:261
  25.0 3.9 %collective-permute-start.15 = (f32[280,1024]{1,0:T(8,128)S(1)}, f32[280,1024]{1,0:T(8,128)S(1)}, u32[]{:S(2)}, u32[]{:S(2)}) collective-permute-start(f32[280,1024]{1,0:T(8,128)S(1)} %get-tuple-element.51), channel_id=1, source_target_pairs={{0,8},{1,9},{2,10},{3,11},{4,5},{5,6},{6,7},{7,4},{8,16},{9,17},{1... | collective-permute-start | bytes 3440648 | tf_op jit(solution)/shard_map/ppermute | solution.py:252
  28.9 0.2 collective-permute-done.4.b
  29.1 3.4 %collective-permute-start.5 = (f32[8,1024]{1,0:T(8,128)S(1)}, f32[8,1024]{1,0:T(8,128)S(1)}, u32[]{:S(2)}, u32[]{:S(2)}) collective-permute-start(f32[8,1024]{1,0:T(8,128)S(1)} %shard_map.49), channel_id=1, source_target_pairs={{0,4},{4,0},{8,12},{12,8},{16,20},{20,16},{24,28},{28,24},{1,5},{5... | collective-permute-start | bytes 98312 | tf_op jit(solution)/shard_map/ppermute | solution.py:243
  32.6 0.8 collective-permute-done.5.a
  33.4 1.9 %collective-permute-start.6 = (f32[8,1024]{1,0:T(8,128)S(1)}, f32[8,1024]{1,0:T(8,128)S(1)}, u32[]{:S(2)}, u32[]{:S(2)}) collective-permute-start(f32[8,1024]{1,0:T(8,128)S(1)} %collective-permute-done.5.a), channel_id=1, source_target_pairs={{0,1},{1,0},{2,3},{3,2},{4,12},{5,13},{6,14},{7,15},{8,9},{9,8},{1... | collective-permute-start | bytes 98312 | tf_op jit(solution)/shard_map/ppermute | solution.py:261
  35.4 4.3 %collective-permute-done.6.b = f32[8,1024]{1,0:T(8,128)S(1)} collective-permute-done((f32[8,1024]{1,0:T(8,128)S(1)}, f32[8,1024]{1,0:T(8,128)S(1)}, u32[]{:S(2)}, u32[]{:S(2)}) %collective-permute-start.6) | collective-permute-done | bytes 32800 | tf_op jit(solution)/shard_map/ppermute | solution.py:261
  39.6 0.0 collective-permute-done.1.refs_0_
  39.6 1.9 %collective-permute-start.7 = (f32[256,1024]{1,0:T(8,128)S(1)}, f32[256,1024]{1,0:T(8,128)S(1)}, u32[]{:S(2)}, u32[]{:S(2)}) collective-permute-start(f32[256,1024]{1,0:T(8,128)S(1)} %collective-permute-done.1.refs_0_), channel_id=1, source_target_pairs={{0,4},{4,0},{8,12},{12,8},{16,20},{20,16},{24,28},{28,24},{1,5},{5... | collective-permute-start | bytes 3145736 | tf_op jit(solution)/shard_map/ppermute | solution.py:243
  41.6 2.4 %collective-permute-start.8 = (f32[256,1024]{1,0:T(8,128)S(1)}, f32[256,1024]{1,0:T(8,128)S(1)}, u32[]{:S(2)}, u32[]{:S(2)}) collective-permute-start(f32[256,1024]{1,0:T(8,128)S(1)} %collective-permute-done.2.refs_1_), channel_id=1, source_target_pairs={{0,4},{4,0},{8,12},{12,8},{16,20},{20,16},{24,28},{28,24},{1,5},{5... | collective-permute-start | bytes 3145736 | tf_op jit(solution)/shard_map/ppermute | solution.py:243
  44.0 2.4 %collective-permute-start.14 = (f32[8,1024]{1,0:T(8,128)S(1)}, f32[8,1024]{1,0:T(8,128)S(1)}, u32[]{:S(2)}, u32[]{:S(2)}) collective-permute-start(f32[8,1024]{1,0:T(8,128)S(1)} %shard_map.50.a), channel_id=1, source_target_pairs={{0,2},{1,3},{2,0},{3,1},{4,20},{5,21},{6,22},{7,23},{8,10},{9,11},... | collective-permute-start | bytes 98312 | tf_op jit(solution)/shard_map/ppermute | solution.py:261
  46.4 2.9 %shard_map.51 = (f32[192,768]{1,0:T(8,128)S(1)}, f32[192,768]{1,0:T(8,128)S(1)}, bf16[384,1024]{1,0:T(8,128)(2,1)S(1)}, bf16[384,1024]{1,0:T(8,128)(2,1)S(1)}, b...) custom-call(f32[256,1024]{1,0:T(8,128)S(1)} %get-tuple-element.38.chip, ...), custom_call_target="tpu_custom_call" | custom-call | bytes 8388608 | tf_op jit(solution)/shard_map/pallas_call | solution.py:29
  49.3 2.0 %collective-permute-done.14.b = f32[8,1024]{1,0:T(8,128)S(1)} collective-permute-done((f32[8,1024]{1,0:T(8,128)S(1)}, f32[8,1024]{1,0:T(8,128)S(1)}, u32[]{:S(2)}, u32[]{:S(2)}) %collective-permute-start.14) | collective-permute-done | bytes 32800 | tf_op jit(solution)/shard_map/ppermute | solution.py:261
  51.3 0.1 shard_map.55
  51.4 2.0 %collective-permute-start.16 = (f32[264,1024]{1,0:T(8,128)S(1)}, f32[264,1024]{1,0:T(8,128)S(1)}, u32[]{:S(2)}, u32[]{:S(2)}) collective-permute-start(f32[264,1024]{1,0:T(8,128)S(1)} %get-tuple-element.53.sent), channel_id=1, source_target_pairs={{0,4},{4,0},{8,12},{12,8},{16,20},{20,16},{24,28},{28,24},{1,5},{5... | collective-permute-start | bytes 3244040 | tf_op jit(solution)/shard_map/ppermute | solution.py:243
  53.3 2.8 %collective-permute-start.9 = (f32[192,768]{1,0:T(8,128)S(1)}, f32[192,768]{1,0:T(8,128)S(1)}, u32[]{:S(2)}, u32[]{:S(2)}) collective-permute-start(f32[192,768]{1,0:T(8,128)S(1)} %get-tuple-element.44), channel_id=1, source_target_pairs={{0,32},{4,484},{8,40},{12,492},{16,48},{20,500},{24,56},{28,508},{... | collective-permute-start | bytes 1769480 | tf_op jit(solution)/shard_map/ppermute | solution.py:274
  56.2 3.2 %shard_map.56 = (f32[232,512]{1,0:T(8,128)S(1)}, f32[232,512]{1,0:T(8,128)S(1)}) custom-call(f32[264,1024]{1,0:T(8,128)S(1)} %get-tuple-element.53.sent, f32[264,1024]{1,0:T(8,128)S(1)} %collective-permute-done.16.swap, f32[1,1024]{1,0:T(1,128)S(1)} %get-tuple-element.42.refs_4_.weights, bf16[384,1024]{1,0:T(8,128)(2,1)S(1)} %get-tuple-element.54.ph, ...), custom_call_target="tpu_custom_call" | custom-call | tf_op jit(solution)/shard_map/pallas_call | solution.py:29
  59.4 3.8 %collective-permute-start.17 = (f32[232,512]{1,0:T(8,128)S(1)}, f32[232,512]{1,0:T(8,128)S(1)}, u32[]{:S(2)}, u32[]{:S(2)}) collective-permute-start(f32[232,512]{1,0:T(8,128)S(1)} %get-tuple-element.60), channel_id=1, source_target_pairs={{0,32},{4,484},{8,40},{12,492},{16,48},{20,500},{24,56},{28,508},{... | collective-permute-start | bytes 1425416 | tf_op jit(solution)/shard_map/ppermute | solution.py:274
  63.2 8.4 %collective-permute-done.9.came = f32[192,768]{1,0:T(8,128)S(1)} collective-permute-done((f32[192,768]{1,0:T(8,128)S(1)}, f32[192,768]{1,0:T(8,128)S(1)}, u32[]{:S(2)}, u32[]{:S(2)}) %collective-permute-start.9) | collective-permute-done | bytes 589856 | tf_op jit(solution)/shard_map/ppermute | solution.py:274
  71.6 0.1 shard_map.52
  71.7 1.9 %collective-permute-start.10 = (f32[96,768]{1,0:T(8,128)S(1)}, f32[96,768]{1,0:T(8,128)S(1)}, u32[]{:S(2)}, u32[]{:S(2)}) collective-permute-start(f32[96,768]{1,0:T(8,128)S(1)} %get-tuple-element.46), channel_id=1, source_target_pairs={{0,64},{4,452},{8,72},{12,460},{16,80},{20,468},{24,88},{28,476},{... | collective-permute-start | bytes 884744 | tf_op jit(solution)/shard_map/ppermute | solution.py:274
  73.6 3.1 %collective-permute-done.17.came = f32[232,512]{1,0:T(8,128)S(1)} collective-permute-done((f32[232,512]{1,0:T(8,128)S(1)}, f32[232,512]{1,0:T(8,128)S(1)}, u32[]{:S(2)}, u32[]{:S(2)}) %collective-permute-start.17) | collective-permute-done | bytes 475168 | tf_op jit(solution)/shard_map/ppermute | solution.py:274
  76.7 0.1 shard_map.57
  76.7 1.9 %collective-permute-start.18 = (f32[120,512]{1,0:T(8,128)S(1)}, f32[120,512]{1,0:T(8,128)S(1)}, u32[]{:S(2)}, u32[]{:S(2)}) collective-permute-start(f32[120,512]{1,0:T(8,128)S(1)} %get-tuple-element.63), channel_id=1, source_target_pairs={{0,64},{4,452},{8,72},{12,460},{16,80},{20,468},{24,88},{28,476},{... | collective-permute-start | bytes 737288 | tf_op jit(solution)/shard_map/ppermute | solution.py:274
  78.7 6.1 %collective-permute-done.10.came = f32[96,768]{1,0:T(8,128)S(1)} collective-permute-done((f32[96,768]{1,0:T(8,128)S(1)}, f32[96,768]{1,0:T(8,128)S(1)}, u32[]{:S(2)}, u32[]{:S(2)}) %collective-permute-start.10) | collective-permute-done | bytes 294944 | tf_op jit(solution)/shard_map/ppermute | solution.py:274
  84.8 1.9 %collective-permute-start.11 = (f32[48,768]{1,0:T(8,128)S(1)}, f32[48,768]{1,0:T(8,128)S(1)}, u32[]{:S(2)}, u32[]{:S(2)}) collective-permute-start(f32[48,768]{1,0:T(8,128)S(1)} %get-tuple-element.48), channel_id=1, source_target_pairs={{0,128},{4,388},{8,136},{12,396},{16,144},{20,404},{24,152},{28,41... | collective-permute-start | bytes 442376 | tf_op jit(solution)/shard_map/ppermute | solution.py:274
  86.8 3.8 %collective-permute-done.18.came = f32[120,512]{1,0:T(8,128)S(1)} collective-permute-done((f32[120,512]{1,0:T(8,128)S(1)}, f32[120,512]{1,0:T(8,128)S(1)}, u32[]{:S(2)}, u32[]{:S(2)}) %collective-permute-start.18) | collective-permute-done | bytes 245792 | tf_op jit(solution)/shard_map/ppermute | solution.py:274
  90.6 5.8 %collective-permute-start.19 = (f32[64,512]{1,0:T(8,128)S(1)}, f32[64,512]{1,0:T(8,128)S(1)}, u32[]{:S(2)}, u32[]{:S(2)}) collective-permute-start(f32[64,512]{1,0:T(8,128)S(1)} %get-tuple-element.66), channel_id=1, source_target_pairs={{0,128},{4,388},{8,136},{12,396},{16,144},{20,404},{24,152},{28,41... | collective-permute-start | bytes 393224 | tf_op jit(solution)/shard_map/ppermute | solution.py:274
  96.4 6.2 %collective-permute-done.11.came = f32[48,768]{1,0:T(8,128)S(1)} collective-permute-done((f32[48,768]{1,0:T(8,128)S(1)}, f32[48,768]{1,0:T(8,128)S(1)}, u32[]{:S(2)}, u32[]{:S(2)}) %collective-permute-start.11) | collective-permute-done | bytes 147488 | tf_op jit(solution)/shard_map/ppermute | solution.py:274
  102.7 0.7 collective-permute-start.12
  103.4 1.9 %collective-permute-start.13 = (f32[24,768]{1,0:T(8,128)S(1)}, f32[24,768]{1,0:T(8,128)S(1)}, u32[]{:S(2)}, u32[]{:S(2)}) collective-permute-start(f32[24,768]{1,0:T(8,128)S(1)} %get-tuple-element.50), channel_id=1, source_target_pairs={{0,4},{4,480},{8,12},{12,488},{16,20},{20,496},{24,28},{28,504},{3... | collective-permute-start | bytes 221192 | tf_op jit(solution)/shard_map/ppermute | solution.py:283
  105.3 3.7 %collective-permute-done.13.here_a = f32[24,768]{1,0:T(8,128)S(1)} collective-permute-done((f32[24,768]{1,0:T(8,128)S(1)}, f32[24,768]{1,0:T(8,128)S(1)}, u32[]{:S(2)}, u32[]{:S(2)}) %collective-permute-start.13) | collective-permute-done | bytes 73760 | tf_op jit(solution)/shard_map/ppermute | solution.py:283
  109.1 0.7 collective-permute-start.20
  109.7 1.9 %collective-permute-start.21 = (f32[48,512]{1,0:T(8,128)S(1)}, f32[48,512]{1,0:T(8,128)S(1)}, u32[]{:S(2)}, u32[]{:S(2)}) collective-permute-start(f32[48,512]{1,0:T(8,128)S(1)} %get-tuple-element.68), channel_id=1, source_target_pairs={{0,4},{4,480},{8,12},{12,488},{16,20},{20,496},{24,28},{28,504},{3... | collective-permute-start | bytes 294920 | tf_op jit(solution)/shard_map/ppermute | solution.py:283
  111.7 4.0 %collective-permute-done.21.here_b = f32[48,512]{1,0:T(8,128)S(1)} collective-permute-done((f32[48,512]{1,0:T(8,128)S(1)}, f32[48,512]{1,0:T(8,128)S(1)}, u32[]{:S(2)}, u32[]{:S(2)}) %collective-permute-start.21) | collective-permute-done | bytes 98336 | tf_op jit(solution)/shard_map/ppermute | solution.py:283
  115.7 0.7 shard_map.60
  (19 shorter events, 0.1 us)
Async XLA Ops:
  0.0 1.0 copy-start
  1.0 0.7 copy-start.1
  1.7 0.7 copy-start.2
  2.4 0.7 copy-start.3
  3.8 3.8 %collective-permute-start = (f32[128,1024]{1,0:T(8,128)S(1)}, f32[128,1024]{1,0:T(8,128)S(1)}, u32[]{:S(2)}, u32[]{:S(2)}) collective-permute-start(f32[128,1024]{1,0:T(8,128)S(1)} %get-tuple-element.37.own), channel_id=1, source_target_pairs={{0,4},{4,0},{8,12},{12,8},{16,20},{20,16},{24,28},{28,24},{1,5},{5... | collective-permute-start | bytes 1572872 | tf_op jit(solution)/shard_map/ppermute | solution.py:243
  7.7 31.9 %collective-permute-start.1 = (f32[256,1024]{1,0:T(8,128)S(1)}, f32[256,1024]{1,0:T(8,128)S(1)}, u32[]{:S(2)}, u32[]{:S(2)}) collective-permute-start(f32[256,1024]{1,0:T(8,128)S(1)} %get-tuple-element.38.chip), channel_id=1, source_target_pairs={{0,24},{1,25},{2,26},{3,27},{4,7},{5,4},{6,5},{7,6},{8,0},{9,1},{1... | collective-permute-start | bytes 3145736 | tf_op jit(solution)/shard_map/ppermute | solution.py:252
  12.6 28.9 %collective-permute-start.2 = (f32[256,1024]{1,0:T(8,128)S(1)}, f32[256,1024]{1,0:T(8,128)S(1)}, u32[]{:S(2)}, u32[]{:S(2)}) collective-permute-start(f32[256,1024]{1,0:T(8,128)S(1)} %get-tuple-element.38.chip), channel_id=1, source_target_pairs={{0,16},{1,17},{2,18},{3,19},{4,6},{5,7},{6,4},{7,5},{8,24},{9,25},... | collective-permute-start | bytes 3145736 | tf_op jit(solution)/shard_map/ppermute | solution.py:252
  15.2 6.2 %collective-permute-start.3 = (f32[8,1024]{1,0:T(8,128)S(1)}, f32[8,1024]{1,0:T(8,128)S(1)}, u32[]{:S(2)}, u32[]{:S(2)}) collective-permute-start(f32[8,1024]{1,0:T(8,128)S(1)} %get-tuple-element.39.a), channel_id=1, source_target_pairs={{0,1},{1,0},{2,3},{3,2},{4,12},{5,13},{6,14},{7,15},{8,9},{9,8},{1... | collective-permute-start | bytes 98312 | tf_op jit(solution)/shard_map/ppermute | solution.py:261
  21.4 7.7 %collective-permute-start.4 = (f32[8,1024]{1,0:T(8,128)S(1)}, f32[8,1024]{1,0:T(8,128)S(1)}, u32[]{:S(2)}, u32[]{:S(2)}) collective-permute-start(f32[8,1024]{1,0:T(8,128)S(1)} %shard_map.48.a), channel_id=1, source_target_pairs={{0,2},{1,3},{2,0},{3,1},{4,20},{5,21},{6,22},{7,23},{8,10},{9,11},... | collective-permute-start | bytes 98312 | tf_op jit(solution)/shard_map/ppermute | solution.py:261
  25.0 24.3 %collective-permute-start.15 = (f32[280,1024]{1,0:T(8,128)S(1)}, f32[280,1024]{1,0:T(8,128)S(1)}, u32[]{:S(2)}, u32[]{:S(2)}) collective-permute-start(f32[280,1024]{1,0:T(8,128)S(1)} %get-tuple-element.51), channel_id=1, source_target_pairs={{0,8},{1,9},{2,10},{3,11},{4,5},{5,6},{6,7},{7,4},{8,16},{9,17},{1... | collective-permute-start | bytes 3440648 | tf_op jit(solution)/shard_map/ppermute | solution.py:252
  29.1 4.3 %collective-permute-start.5 = (f32[8,1024]{1,0:T(8,128)S(1)}, f32[8,1024]{1,0:T(8,128)S(1)}, u32[]{:S(2)}, u32[]{:S(2)}) collective-permute-start(f32[8,1024]{1,0:T(8,128)S(1)} %shard_map.49), channel_id=1, source_target_pairs={{0,4},{4,0},{8,12},{12,8},{16,20},{20,16},{24,28},{28,24},{1,5},{5... | collective-permute-start | bytes 98312 | tf_op jit(solution)/shard_map/ppermute | solution.py:243
  33.4 6.2 %collective-permute-start.6 = (f32[8,1024]{1,0:T(8,128)S(1)}, f32[8,1024]{1,0:T(8,128)S(1)}, u32[]{:S(2)}, u32[]{:S(2)}) collective-permute-start(f32[8,1024]{1,0:T(8,128)S(1)} %collective-permute-done.5.a), channel_id=1, source_target_pairs={{0,1},{1,0},{2,3},{3,2},{4,12},{5,13},{6,14},{7,15},{8,9},{9,8},{1... | collective-permute-start | bytes 98312 | tf_op jit(solution)/shard_map/ppermute | solution.py:261
  39.6 6.8 %collective-permute-start.7 = (f32[256,1024]{1,0:T(8,128)S(1)}, f32[256,1024]{1,0:T(8,128)S(1)}, u32[]{:S(2)}, u32[]{:S(2)}) collective-permute-start(f32[256,1024]{1,0:T(8,128)S(1)} %collective-permute-done.1.refs_0_), channel_id=1, source_target_pairs={{0,4},{4,0},{8,12},{12,8},{16,20},{20,16},{24,28},{28,24},{1,5},{5... | collective-permute-start | bytes 3145736 | tf_op jit(solution)/shard_map/ppermute | solution.py:243
  41.6 4.8 %collective-permute-start.8 = (f32[256,1024]{1,0:T(8,128)S(1)}, f32[256,1024]{1,0:T(8,128)S(1)}, u32[]{:S(2)}, u32[]{:S(2)}) collective-permute-start(f32[256,1024]{1,0:T(8,128)S(1)} %collective-permute-done.2.refs_1_), channel_id=1, source_target_pairs={{0,4},{4,0},{8,12},{12,8},{16,20},{20,16},{24,28},{28,24},{1,5},{5... | collective-permute-start | bytes 3145736 | tf_op jit(solution)/shard_map/ppermute | solution.py:243
  44.0 7.3 %collective-permute-start.14 = (f32[8,1024]{1,0:T(8,128)S(1)}, f32[8,1024]{1,0:T(8,128)S(1)}, u32[]{:S(2)}, u32[]{:S(2)}) collective-permute-start(f32[8,1024]{1,0:T(8,128)S(1)} %shard_map.50.a), channel_id=1, source_target_pairs={{0,2},{1,3},{2,0},{3,1},{4,20},{5,21},{6,22},{7,23},{8,10},{9,11},... | collective-permute-start | bytes 98312 | tf_op jit(solution)/shard_map/ppermute | solution.py:261
  51.4 4.8 %collective-permute-start.16 = (f32[264,1024]{1,0:T(8,128)S(1)}, f32[264,1024]{1,0:T(8,128)S(1)}, u32[]{:S(2)}, u32[]{:S(2)}) collective-permute-start(f32[264,1024]{1,0:T(8,128)S(1)} %get-tuple-element.53.sent), channel_id=1, source_target_pairs={{0,4},{4,0},{8,12},{12,8},{16,20},{20,16},{24,28},{28,24},{1,5},{5... | collective-permute-start | bytes 3244040 | tf_op jit(solution)/shard_map/ppermute | solution.py:243
  53.3 18.3 %collective-permute-start.9 = (f32[192,768]{1,0:T(8,128)S(1)}, f32[192,768]{1,0:T(8,128)S(1)}, u32[]{:S(2)}, u32[]{:S(2)}) collective-permute-start(f32[192,768]{1,0:T(8,128)S(1)} %get-tuple-element.44), channel_id=1, source_target_pairs={{0,32},{4,484},{8,40},{12,492},{16,48},{20,500},{24,56},{28,508},{... | collective-permute-start | bytes 1769480 | tf_op jit(solution)/shard_map/ppermute | solution.py:274
  59.4 17.3 %collective-permute-start.17 = (f32[232,512]{1,0:T(8,128)S(1)}, f32[232,512]{1,0:T(8,128)S(1)}, u32[]{:S(2)}, u32[]{:S(2)}) collective-permute-start(f32[232,512]{1,0:T(8,128)S(1)} %get-tuple-element.60), channel_id=1, source_target_pairs={{0,32},{4,484},{8,40},{12,492},{16,48},{20,500},{24,56},{28,508},{... | collective-permute-start | bytes 1425416 | tf_op jit(solution)/shard_map/ppermute | solution.py:274
  71.7 13.1 %collective-permute-start.10 = (f32[96,768]{1,0:T(8,128)S(1)}, f32[96,768]{1,0:T(8,128)S(1)}, u32[]{:S(2)}, u32[]{:S(2)}) collective-permute-start(f32[96,768]{1,0:T(8,128)S(1)} %get-tuple-element.46), channel_id=1, source_target_pairs={{0,64},{4,452},{8,72},{12,460},{16,80},{20,468},{24,88},{28,476},{... | collective-permute-start | bytes 884744 | tf_op jit(solution)/shard_map/ppermute | solution.py:274
  76.7 13.9 %collective-permute-start.18 = (f32[120,512]{1,0:T(8,128)S(1)}, f32[120,512]{1,0:T(8,128)S(1)}, u32[]{:S(2)}, u32[]{:S(2)}) collective-permute-start(f32[120,512]{1,0:T(8,128)S(1)} %get-tuple-element.63), channel_id=1, source_target_pairs={{0,64},{4,452},{8,72},{12,460},{16,80},{20,468},{24,88},{28,476},{... | collective-permute-start | bytes 737288 | tf_op jit(solution)/shard_map/ppermute | solution.py:274
  84.8 17.8 %collective-permute-start.11 = (f32[48,768]{1,0:T(8,128)S(1)}, f32[48,768]{1,0:T(8,128)S(1)}, u32[]{:S(2)}, u32[]{:S(2)}) collective-permute-start(f32[48,768]{1,0:T(8,128)S(1)} %get-tuple-element.48), channel_id=1, source_target_pairs={{0,128},{4,388},{8,136},{12,396},{16,144},{20,404},{24,152},{28,41... | collective-permute-start | bytes 442376 | tf_op jit(solution)/shard_map/ppermute | solution.py:274
  90.6 18.4 %collective-permute-start.19 = (f32[64,512]{1,0:T(8,128)S(1)}, f32[64,512]{1,0:T(8,128)S(1)}, u32[]{:S(2)}, u32[]{:S(2)}) collective-permute-start(f32[64,512]{1,0:T(8,128)S(1)} %get-tuple-element.66), channel_id=1, source_target_pairs={{0,128},{4,388},{8,136},{12,396},{16,144},{20,404},{24,152},{28,41... | collective-permute-start | bytes 393224 | tf_op jit(solution)/shard_map/ppermute | solution.py:274
  102.7 2.6 %collective-permute-start.12 = (f32[24,768]{1,0:T(8,128)S(1)}, f32[24,768]{1,0:T(8,128)S(1)}, u32[]{:S(2)}, u32[]{:S(2)}) collective-permute-start(f32[24,768]{1,0:T(8,128)S(1)} %get-tuple-element.49), channel_id=1, source_target_pairs={{0,0},{4,484},{8,8},{12,492},{16,16},{20,500},{24,24},{28,508},{32... | collective-permute-start | bytes 221192 | tf_op jit(solution)/shard_map/ppermute | solution.py:283
  103.4 5.7 %collective-permute-start.13 = (f32[24,768]{1,0:T(8,128)S(1)}, f32[24,768]{1,0:T(8,128)S(1)}, u32[]{:S(2)}, u32[]{:S(2)}) collective-permute-start(f32[24,768]{1,0:T(8,128)S(1)} %get-tuple-element.50), channel_id=1, source_target_pairs={{0,4},{4,480},{8,12},{12,488},{16,20},{20,496},{24,28},{28,504},{3... | collective-permute-start | bytes 221192 | tf_op jit(solution)/shard_map/ppermute | solution.py:283
  109.1 2.6 %collective-permute-start.20 = (f32[48,512]{1,0:T(8,128)S(1)}, f32[48,512]{1,0:T(8,128)S(1)}, u32[]{:S(2)}, u32[]{:S(2)}) collective-permute-start(f32[48,512]{1,0:T(8,128)S(1)} %get-tuple-element.67), channel_id=1, source_target_pairs={{0,0},{4,484},{8,8},{12,492},{16,16},{20,500},{24,24},{28,508},{32... | collective-permute-start | bytes 294920 | tf_op jit(solution)/shard_map/ppermute | solution.py:283
  109.7 5.9 %collective-permute-start.21 = (f32[48,512]{1,0:T(8,128)S(1)}, f32[48,512]{1,0:T(8,128)S(1)}, u32[]{:S(2)}, u32[]{:S(2)}) collective-permute-start(f32[48,512]{1,0:T(8,128)S(1)} %get-tuple-element.68), channel_id=1, source_target_pairs={{0,4},{4,480},{8,12},{12,488},{16,20},{20,496},{24,28},{28,504},{3... | collective-permute-start | bytes 294920 | tf_op jit(solution)/shard_map/ppermute | solution.py:283

commit v6 on v4

--- a/solution.py
+++ b/solution.py
@@ -44,7 +44,7 @@
 
 
 def mask_body(*refs):
-    sources, (own, sums, weights), targets, done = refs[:4], refs[4:7], refs[7:11], refs[11]
+    sources, (own, weights), targets, done = refs[:4], refs[4:6], refs[6:10], refs[10]
     copies = [pltpu.make_async_copy(a, b, done.at[i]) for i, (a, b) in enumerate(zip(sources, targets))]
     for copy in copies:
         copy.start()
@@ -60,24 +60,19 @@
     for t in range(PANEL // TILE):
         at = pl.ds(t * TILE, TILE)
         kept = panel[:, at] * tile_mask[0, t].astype(F32)
-        own[:, at] = kept
-        sums[:, at] = jnp.broadcast_to(jnp.sum(kept, axis=0, keepdims=True), (8, TILE))
-
-
-def join_body(own, other, chip, again):
+        own[pl.ds(0, WIDTH), at] = kept
+        own[pl.ds(WIDTH, 8), at] = jnp.broadcast_to(jnp.sum(kept, axis=0, keepdims=True), (8, TILE))
+
+
+def join_body(own, other, chip, again, sums):
     for out in (chip, again):
-        out[pl.ds(0, WIDTH), :] = own[...]
-        out[pl.ds(WIDTH, WIDTH), :] = other[...]
+        out[pl.ds(0, WIDTH), :] = own[pl.ds(0, WIDTH), :]
+        out[pl.ds(WIDTH, WIDTH), :] = other[pl.ds(0, WIDTH), :]
+    sums[...] = own[pl.ds(WIDTH, 8), :] + other[pl.ds(WIDTH, 8), :]
 
 
 def add_body(a, b, out):
     out[...] = a[...] + b[...]
-
-
-def put_body(a, b, panels, out, sums):
-    sums[...] = a[...] + b[...]
-    out[pl.ds(0, 2 * WIDTH), :] = panels[pl.ds(0, 2 * WIDTH), :]
-    out[pl.ds(2 * WIDTH, 8), :] = sums[...]
 
 
 def split(x):
@@ -136,7 +131,7 @@
             outs[j // 4][at, :] = block[rows : rows + 2 * POS]
 
 
-def late_body(sent, swap, weights, ph, pl_, qh, ql, sums, first, second, fh, fl, gh, gl):
+def late_body(sent, swap, weights, ph, pl_, qh, ql, sums, pair, first, second, fh, fl, gh, gl):
     core = core_of()
 
     @pl.when(core == 0)
@@ -149,7 +144,7 @@
         fill_rows(fh, fl, weights, 0, sent, False)
         fill_columns(gh, gl, 0, swap, True)
 
-    total = (sums[...] + swap[pl.ds(2 * WIDTH, 8), :]) * weights[...]
+    total = (sums[...] + pair[...]) * weights[...]
     at = pl.ds(WIDTH, 16)
     fh[at, :], fl[at, :] = split(jnp.concatenate([total, total], axis=0))
     late_early = dot3(fh[...], fl[...], qh[...], ql[...])
@@ -278,9 +273,9 @@
 
 def per_device(protein_panel, tile_mask, domain_class, class_weight):
     tiles, classes = PANEL // TILE, class_weight.shape[0]
-    own, sums, weights = call(
+    own, weights = call(
         mask_body,
-        [(WIDTH, PANEL), (8, PANEL), (1, PANEL)],
+        [(WIDTH + 8, PANEL), (1, PANEL)],
         [
             protein_panel.reshape(WIDTH, PANEL),
             tile_mask.reshape(1, tiles),
@@ -297,7 +292,11 @@
         ],
     )
     other = across(own)
-    chip, again = call(join_body, [(2 * WIDTH, PANEL), (2 * WIDTH + 24, PANEL)], [own, other])
+    chip, again, sums = call(
+        join_body,
+        [(2 * WIDTH, PANEL), (2 * WIDTH + 24, PANEL), (8, PANEL)],
+        [own, other],
+    )
     from_next, from_far, from_last = around(chip, -1), around(chip, 2), around(again, 1)
 
     def both(a, bit):
@@ -307,6 +306,7 @@
     swap_far = across(after(from_far, sums))
     sums = both(sums, 1)
     swap_next = across(after(from_next, sums))
+
     early, columns = (3 * WIDTH, PANEL, BF16), (EARLY_COLS, PANEL, BF16)
     a0, a1, ph, pl_, qh, ql = call(
         early_body,
@@ -315,12 +315,12 @@
         mib=16, nbytes=8 << 20,
     )
     came_a = along_z(a0, 1)
-    from_last, sums = call(put_body, [(2 * WIDTH + 8, PANEL), (8, PANEL)], [sums, doubled(sums, 2), after(from_last, a0)])
-    swap_last = across(from_last)
+    pair = doubled(sums, 2)
+    swap_last = across(after(from_last, a0, pair))
     b0, b1 = call(
         late_body,
         [(4 * LATE_ROWS + TOTALS, LATE_COLS)] * 2,
-        [from_last, swap_last, weights, ph, pl_, qh, ql, sums],
+        [from_last, swap_last, weights, ph, pl_, qh, ql, sums, pair],
         mib=16, nbytes=0,
         scratch=[pltpu.VMEM((WIDTH + 16, PANEL), BF16)] * 2 + [pltpu.VMEM((PAIR, PANEL), BF16)] * 2,
     )

time: 113 us -> 113 us (level)
    pallas_call x14 -> x13, Pallas kernels: 7.9 us -> 7.82 us  [call(): pl.pallas_call(body, out_shape=[jax.ShapeDtypeStruct(s[:-1], BF16) if s[-...]
where the time goes in v6:
time: 113 us
  starting transfers between devices  54.7 us (48%)
  waiting for transfers between devices  46.9 us (42%)
  Pallas kernels  7.82 us (7%)
  local copies, waits for them, and re-layouts  3.04 us (3%)
    ppermute x6, waiting for transfers between devices, along_z(): return lax.ppermute(a, ('dom', 'row'), pairs)  29.8 us
    ppermute x6, starting transfers between devices, along_z(): return lax.ppermute(a, ('dom', 'row'), pairs)  18.2 us
    ppermute x5, starting transfers between devices, across(): return lax.ppermute(a, 'row', [(i, i ^ 1) for i in range(N_ROW)])  11.6 us
    ppermute x3, starting transfers between devices, around(): return lax.ppermute(a, ('row', 'col'), pairs)  11.4 us
    ppermute x4, starting transfers between devices, doubled(): return lax.ppermute(a, ('row', 'col'), pairs)  10.7 us
    ppermute x4, waiting for transfers between devices, doubled(): return lax.ppermute(a, ('row', 'col'), pairs)  9.92 us
    pallas_call x13, Pallas kernels, call(): pl.pallas_call(body, out_shape=[jax.ShapeDtypeStruct(s[:-1], BF16) if s[-...  7.82 us
    ppermute x2, waiting for transfers between devices, settled(): return lax.ppermute(a, ('dom', 'row'), pairs)  4.45 us
  transfers between devices with their start and end apart: 20, of which 13 were waited for; matrix products, arithmetic and copies ran while one was open for 0% of the time, Pallas kernels for 6%

profile of v6, /device:TPU:6, one launch (start us, length us, event | category | flops | bytes accessed | tf_op | source)
XLA Modules:
  0.0 112.7 jit_solution(17589618075723907902)
XLA Ops:
  0.0 1.0 copy-done
  1.0 0.7 copy-done.1
  1.7 0.7 copy-done.2
  2.4 0.7 copy-done.3
  3.0 0.7 shard_map.46
  3.8 1.9 %collective-permute-start = (f32[136,1024]{1,0:T(8,128)S(1)}, f32[136,1024]{1,0:T(8,128)S(1)}, u32[]{:S(2)}, u32[]{:S(2)}) collective-permute-start(f32[136,1024]{1,0:T(8,128)S(1)} %get-tuple-element.31.own), channel_id=1, source_target_pairs={{0,4},{4,0},{8,12},{12,8},{16,20},{20,16},{24,28},{28,24},{1,5},{5... | collective-permute-start | bytes 1671176 | tf_op jit(solution)/shard_map/ppermute | solution.py:231
  5.7 1.9 %collective-permute-done.other = f32[136,1024]{1,0:T(8,128)S(1)} collective-permute-done((f32[136,1024]{1,0:T(8,128)S(1)}, f32[136,1024]{1,0:T(8,128)S(1)}, u32[]{:S(2)}, u32[]{:S(2)}) %collective-permute-start) | collective-permute-done | bytes 557088 | tf_op jit(solution)/shard_map/ppermute | solution.py:231
  7.6 0.1 shard_map.47
  7.8 4.9 %collective-permute-start.1 = (f32[256,1024]{1,0:T(8,128)S(1)}, f32[256,1024]{1,0:T(8,128)S(1)}, u32[]{:S(2)}, u32[]{:S(2)}) collective-permute-start(f32[256,1024]{1,0:T(8,128)S(1)} %get-tuple-element.32.chip), channel_id=1, source_target_pairs={{0,24},{1,25},{2,26},{3,27},{4,7},{5,4},{6,5},{7,6},{8,0},{9,1},{1... | collective-permute-start | bytes 3145736 | tf_op jit(solution)/shard_map/ppermute | solution.py:240
  12.7 2.5 %collective-permute-start.2 = (f32[256,1024]{1,0:T(8,128)S(1)}, f32[256,1024]{1,0:T(8,128)S(1)}, u32[]{:S(2)}, u32[]{:S(2)}) collective-permute-start(f32[256,1024]{1,0:T(8,128)S(1)} %get-tuple-element.32.chip), channel_id=1, source_target_pairs={{0,16},{1,17},{2,18},{3,19},{4,6},{5,7},{6,4},{7,5},{8,24},{9,25},... | collective-permute-start | bytes 3145736 | tf_op jit(solution)/shard_map/ppermute | solution.py:240
  15.2 2.7 %collective-permute-start.3 = (f32[8,1024]{1,0:T(8,128)S(1)}, f32[8,1024]{1,0:T(8,128)S(1)}, u32[]{:S(2)}, u32[]{:S(2)}) collective-permute-start(f32[8,1024]{1,0:T(8,128)S(1)} %get-tuple-element.33.a), channel_id=1, source_target_pairs={{0,1},{1,0},{2,3},{3,2},{4,12},{5,13},{6,14},{7,15},{8,9},{9,8},{1... | collective-permute-start | bytes 98312 | tf_op jit(solution)/shard_map/ppermute | solution.py:249
  18.0 3.5 %collective-permute-done.3.b = f32[8,1024]{1,0:T(8,128)S(1)} collective-permute-done((f32[8,1024]{1,0:T(8,128)S(1)}, f32[8,1024]{1,0:T(8,128)S(1)}, u32[]{:S(2)}, u32[]{:S(2)}) %collective-permute-start.3) | collective-permute-done | bytes 32800 | tf_op jit(solution)/shard_map/ppermute | solution.py:249
  21.5 3.6 %collective-permute-start.4 = (f32[8,1024]{1,0:T(8,128)S(1)}, f32[8,1024]{1,0:T(8,128)S(1)}, u32[]{:S(2)}, u32[]{:S(2)}) collective-permute-start(f32[8,1024]{1,0:T(8,128)S(1)} %shard_map.48.a), channel_id=1, source_target_pairs={{0,2},{1,3},{2,0},{3,1},{4,20},{5,21},{6,22},{7,23},{8,10},{9,11},... | collective-permute-start | bytes 98312 | tf_op jit(solution)/shard_map/ppermute | solution.py:249
  25.1 3.9 %collective-permute-start.12 = (f32[280,1024]{1,0:T(8,128)S(1)}, f32[280,1024]{1,0:T(8,128)S(1)}, u32[]{:S(2)}, u32[]{:S(2)}) collective-permute-start(f32[280,1024]{1,0:T(8,128)S(1)} %get-tuple-element.43), channel_id=1, source_target_pairs={{0,8},{1,9},{2,10},{3,11},{4,5},{5,6},{6,7},{7,4},{8,16},{9,17},{1... | collective-permute-start | bytes 3440648 | tf_op jit(solution)/shard_map/ppermute | solution.py:240
  29.0 0.2 collective-permute-done.4.b
  29.2 3.4 %collective-permute-start.5 = (f32[8,1024]{1,0:T(8,128)S(1)}, f32[8,1024]{1,0:T(8,128)S(1)}, u32[]{:S(2)}, u32[]{:S(2)}) collective-permute-start(f32[8,1024]{1,0:T(8,128)S(1)} %shard_map.49), channel_id=1, source_target_pairs={{0,4},{4,0},{8,12},{12,8},{16,20},{20,16},{24,28},{28,24},{1,5},{5... | collective-permute-start | bytes 98312 | tf_op jit(solution)/shard_map/ppermute | solution.py:231
  32.6 0.8 collective-permute-done.5.a
  33.5 1.9 %collective-permute-start.6 = (f32[8,1024]{1,0:T(8,128)S(1)}, f32[8,1024]{1,0:T(8,128)S(1)}, u32[]{:S(2)}, u32[]{:S(2)}) collective-permute-start(f32[8,1024]{1,0:T(8,128)S(1)} %collective-permute-done.5.a), channel_id=1, source_target_pairs={{0,1},{1,0},{2,3},{3,2},{4,12},{5,13},{6,14},{7,15},{8,9},{9,8},{1... | collective-permute-start | bytes 98312 | tf_op jit(solution)/shard_map/ppermute | solution.py:249
  35.4 4.3 %collective-permute-done.6.b = f32[8,1024]{1,0:T(8,128)S(1)} collective-permute-done((f32[8,1024]{1,0:T(8,128)S(1)}, f32[8,1024]{1,0:T(8,128)S(1)}, u32[]{:S(2)}, u32[]{:S(2)}) %collective-permute-start.6) | collective-permute-done | bytes 32800 | tf_op jit(solution)/shard_map/ppermute | solution.py:249
  39.7 1.9 %collective-permute-start.7 = (f32[256,1024]{1,0:T(8,128)S(1)}, f32[256,1024]{1,0:T(8,128)S(1)}, u32[]{:S(2)}, u32[]{:S(2)}) collective-permute-start(f32[256,1024]{1,0:T(8,128)S(1)} %collective-permute-done.1.refs_0_), channel_id=1, source_target_pairs={{0,4},{4,0},{8,12},{12,8},{16,20},{20,16},{24,28},{28,24},{1,5},{5... | collective-permute-start | bytes 3145736 | tf_op jit(solution)/shard_map/ppermute | solution.py:231
  41.6 2.4 %collective-permute-start.8 = (f32[256,1024]{1,0:T(8,128)S(1)}, f32[256,1024]{1,0:T(8,128)S(1)}, u32[]{:S(2)}, u32[]{:S(2)}) collective-permute-start(f32[256,1024]{1,0:T(8,128)S(1)} %collective-permute-done.2.refs_1_), channel_id=1, source_target_pairs={{0,4},{4,0},{8,12},{12,8},{16,20},{20,16},{24,28},{28,24},{1,5},{5... | collective-permute-start | bytes 3145736 | tf_op jit(solution)/shard_map/ppermute | solution.py:231
  44.0 2.4 %collective-permute-start.13 = (f32[8,1024]{1,0:T(8,128)S(1)}, f32[8,1024]{1,0:T(8,128)S(1)}, u32[]{:S(2)}, u32[]{:S(2)}) collective-permute-start(f32[8,1024]{1,0:T(8,128)S(1)} %shard_map.50.sums), channel_id=1, source_target_pairs={{0,2},{1,3},{2,0},{3,1},{4,20},{5,21},{6,22},{7,23},{8,10},{9,11},... | collective-permute-start | bytes 98312 | tf_op jit(solution)/shard_map/ppermute | solution.py:249
  46.5 0.0 collective-permute-done.7.refs_2_
  46.5 0.0 collective-permute-done.8.refs_3_
  46.5 2.9 %shard_map.51 = (f32[192,768]{1,0:T(8,128)S(1)}, f32[192,768]{1,0:T(8,128)S(1)}, bf16[384,1024]{1,0:T(8,128)(2,1)S(1)}, bf16[384,1024]{1,0:T(8,128)(2,1)S(1)}, b...) custom-call(f32[256,1024]{1,0:T(8,128)S(1)} %get-tuple-element.32.chip, ...), custom_call_target="tpu_custom_call" | custom-call | bytes 8388608 | tf_op jit(solution)/shard_map/pallas_call | solution.py:29
  49.4 2.0 %collective-permute-done.13.pair = f32[8,1024]{1,0:T(8,128)S(1)} collective-permute-done((f32[8,1024]{1,0:T(8,128)S(1)}, f32[8,1024]{1,0:T(8,128)S(1)}, u32[]{:S(2)}, u32[]{:S(2)}) %collective-permute-start.13) | collective-permute-done | bytes 32800 | tf_op jit(solution)/shard_map/ppermute | solution.py:249
  51.4 0.0 collective-permute-done.12.sent
  51.4 1.9 %collective-permute-start.14 = (f32[280,1024]{1,0:T(8,128)S(1)}, f32[280,1024]{1,0:T(8,128)S(1)}, u32[]{:S(2)}, u32[]{:S(2)}) collective-permute-start(f32[280,1024]{1,0:T(8,128)S(1)} %collective-permute-done.12.sent), channel_id=1, source_target_pairs={{0,4},{4,0},{8,12},{12,8},{16,20},{20,16},{24,28},{28,24},{1,5},{5... | collective-permute-start | bytes 3440648 | tf_op jit(solution)/shard_map/ppermute | solution.py:231
  53.3 2.8 %collective-permute-start.9 = (f32[192,768]{1,0:T(8,128)S(1)}, f32[192,768]{1,0:T(8,128)S(1)}, u32[]{:S(2)}, u32[]{:S(2)}) collective-permute-start(f32[192,768]{1,0:T(8,128)S(1)} %get-tuple-element.38), channel_id=1, source_target_pairs={{0,32},{4,484},{8,40},{12,492},{16,48},{20,500},{24,56},{28,508},{... | collective-permute-start | bytes 1769480 | tf_op jit(solution)/shard_map/ppermute | solution.py:262
  56.1 0.0 collective-permute-done.14.swap
  56.2 3.2 %shard_map.54 = (f32[232,512]{1,0:T(8,128)S(1)}, f32[232,512]{1,0:T(8,128)S(1)}) custom-call(f32[280,1024]{1,0:T(8,128)S(1)} %collective-permute-done.12.sent, f32[280,1024]{1,0:T(8,128)S(1)} %collective-permute-done.14.swap, f32[1,1024]{1,0:T(1,128)S(1)} %get-tuple-element.36.refs_4_.weights, bf16[384,1024]{1,0:T(8,128)(2,1)S(1)} %get-tuple-element.45.ph, ...), custom_call_target="tpu_custom_call" | custom-call | tf_op jit(solution)/shard_map/pallas_call | solution.py:29
  59.3 3.8 %collective-permute-start.15 = (f32[232,512]{1,0:T(8,128)S(1)}, f32[232,512]{1,0:T(8,128)S(1)}, u32[]{:S(2)}, u32[]{:S(2)}) collective-permute-start(f32[232,512]{1,0:T(8,128)S(1)} %get-tuple-element.50), channel_id=1, source_target_pairs={{0,32},{4,484},{8,40},{12,492},{16,48},{20,500},{24,56},{28,508},{... | collective-permute-start | bytes 1425416 | tf_op jit(solution)/shard_map/ppermute | solution.py:262
  63.2 8.4 %collective-permute-done.9.came = f32[192,768]{1,0:T(8,128)S(1)} collective-permute-done((f32[192,768]{1,0:T(8,128)S(1)}, f32[192,768]{1,0:T(8,128)S(1)}, u32[]{:S(2)}, u32[]{:S(2)}) %collective-permute-start.9) | collective-permute-done | bytes 589856 | tf_op jit(solution)/shard_map/ppermute | solution.py:262
  71.6 0.1 shard_map.52
  71.6 1.9 %collective-permute-start.10 = (f32[96,768]{1,0:T(8,128)S(1)}, f32[96,768]{1,0:T(8,128)S(1)}, u32[]{:S(2)}, u32[]{:S(2)}) collective-permute-start(f32[96,768]{1,0:T(8,128)S(1)} %get-tuple-element.40), channel_id=1, source_target_pairs={{0,64},{4,452},{8,72},{12,460},{16,80},{20,468},{24,88},{28,476},{... | collective-permute-start | bytes 884744 | tf_op jit(solution)/shard_map/ppermute | solution.py:262
  73.6 3.1 %collective-permute-done.15.came = f32[232,512]{1,0:T(8,128)S(1)} collective-permute-done((f32[232,512]{1,0:T(8,128)S(1)}, f32[232,512]{1,0:T(8,128)S(1)}, u32[]{:S(2)}, u32[]{:S(2)}) %collective-permute-start.15) | collective-permute-done | bytes 475168 | tf_op jit(solution)/shard_map/ppermute | solution.py:262
  76.7 0.1 shard_map.55
  76.7 1.9 %collective-permute-start.16 = (f32[120,512]{1,0:T(8,128)S(1)}, f32[120,512]{1,0:T(8,128)S(1)}, u32[]{:S(2)}, u32[]{:S(2)}) collective-permute-start(f32[120,512]{1,0:T(8,128)S(1)} %get-tuple-element.52), channel_id=1, source_target_pairs={{0,64},{4,452},{8,72},{12,460},{16,80},{20,468},{24,88},{28,476},{... | collective-permute-start | bytes 737288 | tf_op jit(solution)/shard_map/ppermute | solution.py:262
  78.6 6.1 %collective-permute-done.10.came = f32[96,768]{1,0:T(8,128)S(1)} collective-permute-done((f32[96,768]{1,0:T(8,128)S(1)}, f32[96,768]{1,0:T(8,128)S(1)}, u32[]{:S(2)}, u32[]{:S(2)}) %collective-permute-start.10) | collective-permute-done | bytes 294944 | tf_op jit(solution)/shard_map/ppermute | solution.py:262
  84.8 1.9 %collective-permute-start.11 = (f32[48,768]{1,0:T(8,128)S(1)}, f32[48,768]{1,0:T(8,128)S(1)}, u32[]{:S(2)}, u32[]{:S(2)}) collective-permute-start(f32[48,768]{1,0:T(8,128)S(1)} %get-tuple-element.42), channel_id=1, source_target_pairs={{0,128},{4,388},{8,136},{12,396},{16,144},{20,404},{24,152},{28,41... | collective-permute-start | bytes 442376 | tf_op jit(solution)/shard_map/ppermute | solution.py:262
  86.7 3.8 %collective-permute-done.16.came = f32[120,512]{1,0:T(8,128)S(1)} collective-permute-done((f32[120,512]{1,0:T(8,128)S(1)}, f32[120,512]{1,0:T(8,128)S(1)}, u32[]{:S(2)}, u32[]{:S(2)}) %collective-permute-start.16) | collective-permute-done | bytes 245792 | tf_op jit(solution)/shard_map/ppermute | solution.py:262
  90.6 5.8 %collective-permute-start.17 = (f32[64,512]{1,0:T(8,128)S(1)}, f32[64,512]{1,0:T(8,128)S(1)}, u32[]{:S(2)}, u32[]{:S(2)}) collective-permute-start(f32[64,512]{1,0:T(8,128)S(1)} %get-tuple-element.54), channel_id=1, source_target_pairs={{0,128},{4,388},{8,136},{12,396},{16,144},{20,404},{24,152},{28,41... | collective-permute-start | bytes 393224 | tf_op jit(solution)/shard_map/ppermute | solution.py:262
  96.4 6.3 %collective-permute-done.11.came_a = f32[48,768]{1,0:T(8,128)S(1)} collective-permute-done((f32[48,768]{1,0:T(8,128)S(1)}, f32[48,768]{1,0:T(8,128)S(1)}, u32[]{:S(2)}, u32[]{:S(2)}) %collective-permute-start.11) | collective-permute-done | bytes 147488 | tf_op jit(solution)/shard_map/ppermute | solution.py:262
  102.6 2.1 %collective-permute-done.17.came_b = f32[64,512]{1,0:T(8,128)S(1)} collective-permute-done((f32[64,512]{1,0:T(8,128)S(1)}, f32[64,512]{1,0:T(8,128)S(1)}, u32[]{:S(2)}, u32[]{:S(2)}) %collective-permute-start.17) | collective-permute-done | bytes 131104 | tf_op jit(solution)/shard_map/ppermute | solution.py:262
  104.7 0.7 collective-permute-start.18
  105.4 2.2 %collective-permute-start.19 = (f32[40,1024]{1,0:T(8,128)S(1)}, f32[40,1024]{1,0:T(8,128)S(1)}, u32[]{:S(2)}, u32[]{:S(2)}) collective-permute-start(f32[40,1024]{1,0:T(8,128)S(1)} %get-tuple-element.56), channel_id=1, source_target_pairs={{0,4},{4,480},{8,12},{12,488},{16,20},{20,496},{24,28},{28,504},{3... | collective-permute-start | bytes 491528 | tf_op jit(solution)/shard_map/ppermute | solution.py:271
  107.6 4.4 %collective-permute-done.19.here = f32[40,1024]{1,0:T(8,128)S(1)} collective-permute-done((f32[40,1024]{1,0:T(8,128)S(1)}, f32[40,1024]{1,0:T(8,128)S(1)}, u32[]{:S(2)}, u32[]{:S(2)}) %collective-permute-start.19) | collective-permute-done | bytes 163872 | tf_op jit(solution)/shard_map/ppermute | solution.py:271
  112.0 0.7 shard_map.58
  (13 shorter events, 0.1 us)
Async XLA Ops:
  0.0 1.0 copy-start
  1.0 0.7 copy-start.1
  1.7 0.7 copy-start.2
  2.4 0.7 copy-start.3
  3.8 3.9 %collective-permute-start = (f32[136,1024]{1,0:T(8,128)S(1)}, f32[136,1024]{1,0:T(8,128)S(1)}, u32[]{:S(2)}, u32[]{:S(2)}) collective-permute-start(f32[136,1024]{1,0:T(8,128)S(1)} %get-tuple-element.31.own), channel_id=1, source_target_pairs={{0,4},{4,0},{8,12},{12,8},{16,20},{20,16},{24,28},{28,24},{1,5},{5... | collective-permute-start | bytes 1671176 | tf_op jit(solution)/shard_map/ppermute | solution.py:231
  7.8 31.9 %collective-permute-start.1 = (f32[256,1024]{1,0:T(8,128)S(1)}, f32[256,1024]{1,0:T(8,128)S(1)}, u32[]{:S(2)}, u32[]{:S(2)}) collective-permute-start(f32[256,1024]{1,0:T(8,128)S(1)} %get-tuple-element.32.chip), channel_id=1, source_target_pairs={{0,24},{1,25},{2,26},{3,27},{4,7},{5,4},{6,5},{7,6},{8,0},{9,1},{1... | collective-permute-start | bytes 3145736 | tf_op jit(solution)/shard_map/ppermute | solution.py:240
  12.7 28.9 %collective-permute-start.2 = (f32[256,1024]{1,0:T(8,128)S(1)}, f32[256,1024]{1,0:T(8,128)S(1)}, u32[]{:S(2)}, u32[]{:S(2)}) collective-permute-start(f32[256,1024]{1,0:T(8,128)S(1)} %get-tuple-element.32.chip), channel_id=1, source_target_pairs={{0,16},{1,17},{2,18},{3,19},{4,6},{5,7},{6,4},{7,5},{8,24},{9,25},... | collective-permute-start | bytes 3145736 | tf_op jit(solution)/shard_map/ppermute | solution.py:240
  15.2 6.2 %collective-permute-start.3 = (f32[8,1024]{1,0:T(8,128)S(1)}, f32[8,1024]{1,0:T(8,128)S(1)}, u32[]{:S(2)}, u32[]{:S(2)}) collective-permute-start(f32[8,1024]{1,0:T(8,128)S(1)} %get-tuple-element.33.a), channel_id=1, source_target_pairs={{0,1},{1,0},{2,3},{3,2},{4,12},{5,13},{6,14},{7,15},{8,9},{9,8},{1... | collective-permute-start | bytes 98312 | tf_op jit(solution)/shard_map/ppermute | solution.py:249
  21.5 7.7 %collective-permute-start.4 = (f32[8,1024]{1,0:T(8,128)S(1)}, f32[8,1024]{1,0:T(8,128)S(1)}, u32[]{:S(2)}, u32[]{:S(2)}) collective-permute-start(f32[8,1024]{1,0:T(8,128)S(1)} %shard_map.48.a), channel_id=1, source_target_pairs={{0,2},{1,3},{2,0},{3,1},{4,20},{5,21},{6,22},{7,23},{8,10},{9,11},... | collective-permute-start | bytes 98312 | tf_op jit(solution)/shard_map/ppermute | solution.py:249
  25.1 26.3 %collective-permute-start.12 = (f32[280,1024]{1,0:T(8,128)S(1)}, f32[280,1024]{1,0:T(8,128)S(1)}, u32[]{:S(2)}, u32[]{:S(2)}) collective-permute-start(f32[280,1024]{1,0:T(8,128)S(1)} %get-tuple-element.43), channel_id=1, source_target_pairs={{0,8},{1,9},{2,10},{3,11},{4,5},{5,6},{6,7},{7,4},{8,16},{9,17},{1... | collective-permute-start | bytes 3440648 | tf_op jit(solution)/shard_map/ppermute | solution.py:240
  29.2 4.3 %collective-permute-start.5 = (f32[8,1024]{1,0:T(8,128)S(1)}, f32[8,1024]{1,0:T(8,128)S(1)}, u32[]{:S(2)}, u32[]{:S(2)}) collective-permute-start(f32[8,1024]{1,0:T(8,128)S(1)} %shard_map.49), channel_id=1, source_target_pairs={{0,4},{4,0},{8,12},{12,8},{16,20},{20,16},{24,28},{28,24},{1,5},{5... | collective-permute-start | bytes 98312 | tf_op jit(solution)/shard_map/ppermute | solution.py:231
  33.5 6.2 %collective-permute-start.6 = (f32[8,1024]{1,0:T(8,128)S(1)}, f32[8,1024]{1,0:T(8,128)S(1)}, u32[]{:S(2)}, u32[]{:S(2)}) collective-permute-start(f32[8,1024]{1,0:T(8,128)S(1)} %collective-permute-done.5.a), channel_id=1, source_target_pairs={{0,1},{1,0},{2,3},{3,2},{4,12},{5,13},{6,14},{7,15},{8,9},{9,8},{1... | collective-permute-start | bytes 98312 | tf_op jit(solution)/shard_map/ppermute | solution.py:249
  39.7 6.8 %collective-permute-start.7 = (f32[256,1024]{1,0:T(8,128)S(1)}, f32[256,1024]{1,0:T(8,128)S(1)}, u32[]{:S(2)}, u32[]{:S(2)}) collective-permute-start(f32[256,1024]{1,0:T(8,128)S(1)} %collective-permute-done.1.refs_0_), channel_id=1, source_target_pairs={{0,4},{4,0},{8,12},{12,8},{16,20},{20,16},{24,28},{28,24},{1,5},{5... | collective-permute-start | bytes 3145736 | tf_op jit(solution)/shard_map/ppermute | solution.py:231
  41.6 4.8 %collective-permute-start.8 = (f32[256,1024]{1,0:T(8,128)S(1)}, f32[256,1024]{1,0:T(8,128)S(1)}, u32[]{:S(2)}, u32[]{:S(2)}) collective-permute-start(f32[256,1024]{1,0:T(8,128)S(1)} %collective-permute-done.2.refs_1_), channel_id=1, source_target_pairs={{0,4},{4,0},{8,12},{12,8},{16,20},{20,16},{24,28},{28,24},{1,5},{5... | collective-permute-start | bytes 3145736 | tf_op jit(solution)/shard_map/ppermute | solution.py:231
  44.0 7.3 %collective-permute-start.13 = (f32[8,1024]{1,0:T(8,128)S(1)}, f32[8,1024]{1,0:T(8,128)S(1)}, u32[]{:S(2)}, u32[]{:S(2)}) collective-permute-start(f32[8,1024]{1,0:T(8,128)S(1)} %shard_map.50.sums), channel_id=1, source_target_pairs={{0,2},{1,3},{2,0},{3,1},{4,20},{5,21},{6,22},{7,23},{8,10},{9,11},... | collective-permute-start | bytes 98312 | tf_op jit(solution)/shard_map/ppermute | solution.py:249
  51.4 4.8 %collective-permute-start.14 = (f32[280,1024]{1,0:T(8,128)S(1)}, f32[280,1024]{1,0:T(8,128)S(1)}, u32[]{:S(2)}, u32[]{:S(2)}) collective-permute-start(f32[280,1024]{1,0:T(8,128)S(1)} %collective-permute-done.12.sent), channel_id=1, source_target_pairs={{0,4},{4,0},{8,12},{12,8},{16,20},{20,16},{24,28},{28,24},{1,5},{5... | collective-permute-start | bytes 3440648 | tf_op jit(solution)/shard_map/ppermute | solution.py:231
  53.3 18.3 %collective-permute-start.9 = (f32[192,768]{1,0:T(8,128)S(1)}, f32[192,768]{1,0:T(8,128)S(1)}, u32[]{:S(2)}, u32[]{:S(2)}) collective-permute-start(f32[192,768]{1,0:T(8,128)S(1)} %get-tuple-element.38), channel_id=1, source_target_pairs={{0,32},{4,484},{8,40},{12,492},{16,48},{20,500},{24,56},{28,508},{... | collective-permute-start | bytes 1769480 | tf_op jit(solution)/shard_map/ppermute | solution.py:262
  59.3 17.3 %collective-permute-start.15 = (f32[232,512]{1,0:T(8,128)S(1)}, f32[232,512]{1,0:T(8,128)S(1)}, u32[]{:S(2)}, u32[]{:S(2)}) collective-permute-start(f32[232,512]{1,0:T(8,128)S(1)} %get-tuple-element.50), channel_id=1, source_target_pairs={{0,32},{4,484},{8,40},{12,492},{16,48},{20,500},{24,56},{28,508},{... | collective-permute-start | bytes 1425416 | tf_op jit(solution)/shard_map/ppermute | solution.py:262
  71.6 13.1 %collective-permute-start.10 = (f32[96,768]{1,0:T(8,128)S(1)}, f32[96,768]{1,0:T(8,128)S(1)}, u32[]{:S(2)}, u32[]{:S(2)}) collective-permute-start(f32[96,768]{1,0:T(8,128)S(1)} %get-tuple-element.40), channel_id=1, source_target_pairs={{0,64},{4,452},{8,72},{12,460},{16,80},{20,468},{24,88},{28,476},{... | collective-permute-start | bytes 884744 | tf_op jit(solution)/shard_map/ppermute | solution.py:262
  76.7 13.9 %collective-permute-start.16 = (f32[120,512]{1,0:T(8,128)S(1)}, f32[120,512]{1,0:T(8,128)S(1)}, u32[]{:S(2)}, u32[]{:S(2)}) collective-permute-start(f32[120,512]{1,0:T(8,128)S(1)} %get-tuple-element.52), channel_id=1, source_target_pairs={{0,64},{4,452},{8,72},{12,460},{16,80},{20,468},{24,88},{28,476},{... | collective-permute-start | bytes 737288 | tf_op jit(solution)/shard_map/ppermute | solution.py:262
  84.8 17.8 %collective-permute-start.11 = (f32[48,768]{1,0:T(8,128)S(1)}, f32[48,768]{1,0:T(8,128)S(1)}, u32[]{:S(2)}, u32[]{:S(2)}) collective-permute-start(f32[48,768]{1,0:T(8,128)S(1)} %get-tuple-element.42), channel_id=1, source_target_pairs={{0,128},{4,388},{8,136},{12,396},{16,144},{20,404},{24,152},{28,41... | collective-permute-start | bytes 442376 | tf_op jit(solution)/shard_map/ppermute | solution.py:262
  90.6 14.1 %collective-permute-start.17 = (f32[64,512]{1,0:T(8,128)S(1)}, f32[64,512]{1,0:T(8,128)S(1)}, u32[]{:S(2)}, u32[]{:S(2)}) collective-permute-start(f32[64,512]{1,0:T(8,128)S(1)} %get-tuple-element.54), channel_id=1, source_target_pairs={{0,128},{4,388},{8,136},{12,396},{16,144},{20,404},{24,152},{28,41... | collective-permute-start | bytes 393224 | tf_op jit(solution)/shard_map/ppermute | solution.py:262
  104.7 2.9 %collective-permute-start.18 = (f32[40,1024]{1,0:T(8,128)S(1)}, f32[40,1024]{1,0:T(8,128)S(1)}, u32[]{:S(2)}, u32[]{:S(2)}) collective-permute-start(f32[40,1024]{1,0:T(8,128)S(1)} %get-tuple-element.55), channel_id=1, source_target_pairs={{0,0},{4,484},{8,8},{12,492},{16,16},{20,500},{24,24},{28,508},{32... | collective-permute-start | bytes 491528 | tf_op jit(solution)/shard_map/ppermute | solution.py:271
  105.4 6.6 %collective-permute-start.19 = (f32[40,1024]{1,0:T(8,128)S(1)}, f32[40,1024]{1,0:T(8,128)S(1)}, u32[]{:S(2)}, u32[]{:S(2)}) collective-permute-start(f32[40,1024]{1,0:T(8,128)S(1)} %get-tuple-element.56), channel_id=1, source_target_pairs={{0,4},{4,480},{8,12},{12,488},{16,20},{20,496},{24,28},{28,504},{3... | collective-permute-start | bytes 491528 | tf_op jit(solution)/shard_map/ppermute | solution.py:271

commit v7 on v6

--- a/solution.py
+++ b/solution.py
@@ -282,7 +282,7 @@
             domain_class.reshape(1, PANEL),
             class_weight.reshape(1, classes),
         ],
-        in_hbm=range(4),
+        in_hbm=range(4), mib=62,
         scratch=[
             pltpu.VMEM((WIDTH, PANEL), F32),
             pltpu.SMEM((1, tiles), jnp.int32),

time: 113 us -> 113 us (level)
  local copies, waits for them, and re-layouts: 3.04 us -> 1.06 us
  Pallas kernels: 7.82 us -> 9.1 us
    unnamed x8 -> x4, local copies, waits for them, and re-layouts: 3.04 us -> 1.06 us
    pallas_call x13, Pallas kernels: 7.82 us -> 9.1 us  [call(): pl.pallas_call(body, out_shape=[jax.ShapeDtypeStruct(s[:-1], BF16) if s[-...]
where the time goes in v7:
time: 113 us; the launch traced here: 112 us
  starting transfers between devices  54.7 us (48%)
  waiting for transfers between devices  47.2 us (42%)
  Pallas kernels  9.1 us (8%)
    ppermute x6, waiting for transfers between devices, along_z(): return lax.ppermute(a, ('dom', 'row'), pairs)  29.8 us
    ppermute x6, starting transfers between devices, along_z(): return lax.ppermute(a, ('dom', 'row'), pairs)  18.2 us
    ppermute x5, starting transfers between devices, across(): return lax.ppermute(a, 'row', [(i, i ^ 1) for i in range(N_ROW)])  11.6 us
    ppermute x3, starting transfers between devices, around(): return lax.ppermute(a, ('row', 'col'), pairs)  11.4 us
    ppermute x4, starting transfers between devices, doubled(): return lax.ppermute(a, ('row', 'col'), pairs)  10.7 us
    ppermute x4, waiting for transfers between devices, doubled(): return lax.ppermute(a, ('row', 'col'), pairs)  9.92 us
    pallas_call x13, Pallas kernels, call(): pl.pallas_call(body, out_shape=[jax.ShapeDtypeStruct(s[:-1], BF16) if s[-...  9.1 us
    ppermute x2, waiting for transfers between devices, settled(): return lax.ppermute(a, ('dom', 'row'), pairs)  4.48 us
  transfers between devices with their start and end apart: 20, of which 13 were waited for; matrix products, arithmetic and copies ran while one was open for 0% of the time, Pallas kernels for 6%

profile of v7, /device:TPU:6, one launch (start us, length us, event | category | flops | bytes accessed | tf_op | source)
XLA Modules:
  0.0 112.3 jit_solution(17242923481309053357)
XLA Ops:
  0.0 2.0 %shard_map.46 = (f32[136,1024]{1,0:T(8,128)}, f32[1,1024]{1,0:T(1,128)}) custom-call(f32[128,1024]{1,0:T(8,128)} %bitcast.7, s32[1,8]{1,0:T(1,128)} %bitcast.9, s32[1,1024]{1,0:T(1,128)} %bitcast.8, f32[1,16]{1,0:T(1,128)} %bitcast.10), custom_call_target="tpu_custom_call" | custom-call | bytes 524288 | tf_op jit(solution)/shard_map/pallas_call | solution.py:29
  2.0 1.9 %collective-permute-start = (f32[136,1024]{1,0:T(8,128)}, f32[136,1024]{1,0:T(8,128)S(1)}, u32[]{:S(2)}, u32[]{:S(2)}) collective-permute-start(f32[136,1024]{1,0:T(8,128)} %get-tuple-element.31.own), channel_id=1, source_target_pairs={{0,4},{4,0},{8,12},{12,8},{16,20},{20,16},{24,28},{28,24},{1,5},{5... | collective-permute-start | bytes 1671176 | tf_op jit(solution)/shard_map/ppermute | solution.py:231
  3.9 2.1 %collective-permute-done.other = f32[136,1024]{1,0:T(8,128)S(1)} collective-permute-done((f32[136,1024]{1,0:T(8,128)}, f32[136,1024]{1,0:T(8,128)S(1)}, u32[]{:S(2)}, u32[]{:S(2)}) %collective-permute-start) | collective-permute-done | bytes 557088 | tf_op jit(solution)/shard_map/ppermute | solution.py:231
  6.1 1.1 copy-done
  7.1 0.1 shard_map.47
  7.3 4.9 %collective-permute-start.1 = (f32[256,1024]{1,0:T(8,128)S(1)}, f32[256,1024]{1,0:T(8,128)S(1)}, u32[]{:S(2)}, u32[]{:S(2)}) collective-permute-start(f32[256,1024]{1,0:T(8,128)S(1)} %get-tuple-element.32.chip), channel_id=1, source_target_pairs={{0,24},{1,25},{2,26},{3,27},{4,7},{5,4},{6,5},{7,6},{8,0},{9,1},{1... | collective-permute-start | bytes 3145736 | tf_op jit(solution)/shard_map/ppermute | solution.py:240
  12.2 2.5 %collective-permute-start.2 = (f32[256,1024]{1,0:T(8,128)S(1)}, f32[256,1024]{1,0:T(8,128)S(1)}, u32[]{:S(2)}, u32[]{:S(2)}) collective-permute-start(f32[256,1024]{1,0:T(8,128)S(1)} %get-tuple-element.32.chip), channel_id=1, source_target_pairs={{0,16},{1,17},{2,18},{3,19},{4,6},{5,7},{6,4},{7,5},{8,24},{9,25},... | collective-permute-start | bytes 3145736 | tf_op jit(solution)/shard_map/ppermute | solution.py:240
  14.7 2.7 %collective-permute-start.3 = (f32[8,1024]{1,0:T(8,128)S(1)}, f32[8,1024]{1,0:T(8,128)S(1)}, u32[]{:S(2)}, u32[]{:S(2)}) collective-permute-start(f32[8,1024]{1,0:T(8,128)S(1)} %get-tuple-element.33.a), channel_id=1, source_target_pairs={{0,1},{1,0},{2,3},{3,2},{4,12},{5,13},{6,14},{7,15},{8,9},{9,8},{1... | collective-permute-start | bytes 98312 | tf_op jit(solution)/shard_map/ppermute | solution.py:249
  17.5 3.5 %collective-permute-done.3.b = f32[8,1024]{1,0:T(8,128)S(1)} collective-permute-done((f32[8,1024]{1,0:T(8,128)S(1)}, f32[8,1024]{1,0:T(8,128)S(1)}, u32[]{:S(2)}, u32[]{:S(2)}) %collective-permute-start.3) | collective-permute-done | bytes 32800 | tf_op jit(solution)/shard_map/ppermute | solution.py:249
  21.0 3.6 %collective-permute-start.4 = (f32[8,1024]{1,0:T(8,128)S(1)}, f32[8,1024]{1,0:T(8,128)S(1)}, u32[]{:S(2)}, u32[]{:S(2)}) collective-permute-start(f32[8,1024]{1,0:T(8,128)S(1)} %shard_map.48.a), channel_id=1, source_target_pairs={{0,2},{1,3},{2,0},{3,1},{4,20},{5,21},{6,22},{7,23},{8,10},{9,11},... | collective-permute-start | bytes 98312 | tf_op jit(solution)/shard_map/ppermute | solution.py:249
  24.6 3.9 %collective-permute-start.12 = (f32[280,1024]{1,0:T(8,128)S(1)}, f32[280,1024]{1,0:T(8,128)S(1)}, u32[]{:S(2)}, u32[]{:S(2)}) collective-permute-start(f32[280,1024]{1,0:T(8,128)S(1)} %get-tuple-element.43), channel_id=1, source_target_pairs={{0,8},{1,9},{2,10},{3,11},{4,5},{5,6},{6,7},{7,4},{8,16},{9,17},{1... | collective-permute-start | bytes 3440648 | tf_op jit(solution)/shard_map/ppermute | solution.py:240
  28.5 0.2 collective-permute-done.4.b
  28.7 3.4 %collective-permute-start.5 = (f32[8,1024]{1,0:T(8,128)S(1)}, f32[8,1024]{1,0:T(8,128)S(1)}, u32[]{:S(2)}, u32[]{:S(2)}) collective-permute-start(f32[8,1024]{1,0:T(8,128)S(1)} %shard_map.49), channel_id=1, source_target_pairs={{0,4},{4,0},{8,12},{12,8},{16,20},{20,16},{24,28},{28,24},{1,5},{5... | collective-permute-start | bytes 98312 | tf_op jit(solution)/shard_map/ppermute | solution.py:231
  32.1 0.8 collective-permute-done.5.a
  33.0 1.9 %collective-permute-start.6 = (f32[8,1024]{1,0:T(8,128)S(1)}, f32[8,1024]{1,0:T(8,128)S(1)}, u32[]{:S(2)}, u32[]{:S(2)}) collective-permute-start(f32[8,1024]{1,0:T(8,128)S(1)} %collective-permute-done.5.a), channel_id=1, source_target_pairs={{0,1},{1,0},{2,3},{3,2},{4,12},{5,13},{6,14},{7,15},{8,9},{9,8},{1... | collective-permute-start | bytes 98312 | tf_op jit(solution)/shard_map/ppermute | solution.py:249
  34.9 4.3 %collective-permute-done.6.b = f32[8,1024]{1,0:T(8,128)S(1)} collective-permute-done((f32[8,1024]{1,0:T(8,128)S(1)}, f32[8,1024]{1,0:T(8,128)S(1)}, u32[]{:S(2)}, u32[]{:S(2)}) %collective-permute-start.6) | collective-permute-done | bytes 32800 | tf_op jit(solution)/shard_map/ppermute | solution.py:249
  39.2 0.0 collective-permute-done.1.refs_0_
  39.2 1.9 %collective-permute-start.7 = (f32[256,1024]{1,0:T(8,128)S(1)}, f32[256,1024]{1,0:T(8,128)S(1)}, u32[]{:S(2)}, u32[]{:S(2)}) collective-permute-start(f32[256,1024]{1,0:T(8,128)S(1)} %collective-permute-done.1.refs_0_), channel_id=1, source_target_pairs={{0,4},{4,0},{8,12},{12,8},{16,20},{20,16},{24,28},{28,24},{1,5},{5... | collective-permute-start | bytes 3145736 | tf_op jit(solution)/shard_map/ppermute | solution.py:231
  41.1 0.0 collective-permute-done.2.refs_1_
  41.1 2.4 %collective-permute-start.8 = (f32[256,1024]{1,0:T(8,128)S(1)}, f32[256,1024]{1,0:T(8,128)S(1)}, u32[]{:S(2)}, u32[]{:S(2)}) collective-permute-start(f32[256,1024]{1,0:T(8,128)S(1)} %collective-permute-done.2.refs_1_), channel_id=1, source_target_pairs={{0,4},{4,0},{8,12},{12,8},{16,20},{20,16},{24,28},{28,24},{1,5},{5... | collective-permute-start | bytes 3145736 | tf_op jit(solution)/shard_map/ppermute | solution.py:231
  43.5 2.4 %collective-permute-start.13 = (f32[8,1024]{1,0:T(8,128)S(1)}, f32[8,1024]{1,0:T(8,128)S(1)}, u32[]{:S(2)}, u32[]{:S(2)}) collective-permute-start(f32[8,1024]{1,0:T(8,128)S(1)} %shard_map.50.sums), channel_id=1, source_target_pairs={{0,2},{1,3},{2,0},{3,1},{4,20},{5,21},{6,22},{7,23},{8,10},{9,11},... | collective-permute-start | bytes 98312 | tf_op jit(solution)/shard_map/ppermute | solution.py:249
  46.0 0.0 collective-permute-done.7.refs_2_
  46.0 0.0 collective-permute-done.8.refs_3_
  46.0 2.9 %shard_map.51 = (f32[192,768]{1,0:T(8,128)S(1)}, f32[192,768]{1,0:T(8,128)S(1)}, bf16[384,1024]{1,0:T(8,128)(2,1)S(1)}, bf16[384,1024]{1,0:T(8,128)(2,1)S(1)}, b...) custom-call(f32[256,1024]{1,0:T(8,128)S(1)} %get-tuple-element.32.chip, ...), custom_call_target="tpu_custom_call" | custom-call | bytes 8388608 | tf_op jit(solution)/shard_map/pallas_call | solution.py:29
  48.9 2.0 %collective-permute-done.13.pair = f32[8,1024]{1,0:T(8,128)S(1)} collective-permute-done((f32[8,1024]{1,0:T(8,128)S(1)}, f32[8,1024]{1,0:T(8,128)S(1)}, u32[]{:S(2)}, u32[]{:S(2)}) %collective-permute-start.13) | collective-permute-done | bytes 32800 | tf_op jit(solution)/shard_map/ppermute | solution.py:249
  50.9 0.0 collective-permute-done.12.sent
  50.9 2.0 %collective-permute-start.14 = (f32[280,1024]{1,0:T(8,128)S(1)}, f32[280,1024]{1,0:T(8,128)S(1)}, u32[]{:S(2)}, u32[]{:S(2)}) collective-permute-start(f32[280,1024]{1,0:T(8,128)S(1)} %collective-permute-done.12.sent), channel_id=1, source_target_pairs={{0,4},{4,0},{8,12},{12,8},{16,20},{20,16},{24,28},{28,24},{1,5},{5... | collective-permute-start | bytes 3440648 | tf_op jit(solution)/shard_map/ppermute | solution.py:231
  52.8 2.8 %collective-permute-start.9 = (f32[192,768]{1,0:T(8,128)S(1)}, f32[192,768]{1,0:T(8,128)S(1)}, u32[]{:S(2)}, u32[]{:S(2)}) collective-permute-start(f32[192,768]{1,0:T(8,128)S(1)} %get-tuple-element.38), channel_id=1, source_target_pairs={{0,32},{4,484},{8,40},{12,492},{16,48},{20,500},{24,56},{28,508},{... | collective-permute-start | bytes 1769480 | tf_op jit(solution)/shard_map/ppermute | solution.py:262
  55.7 0.0 collective-permute-done.14.swap
  55.7 3.2 %shard_map.54 = (f32[232,512]{1,0:T(8,128)S(1)}, f32[232,512]{1,0:T(8,128)S(1)}) custom-call(f32[280,1024]{1,0:T(8,128)S(1)} %collective-permute-done.12.sent, f32[280,1024]{1,0:T(8,128)S(1)} %collective-permute-done.14.swap, f32[1,1024]{1,0:T(1,128)S(1)} %copy-done.1, bf16[384,1024]{1,0:T(8,128)(2,1)S(1)} %get-tuple-element.45.ph, ...), custom_call_target="tpu_custom_call" | custom-call | tf_op jit(solution)/shard_map/pallas_call | solution.py:29
  58.9 3.8 %collective-permute-start.15 = (f32[232,512]{1,0:T(8,128)S(1)}, f32[232,512]{1,0:T(8,128)S(1)}, u32[]{:S(2)}, u32[]{:S(2)}) collective-permute-start(f32[232,512]{1,0:T(8,128)S(1)} %get-tuple-element.50), channel_id=1, source_target_pairs={{0,32},{4,484},{8,40},{12,492},{16,48},{20,500},{24,56},{28,508},{... | collective-permute-start | bytes 1425416 | tf_op jit(solution)/shard_map/ppermute | solution.py:262
  62.7 8.4 %collective-permute-done.9.came = f32[192,768]{1,0:T(8,128)S(1)} collective-permute-done((f32[192,768]{1,0:T(8,128)S(1)}, f32[192,768]{1,0:T(8,128)S(1)}, u32[]{:S(2)}, u32[]{:S(2)}) %collective-permute-start.9) | collective-permute-done | bytes 589856 | tf_op jit(solution)/shard_map/ppermute | solution.py:262
  71.1 0.1 shard_map.52
  71.2 1.9 %collective-permute-start.10 = (f32[96,768]{1,0:T(8,128)S(1)}, f32[96,768]{1,0:T(8,128)S(1)}, u32[]{:S(2)}, u32[]{:S(2)}) collective-permute-start(f32[96,768]{1,0:T(8,128)S(1)} %get-tuple-element.40), channel_id=1, source_target_pairs={{0,64},{4,452},{8,72},{12,460},{16,80},{20,468},{24,88},{28,476},{... | collective-permute-start | bytes 884744 | tf_op jit(solution)/shard_map/ppermute | solution.py:262
  73.1 3.1 %collective-permute-done.15.came = f32[232,512]{1,0:T(8,128)S(1)} collective-permute-done((f32[232,512]{1,0:T(8,128)S(1)}, f32[232,512]{1,0:T(8,128)S(1)}, u32[]{:S(2)}, u32[]{:S(2)}) %collective-permute-start.15) | collective-permute-done | bytes 475168 | tf_op jit(solution)/shard_map/ppermute | solution.py:262
  76.2 0.1 shard_map.55
  76.2 1.9 %collective-permute-start.16 = (f32[120,512]{1,0:T(8,128)S(1)}, f32[120,512]{1,0:T(8,128)S(1)}, u32[]{:S(2)}, u32[]{:S(2)}) collective-permute-start(f32[120,512]{1,0:T(8,128)S(1)} %get-tuple-element.52), channel_id=1, source_target_pairs={{0,64},{4,452},{8,72},{12,460},{16,80},{20,468},{24,88},{28,476},{... | collective-permute-start | bytes 737288 | tf_op jit(solution)/shard_map/ppermute | solution.py:262
  78.2 6.1 %collective-permute-done.10.came = f32[96,768]{1,0:T(8,128)S(1)} collective-permute-done((f32[96,768]{1,0:T(8,128)S(1)}, f32[96,768]{1,0:T(8,128)S(1)}, u32[]{:S(2)}, u32[]{:S(2)}) %collective-permute-start.10) | collective-permute-done | bytes 294944 | tf_op jit(solution)/shard_map/ppermute | solution.py:262
  84.3 1.9 %collective-permute-start.11 = (f32[48,768]{1,0:T(8,128)S(1)}, f32[48,768]{1,0:T(8,128)S(1)}, u32[]{:S(2)}, u32[]{:S(2)}) collective-permute-start(f32[48,768]{1,0:T(8,128)S(1)} %get-tuple-element.42), channel_id=1, source_target_pairs={{0,128},{4,388},{8,136},{12,396},{16,144},{20,404},{24,152},{28,41... | collective-permute-start | bytes 442376 | tf_op jit(solution)/shard_map/ppermute | solution.py:262
  86.2 3.8 %collective-permute-done.16.came = f32[120,512]{1,0:T(8,128)S(1)} collective-permute-done((f32[120,512]{1,0:T(8,128)S(1)}, f32[120,512]{1,0:T(8,128)S(1)}, u32[]{:S(2)}, u32[]{:S(2)}) %collective-permute-start.16) | collective-permute-done | bytes 245792 | tf_op jit(solution)/shard_map/ppermute | solution.py:262
  90.1 5.8 %collective-permute-start.17 = (f32[64,512]{1,0:T(8,128)S(1)}, f32[64,512]{1,0:T(8,128)S(1)}, u32[]{:S(2)}, u32[]{:S(2)}) collective-permute-start(f32[64,512]{1,0:T(8,128)S(1)} %get-tuple-element.54), channel_id=1, source_target_pairs={{0,128},{4,388},{8,136},{12,396},{16,144},{20,404},{24,152},{28,41... | collective-permute-start | bytes 393224 | tf_op jit(solution)/shard_map/ppermute | solution.py:262
  95.9 6.3 %collective-permute-done.11.came_a = f32[48,768]{1,0:T(8,128)S(1)} collective-permute-done((f32[48,768]{1,0:T(8,128)S(1)}, f32[48,768]{1,0:T(8,128)S(1)}, u32[]{:S(2)}, u32[]{:S(2)}) %collective-permute-start.11) | collective-permute-done | bytes 147488 | tf_op jit(solution)/shard_map/ppermute | solution.py:262
  102.1 2.1 %collective-permute-done.17.came_b = f32[64,512]{1,0:T(8,128)S(1)} collective-permute-done((f32[64,512]{1,0:T(8,128)S(1)}, f32[64,512]{1,0:T(8,128)S(1)}, u32[]{:S(2)}, u32[]{:S(2)}) %collective-permute-start.17) | collective-permute-done | bytes 131104 | tf_op jit(solution)/shard_map/ppermute | solution.py:262
  104.2 0.7 collective-permute-start.18
  104.9 2.1 %collective-permute-start.19 = (f32[40,1024]{1,0:T(8,128)S(1)}, f32[40,1024]{1,0:T(8,128)S(1)}, u32[]{:S(2)}, u32[]{:S(2)}) collective-permute-start(f32[40,1024]{1,0:T(8,128)S(1)} %get-tuple-element.56), channel_id=1, source_target_pairs={{0,4},{4,480},{8,12},{12,488},{16,20},{20,496},{24,28},{28,504},{3... | collective-permute-start | bytes 491528 | tf_op jit(solution)/shard_map/ppermute | solution.py:271
  107.1 0.0 collective-permute-done.18.keep
  107.1 4.5 %collective-permute-done.19.here = f32[40,1024]{1,0:T(8,128)S(1)} collective-permute-done((f32[40,1024]{1,0:T(8,128)S(1)}, f32[40,1024]{1,0:T(8,128)S(1)}, u32[]{:S(2)}, u32[]{:S(2)}) %collective-permute-start.19) | collective-permute-done | bytes 163872 | tf_op jit(solution)/shard_map/ppermute | solution.py:271
  111.6 0.7 shard_map.58
  (9 shorter events, 0.1 us)
Async XLA Ops:
  2.0 4.1 %collective-permute-start = (f32[136,1024]{1,0:T(8,128)}, f32[136,1024]{1,0:T(8,128)S(1)}, u32[]{:S(2)}, u32[]{:S(2)}) collective-permute-start(f32[136,1024]{1,0:T(8,128)} %get-tuple-element.31.own), channel_id=1, source_target_pairs={{0,4},{4,0},{8,12},{12,8},{16,20},{20,16},{24,28},{28,24},{1,5},{5... | collective-permute-start | bytes 1671176 | tf_op jit(solution)/shard_map/ppermute | solution.py:231
  6.1 1.1 copy-start
  7.1 38.9 %copy-start.1 = (f32[1,1024]{1,0:T(1,128)S(1)}, f32[1,1024]{1,0:T(1,128)}, u32[]{:S(2)}) copy-start(f32[1,1024]{1,0:T(1,128)} %get-tuple-element.36.refs_4_.weights) | copy-start | bytes 12292
  7.3 31.9 %collective-permute-start.1 = (f32[256,1024]{1,0:T(8,128)S(1)}, f32[256,1024]{1,0:T(8,128)S(1)}, u32[]{:S(2)}, u32[]{:S(2)}) collective-permute-start(f32[256,1024]{1,0:T(8,128)S(1)} %get-tuple-element.32.chip), channel_id=1, source_target_pairs={{0,24},{1,25},{2,26},{3,27},{4,7},{5,4},{6,5},{7,6},{8,0},{9,1},{1... | collective-permute-start | bytes 3145736 | tf_op jit(solution)/shard_map/ppermute | solution.py:240
  12.2 28.9 %collective-permute-start.2 = (f32[256,1024]{1,0:T(8,128)S(1)}, f32[256,1024]{1,0:T(8,128)S(1)}, u32[]{:S(2)}, u32[]{:S(2)}) collective-permute-start(f32[256,1024]{1,0:T(8,128)S(1)} %get-tuple-element.32.chip), channel_id=1, source_target_pairs={{0,16},{1,17},{2,18},{3,19},{4,6},{5,7},{6,4},{7,5},{8,24},{9,25},... | collective-permute-start | bytes 3145736 | tf_op jit(solution)/shard_map/ppermute | solution.py:240
  14.7 6.2 %collective-permute-start.3 = (f32[8,1024]{1,0:T(8,128)S(1)}, f32[8,1024]{1,0:T(8,128)S(1)}, u32[]{:S(2)}, u32[]{:S(2)}) collective-permute-start(f32[8,1024]{1,0:T(8,128)S(1)} %get-tuple-element.33.a), channel_id=1, source_target_pairs={{0,1},{1,0},{2,3},{3,2},{4,12},{5,13},{6,14},{7,15},{8,9},{9,8},{1... | collective-permute-start | bytes 98312 | tf_op jit(solution)/shard_map/ppermute | solution.py:249
  21.0 7.7 %collective-permute-start.4 = (f32[8,1024]{1,0:T(8,128)S(1)}, f32[8,1024]{1,0:T(8,128)S(1)}, u32[]{:S(2)}, u32[]{:S(2)}) collective-permute-start(f32[8,1024]{1,0:T(8,128)S(1)} %shard_map.48.a), channel_id=1, source_target_pairs={{0,2},{1,3},{2,0},{3,1},{4,20},{5,21},{6,22},{7,23},{8,10},{9,11},... | collective-permute-start | bytes 98312 | tf_op jit(solution)/shard_map/ppermute | solution.py:249
  24.6 26.3 %collective-permute-start.12 = (f32[280,1024]{1,0:T(8,128)S(1)}, f32[280,1024]{1,0:T(8,128)S(1)}, u32[]{:S(2)}, u32[]{:S(2)}) collective-permute-start(f32[280,1024]{1,0:T(8,128)S(1)} %get-tuple-element.43), channel_id=1, source_target_pairs={{0,8},{1,9},{2,10},{3,11},{4,5},{5,6},{6,7},{7,4},{8,16},{9,17},{1... | collective-permute-start | bytes 3440648 | tf_op jit(solution)/shard_map/ppermute | solution.py:240
  28.7 4.3 %collective-permute-start.5 = (f32[8,1024]{1,0:T(8,128)S(1)}, f32[8,1024]{1,0:T(8,128)S(1)}, u32[]{:S(2)}, u32[]{:S(2)}) collective-permute-start(f32[8,1024]{1,0:T(8,128)S(1)} %shard_map.49), channel_id=1, source_target_pairs={{0,4},{4,0},{8,12},{12,8},{16,20},{20,16},{24,28},{28,24},{1,5},{5... | collective-permute-start | bytes 98312 | tf_op jit(solution)/shard_map/ppermute | solution.py:231
  33.0 6.2 %collective-permute-start.6 = (f32[8,1024]{1,0:T(8,128)S(1)}, f32[8,1024]{1,0:T(8,128)S(1)}, u32[]{:S(2)}, u32[]{:S(2)}) collective-permute-start(f32[8,1024]{1,0:T(8,128)S(1)} %collective-permute-done.5.a), channel_id=1, source_target_pairs={{0,1},{1,0},{2,3},{3,2},{4,12},{5,13},{6,14},{7,15},{8,9},{9,8},{1... | collective-permute-start | bytes 98312 | tf_op jit(solution)/shard_map/ppermute | solution.py:249
  39.2 6.8 %collective-permute-start.7 = (f32[256,1024]{1,0:T(8,128)S(1)}, f32[256,1024]{1,0:T(8,128)S(1)}, u32[]{:S(2)}, u32[]{:S(2)}) collective-permute-start(f32[256,1024]{1,0:T(8,128)S(1)} %collective-permute-done.1.refs_0_), channel_id=1, source_target_pairs={{0,4},{4,0},{8,12},{12,8},{16,20},{20,16},{24,28},{28,24},{1,5},{5... | collective-permute-start | bytes 3145736 | tf_op jit(solution)/shard_map/ppermute | solution.py:231
  41.1 4.8 %collective-permute-start.8 = (f32[256,1024]{1,0:T(8,128)S(1)}, f32[256,1024]{1,0:T(8,128)S(1)}, u32[]{:S(2)}, u32[]{:S(2)}) collective-permute-start(f32[256,1024]{1,0:T(8,128)S(1)} %collective-permute-done.2.refs_1_), channel_id=1, source_target_pairs={{0,4},{4,0},{8,12},{12,8},{16,20},{20,16},{24,28},{28,24},{1,5},{5... | collective-permute-start | bytes 3145736 | tf_op jit(solution)/shard_map/ppermute | solution.py:231
  43.5 7.3 %collective-permute-start.13 = (f32[8,1024]{1,0:T(8,128)S(1)}, f32[8,1024]{1,0:T(8,128)S(1)}, u32[]{:S(2)}, u32[]{:S(2)}) collective-permute-start(f32[8,1024]{1,0:T(8,128)S(1)} %shard_map.50.sums), channel_id=1, source_target_pairs={{0,2},{1,3},{2,0},{3,1},{4,20},{5,21},{6,22},{7,23},{8,10},{9,11},... | collective-permute-start | bytes 98312 | tf_op jit(solution)/shard_map/ppermute | solution.py:249
  50.9 4.8 %collective-permute-start.14 = (f32[280,1024]{1,0:T(8,128)S(1)}, f32[280,1024]{1,0:T(8,128)S(1)}, u32[]{:S(2)}, u32[]{:S(2)}) collective-permute-start(f32[280,1024]{1,0:T(8,128)S(1)} %collective-permute-done.12.sent), channel_id=1, source_target_pairs={{0,4},{4,0},{8,12},{12,8},{16,20},{20,16},{24,28},{28,24},{1,5},{5... | collective-permute-start | bytes 3440648 | tf_op jit(solution)/shard_map/ppermute | solution.py:231
  52.8 18.3 %collective-permute-start.9 = (f32[192,768]{1,0:T(8,128)S(1)}, f32[192,768]{1,0:T(8,128)S(1)}, u32[]{:S(2)}, u32[]{:S(2)}) collective-permute-start(f32[192,768]{1,0:T(8,128)S(1)} %get-tuple-element.38), channel_id=1, source_target_pairs={{0,32},{4,484},{8,40},{12,492},{16,48},{20,500},{24,56},{28,508},{... | collective-permute-start | bytes 1769480 | tf_op jit(solution)/shard_map/ppermute | solution.py:262
  58.9 17.3 %collective-permute-start.15 = (f32[232,512]{1,0:T(8,128)S(1)}, f32[232,512]{1,0:T(8,128)S(1)}, u32[]{:S(2)}, u32[]{:S(2)}) collective-permute-start(f32[232,512]{1,0:T(8,128)S(1)} %get-tuple-element.50), channel_id=1, source_target_pairs={{0,32},{4,484},{8,40},{12,492},{16,48},{20,500},{24,56},{28,508},{... | collective-permute-start | bytes 1425416 | tf_op jit(solution)/shard_map/ppermute | solution.py:262
  71.2 13.1 %collective-permute-start.10 = (f32[96,768]{1,0:T(8,128)S(1)}, f32[96,768]{1,0:T(8,128)S(1)}, u32[]{:S(2)}, u32[]{:S(2)}) collective-permute-start(f32[96,768]{1,0:T(8,128)S(1)} %get-tuple-element.40), channel_id=1, source_target_pairs={{0,64},{4,452},{8,72},{12,460},{16,80},{20,468},{24,88},{28,476},{... | collective-permute-start | bytes 884744 | tf_op jit(solution)/shard_map/ppermute | solution.py:262
  76.2 13.9 %collective-permute-start.16 = (f32[120,512]{1,0:T(8,128)S(1)}, f32[120,512]{1,0:T(8,128)S(1)}, u32[]{:S(2)}, u32[]{:S(2)}) collective-permute-start(f32[120,512]{1,0:T(8,128)S(1)} %get-tuple-element.52), channel_id=1, source_target_pairs={{0,64},{4,452},{8,72},{12,460},{16,80},{20,468},{24,88},{28,476},{... | collective-permute-start | bytes 737288 | tf_op jit(solution)/shard_map/ppermute | solution.py:262
  84.3 17.8 %collective-permute-start.11 = (f32[48,768]{1,0:T(8,128)S(1)}, f32[48,768]{1,0:T(8,128)S(1)}, u32[]{:S(2)}, u32[]{:S(2)}) collective-permute-start(f32[48,768]{1,0:T(8,128)S(1)} %get-tuple-element.42), channel_id=1, source_target_pairs={{0,128},{4,388},{8,136},{12,396},{16,144},{20,404},{24,152},{28,41... | collective-permute-start | bytes 442376 | tf_op jit(solution)/shard_map/ppermute | solution.py:262
  90.1 14.1 %collective-permute-start.17 = (f32[64,512]{1,0:T(8,128)S(1)}, f32[64,512]{1,0:T(8,128)S(1)}, u32[]{:S(2)}, u32[]{:S(2)}) collective-permute-start(f32[64,512]{1,0:T(8,128)S(1)} %get-tuple-element.54), channel_id=1, source_target_pairs={{0,128},{4,388},{8,136},{12,396},{16,144},{20,404},{24,152},{28,41... | collective-permute-start | bytes 393224 | tf_op jit(solution)/shard_map/ppermute | solution.py:262
  104.2 2.8 %collective-permute-start.18 = (f32[40,1024]{1,0:T(8,128)S(1)}, f32[40,1024]{1,0:T(8,128)S(1)}, u32[]{:S(2)}, u32[]{:S(2)}) collective-permute-start(f32[40,1024]{1,0:T(8,128)S(1)} %get-tuple-element.55), channel_id=1, source_target_pairs={{0,0},{4,484},{8,8},{12,492},{16,16},{20,500},{24,24},{28,508},{32... | collective-permute-start | bytes 491528 | tf_op jit(solution)/shard_map/ppermute | solution.py:271
  104.9 6.6 %collective-permute-start.19 = (f32[40,1024]{1,0:T(8,128)S(1)}, f32[40,1024]{1,0:T(8,128)S(1)}, u32[]{:S(2)}, u32[]{:S(2)}) collective-permute-start(f32[40,1024]{1,0:T(8,128)S(1)} %get-tuple-element.56), channel_id=1, source_target_pairs={{0,4},{4,480},{8,12},{12,488},{16,20},{20,496},{24,28},{28,504},{3... | collective-permute-start | bytes 491528 | tf_op jit(solution)/shard_map/ppermute | solution.py:271
